TPU v7x, 256 devices: a whole 4x4x8 slice. The times are simulated.
256 devices in a mesh: row: 16 (over y, x), col: 16 (over z, core).
Axes of the slice: x: 4, y: 4, z: 8, core: 2. Of those that a mesh axis runs over, the one named last changes fastest.
Arguments:
- queries: bfloat16 [256, 256, 768], P('row', 'col'), may hold values from -15 to 15
- keys: bfloat16 [256, 256, 768], P('row', 'col'), may hold values from -15 to 15
- values: bfloat16 [256, 256, 768], P('row', 'col'), may hold values from -6 to 6
- list_one: int32 [256, 27], replicated, may hold values from -1 to 255, as said below
- list_two: int32 [64, 27], replicated, may hold values from -1 to 63, as said below
Outputs:
- attended: bfloat16 [256, 256, 768], P('row', 'col')
Inputs may be any that keep to these rules, and one draw needn't show every extreme that they name: `list_one`: row b names level-1 blocks (16 x 16 tokens, numbered row-major) that block b interacts with; each entry is -1 or a child of one of the 3 x 3 neighbours of b's parent block that is not among b's own 3 x 3 neighbours, so its block row and column lie within 3 of b's; no block appears twice in a row. `list_two`: row b names level-2 blocks (32 x 32 tokens, numbered row-major) that block b interacts with; each entry is -1 or a block other than b whose block row and column lie within 3 of b's; no block appears twice in a row.
All inputs are finite; a program needn't handle non-finite values.
Results may differ from a plain program's by a relative error of at most 0.0054.
Values may be sent and summed in bfloat16 or wider, within the bound.
No kernel may reach another device: no remote copies, remote signals or barrier semaphores. Data moves between devices by JAX's collectives and lax.ppermute only.
A program may use at most 128 MiB of HBM per device.

v0:
```python
import math

import jax
import jax.numpy as jnp
from jax import lax
from jax.sharding import PartitionSpec as P

HEADS = 12


LOG_FOUR = math.log(4.0)


def passed_along(value, axis, steps):
    count = lax.axis_size(axis)
    initial, last = (max(0, -steps), min(count, count - steps))
    return lax.ppermute(value, axis, [(source, source + steps) for source in range(initial, last)])


def extended(block, sides, width):
    for axis, dim in sides:
        count = lax.axis_size(axis)
        forward = [(i, i + 1) for i in range(count - 1)]
        backward = [(target, source) for source, target in forward]
        low = lax.ppermute(
            lax.slice_in_dim(block, block.shape[dim] - width, None, axis=dim), axis, forward
        )
        high = lax.ppermute(lax.slice_in_dim(block, 0, width, axis=dim), axis, backward)
        block = jnp.concatenate([low, block, high], axis=dim)
    return block


def pooled(source, factor):
    stacked, grid_rows, grid_cols, channels = source.shape
    blocks = source.astype(jnp.float32).reshape(
        stacked, grid_rows // factor, factor, grid_cols // factor, factor, channels
    )
    return jnp.mean(blocks, axis=(2, 4)).astype(jnp.bfloat16)


def far_blocks(coarse_grid, entries, block_cols, row_anchor, col_anchor):
    channels = coarse_grid.shape[-1]
    usable = entries >= 0
    clamped = jnp.maximum(entries, 0)
    top_rows = clamped // block_cols * 8 - row_anchor
    left_cols = clamped % block_cols * 8 - col_anchor

    def pick_block(start_row, start_col):
        anchor_zero = jnp.zeros((), jnp.int32)
        return lax.dynamic_slice(
            coarse_grid, (anchor_zero, start_row, start_col, anchor_zero), (2, 8, 8, channels)
        )

    gathered = jax.vmap(pick_block)(top_rows, left_cols)
    slot_count = entries.shape[0]
    key_value = jnp.moveaxis(gathered, 1, 0).reshape(2, slot_count * 64, channels)
    return (key_value, jnp.repeat(usable, 64))


def contract(form, left, right):
    return jnp.einsum(form, left, right, preferred_element_type=jnp.float32)


def attend(tile_q, window, inside, far_sets):
    tile_rows, tile_cols, channels = tile_q.shape
    head_dim = channels // HEADS
    pairs = HEADS // 2
    score_scale = 1.0 / math.sqrt(head_dim)
    across = tile_cols // 8
    count = tile_rows // 8 * across
    query_blocks = jnp.transpose(
        tile_q.reshape(tile_rows // 8, 8, across, 8, channels), (0, 2, 1, 3, 4)
    )
    query_pairs = jnp.transpose(query_blocks.reshape(count * 64, pairs, 2 * head_dim), (1, 0, 2))
    near_list = []
    ok_list = []
    for index in range(count):
        block_row = index // across
        block_col = index % across
        near_list.append(
            window[
                :, 8 * block_row : 8 * block_row + 24, 8 * block_col : 8 * block_col + 24
            ].reshape(2, 576, channels)
        )
        ok_list.append(
            inside[8 * block_row : 8 * block_row + 24, 8 * block_col : 8 * block_col + 24].reshape(
                576
            )
        )
    near_all = jnp.stack(near_list, axis=1).reshape(2, count, 576, pairs, 2 * head_dim)
    near_pairs = jnp.transpose(near_all, (3, 0, 1, 2, 4))
    near_ok = jnp.stack(ok_list)
    far_all = jnp.concatenate([pair_kv for pair_kv, usable in far_sets], axis=1)
    far_len = far_all.shape[1]
    far_pairs = jnp.transpose(far_all.reshape(2, far_len, pairs, 2 * head_dim), (2, 0, 1, 3))
    bias_list = []
    for depth in range(len(far_sets)):
        bias_list.append(
            jnp.where(far_sets[depth][1], (depth + 1) * LOG_FOUR, -1e30).astype(jnp.float32)
        )
    far_bias = jnp.concatenate(bias_list)

    def one_pair(items):
        query_part, near_part, far_part = items
        query_heads = query_part.reshape(count, 64, 2, head_dim)
        near_keys = near_part[0].reshape(count, 576, 2, head_dim)
        near_values = near_part[1].reshape(count, 576, 2, head_dim)
        far_keys = far_part[0].reshape(far_len, 2, head_dim)
        far_values = far_part[1].reshape(far_len, 2, head_dim)
        near_scores = jnp.where(
            near_ok[:, None, None, :],
            contract("bqhd,bkhd->bhqk", query_heads, near_keys) * score_scale,
            -1e30,
        )
        far_scores = contract("bqhd,khd->bhqk", query_heads, far_keys) * score_scale + far_bias
        highest = jnp.maximum(jnp.max(near_scores, axis=3), jnp.max(far_scores, axis=3))[
            :, :, :, None
        ]
        near_weights = jnp.exp(near_scores - highest)
        far_weights = jnp.exp(far_scores - highest)
        totals = jnp.sum(near_weights, axis=3) + jnp.sum(far_weights, axis=3)
        merged = contract("bhqk,bkhd->bqhd", near_weights.astype(jnp.bfloat16), near_values)
        merged = merged + contract("bhqk,khd->bqhd", far_weights.astype(jnp.bfloat16), far_values)
        merged = merged / jnp.transpose(totals, (0, 2, 1))[:, :, :, None]
        return merged.reshape(count * 64, 2 * head_dim)

    outputs = lax.map(one_pair, (query_pairs, near_pairs, far_pairs))
    outputs = jnp.transpose(outputs, (1, 0, 2)).reshape(tile_rows // 8, across, 8, 8, channels)
    return (
        jnp.transpose(outputs, (0, 2, 1, 3, 4))
        .reshape(tile_rows, tile_cols, channels)
        .astype(jnp.bfloat16)
    )


def reach_one(coarse):
    reach_rows = min(3, lax.axis_size("row") - 1)
    reach_cols = min(3, lax.axis_size("col") - 1)
    pieces = []
    for offset in range(-reach_rows, reach_rows + 1):
        if offset == 0:
            pieces.append(coarse)
        else:
            pieces.append(passed_along(coarse, "row", -offset))
    column = jnp.concatenate(pieces, axis=1)
    pieces = []
    for offset in range(-reach_cols, reach_cols + 1):
        if offset == 0:
            pieces.append(column)
        else:
            pieces.append(passed_along(column, "col", -offset))
    return (jnp.concatenate(pieces, axis=2), reach_rows, reach_cols)


def reach_two(coarse):
    reach_rows = min(7, lax.axis_size("row") - 1)
    reach_cols = min(7, lax.axis_size("col") - 1)
    pieces = []
    for offset in range(-reach_rows, reach_rows + 1):
        if offset == 0:
            pieces.append(coarse)
        else:
            pieces.append(passed_along(coarse, "row", -offset))
    column = jnp.concatenate(pieces, axis=1)
    pieces = []
    for offset in range(-reach_cols, reach_cols + 1):
        if offset == 0:
            pieces.append(column)
        else:
            pieces.append(passed_along(column, "col", -offset))
    return (jnp.concatenate(pieces, axis=2), reach_rows, reach_cols)


def body(queries, keys, values, list_one, list_two):
    tile_rows, tile_cols, channels = queries.shape
    rows_count = lax.axis_size("row")
    cols_count = lax.axis_size("col")
    my_row = lax.axis_index("row")
    my_col = lax.axis_index("col")
    key_value = jnp.stack([keys, values])
    window = extended(key_value, (("row", 1), ("col", 2)), 8)
    row_ids = my_row * tile_rows - 8 + jnp.arange(tile_rows + 16, dtype=jnp.int32)
    col_ids = my_col * tile_cols - 8 + jnp.arange(tile_cols + 16, dtype=jnp.int32)
    row_ok = (row_ids >= 0) & (row_ids < rows_count * tile_rows)
    col_ok = (col_ids >= 0) & (col_ids < cols_count * tile_cols)
    inside = row_ok[:, None] & col_ok[None, :]
    image_cols = cols_count * tile_cols
    top_row = my_row * tile_rows
    left_col = my_col * tile_cols
    coarse_one = pooled(key_value, 2)
    cols_one = image_cols // 16
    entries_one = list_one[top_row // 16 * cols_one + left_col // 16]
    grid_one, reach_rows, reach_cols = reach_one(coarse_one)
    set_one = far_blocks(
        grid_one,
        entries_one,
        cols_one,
        (my_row - reach_rows) * (tile_rows // 2),
        (my_col - reach_cols) * (tile_cols // 2),
    )
    coarse_two = pooled(key_value, 4)
    cols_two = image_cols // 32
    entries_two = list_two[top_row // 32 * cols_two + left_col // 32]
    grid_two, reach_rows, reach_cols = reach_two(coarse_two)
    set_two = far_blocks(
        grid_two,
        entries_two,
        cols_two,
        (my_row - reach_rows) * (tile_rows // 4),
        (my_col - reach_cols) * (tile_cols // 4),
    )
    return attend(queries, window, inside, [set_one, set_two])


def solution(mesh):
    placed = (P("row", "col", None), P("row", "col", None), P("row", "col", None), P(), P())
    return jax.shard_map(
        body, mesh=mesh, in_specs=placed, out_specs=P("row", "col", None), check_vma=False
    )
```

profile of v0, /device:TPU:48, one launch (start us, length us, event | category | flops | bytes accessed | tf_op | source)
XLA Modules:
  0.0 752.8 jit_solution(16102050226229427043)
XLA Ops:
  3.6 5.4 collective-permute-start.16
  36.0 6.0 collective-permute-start.23
  42.1 4.0 collective-permute-start.24
  46.2 4.8 collective-permute-start.25
  59.7 3.4 collective-permute-start.4
  63.2 6.0 collective-permute-start.5
  71.5 5.8 collective-permute-start.7
  79.6 3.3 collective-permute-start
  83.8 4.6 collective-permute-start.1
  89.2 3.3 collective-permute-start.30
  96.3 6.4 collective-permute-start.31
  104.4 6.1 collective-permute-start.32
  116.0 62.8 %collective-permute-done.30 = bf16[2,60,4,768]{3,0,2,1:T(2,128)(2,1)S(1)} collective-permute-done((bf16[2,60,4,768]{3,0,2,1:T(2,128)(2,1)S(1)}, bf16[2,60,4,768]{3,0,2,1:T(2,128)(2,1)S(1)}, u32[]{:S(2)}, u32[]{:S(2)}) %collective-permute-start.30) | collective-permute-done | bytes 737312 | tf_op jit(solution)/shard_map/ppermute | solution.py:17
  181.9 12.6 %collective-permute-done.31 = bf16[2,60,4,768]{3,0,2,1:T(2,128)(2,1)S(1)} collective-permute-done((bf16[2,60,4,768]{3,0,2,1:T(2,128)(2,1)S(1)}, bf16[2,60,4,768]{3,0,2,1:T(2,128)(2,1)S(1)}, u32[]{:S(2)}, u32[]{:S(2)}) %collective-permute-start.31) | collective-permute-done | bytes 737312 | tf_op jit(solution)/shard_map/ppermute | solution.py:17
  199.4 10.9 %collective-permute-done.32 = bf16[2,60,4,768]{3,0,2,1:T(2,128)(2,1)S(1)} collective-permute-done((bf16[2,60,4,768]{3,0,2,1:T(2,128)(2,1)S(1)}, bf16[2,60,4,768]{3,0,2,1:T(2,128)(2,1)S(1)}, u32[]{:S(2)}, u32[]{:S(2)}) %collective-permute-start.32) | collective-permute-done | bytes 737312 | tf_op jit(solution)/shard_map/ppermute | solution.py:17
  213.7 12.4 %collective-permute-done.33 = bf16[2,60,4,768]{3,0,2,1:T(2,128)(2,1)S(1)} collective-permute-done((bf16[2,60,4,768]{3,0,2,1:T(2,128)(2,1)S(1)}, bf16[2,60,4,768]{3,0,2,1:T(2,128)(2,1)S(1)}, u32[]{:S(2)}, u32[]{:S(2)}) %collective-permute-start.33) | collective-permute-done | bytes 737312 | tf_op jit(solution)/shard_map/ppermute | solution.py:17
  229.8 12.2 %collective-permute-done.34 = bf16[2,60,4,768]{3,0,2,1:T(2,128)(2,1)S(1)} collective-permute-done((bf16[2,60,4,768]{3,0,2,1:T(2,128)(2,1)S(1)}, bf16[2,60,4,768]{3,0,2,1:T(2,128)(2,1)S(1)}, u32[]{:S(2)}, u32[]{:S(2)}) %collective-permute-start.34) | collective-permute-done | bytes 737312 | tf_op jit(solution)/shard_map/ppermute | solution.py:17
  244.7 13.1 %collective-permute-done.35 = bf16[2,60,4,768]{3,0,2,1:T(2,128)(2,1)S(1)} collective-permute-done((bf16[2,60,4,768]{3,0,2,1:T(2,128)(2,1)S(1)}, bf16[2,60,4,768]{3,0,2,1:T(2,128)(2,1)S(1)}, u32[]{:S(2)}, u32[]{:S(2)}) %collective-permute-start.35) | collective-permute-done | bytes 737312 | tf_op jit(solution)/shard_map/ppermute | solution.py:17
  274.4 3.7 collective-permute-done.38
  279.4 39.0 %collective-permute-done.39 = bf16[2,60,4,768]{3,0,2,1:T(2,128)(2,1)S(1)} collective-permute-done((bf16[2,60,4,768]{3,0,2,1:T(2,128)(2,1)S(1)}, bf16[2,60,4,768]{3,0,2,1:T(2,128)(2,1)S(1)}, u32[]{:S(2)}, u32[]{:S(2)}) %collective-permute-start.39) | collective-permute-done | bytes 737312 | tf_op jit(solution)/shard_map/ppermute | solution.py:17
  320.4 20.0 %collective-permute-start.3 = (bf16[2,32,8,768]{3,2,1,0:T(8,128)(2,1)}, bf16[2,32,8,768]{3,2,1,0:T(8,128)(2,1)}, u32[]{:S(2)}, u32[]{:S(2)}) collective-permute-start(bf16[2,32,8,768]{3,2,1,0:T(8,128)(2,1)} %get-tuple-element.111), channel_id=1, source_target_pairs={{1,0},{2,1},{3,2},{4,3},{5,4},{6,5},{7,6},{8,7},{9,8},{10,9},{11,1... | collective-permute-start | bytes 2359304 | tf_op jit(solution)/shard_map/ppermute | solution.py:28
  346.2 24.3 %collective-permute-done.41 = bf16[2,60,4,768]{3,0,2,1:T(2,128)(2,1)S(1)} collective-permute-done((bf16[2,60,4,768]{3,0,2,1:T(2,128)(2,1)S(1)}, bf16[2,60,4,768]{3,0,2,1:T(2,128)(2,1)S(1)}, u32[]{:S(2)}, u32[]{:S(2)}) %collective-permute-start.41) | collective-permute-done | bytes 737312 | tf_op jit(solution)/shard_map/ppermute | solution.py:17
  370.5 65.2 %collective-permute-start.10 = (bf16[2,56,8,768]{3,0,2,1:T(2,128)(2,1)}, bf16[2,56,8,768]{3,0,2,1:T(2,128)(2,1)}, u32[]{:S(2)}, u32[]{:S(2)}) collective-permute-start(bf16[2,56,8,768]{3,0,2,1:T(2,128)(2,1)} %constant_dynamic-update-slice_fusion.1), channel_id=1, source_target_pairs={{0,3},{1,4},{2,5},{3,6},{4,7},{5,8},{6,9},{7,10},{8,11},{9,12},{10... | collective-permute-start | bytes 4128776 | tf_op jit(solution)/shard_map/ppermute | solution.py:17
  437.1 15.3 %collective-permute-start.11 = (bf16[2,56,8,768]{3,0,2,1:T(2,128)(2,1)}, bf16[2,56,8,768]{3,0,2,1:T(2,128)(2,1)}, u32[]{:S(2)}, u32[]{:S(2)}) collective-permute-start(bf16[2,56,8,768]{3,0,2,1:T(2,128)(2,1)} %constant_dynamic-update-slice_fusion.1), channel_id=1, source_target_pairs={{0,2},{1,3},{2,4},{3,5},{4,6},{5,7},{6,8},{7,9},{8,10},{9,11},{10,... | collective-permute-start | bytes 4128776 | tf_op jit(solution)/shard_map/ppermute | solution.py:17
  453.8 15.0 %collective-permute-done.43 = bf16[2,60,4,768]{3,0,2,1:T(2,128)(2,1)S(1)} collective-permute-done((bf16[2,60,4,768]{3,0,2,1:T(2,128)(2,1)S(1)}, bf16[2,60,4,768]{3,0,2,1:T(2,128)(2,1)S(1)}, u32[]{:S(2)}, u32[]{:S(2)}) %collective-permute-start.43) | collective-permute-done | bytes 737312 | tf_op jit(solution)/shard_map/ppermute | solution.py:17
  472.8 19.0 %gather_fusion.1 = bf16[27,2,8,8,768]{4,1,3,2,0:T(2,128)(2,1)} fusion(bf16[2,60,60,768]{3,0,2,1:T(2,128)(2,1)} %constant_dynamic-update-slice_fusion.36, s32[27]{0:T(128)S(1)} %fusion.38), kind=kCustom, calls=%fused_computation.1 | custom fusion | bytes 10617264 | tf_op jit(solution)/shard_map/vmap()/gather | solution.py:50
  491.8 5.9 copy.80
  497.7 11.7 %concatenate.54 = bf16[2,1728,6,128]{3,2,1,0:T(8,128)(2,1)} reshape(bf16[2,27,8,8,768]{4,3,2,1,0:T(8,128)(2,1)} %copy.80) | data formatting | bytes 10616832 | tf_op jit(solution)/shard_map/concatenate | solution.py:93
  509.4 3.6 collective-permute-start.13
  517.5 3.0 fusion.41
  520.5 3.6 stack.38
  524.1 4.7 stack.39
  528.8 4.7 stack.40
  533.5 4.7 stack.41
  538.2 9.2 %maximum_bitcast_fusion.1 = bf16[6,2,4,576,128]{4,0,3,1,2:T(8,128)(2,1)} fusion(bf16[2,1,576,6,128]{4,3,2,0,1:T(8,128)(2,1)} %stack.41, bf16[2,1,576,6,128]{4,3,2,0,1:T(8,128)(2,1)} %stack.40, bf16[2,1,576,6,128]{4,3,2,0,1:T(8,128)(2,1)} %stack.39, bf16[2,1,576,6,128]{4,3,2,0,1:T(8,128)(2,1)S(1)} %stack.38), kind=kLoop, calls=%fused_computation.31 | loop fusion | flops 10616832 | bytes 14155776 | tf_op jit(solution)/shard_map/transpose | solution.py:91
  547.4 15.4 %copy.81 = bf16[6,2,4,576,128]{3,4,2,1,0:T(8,128)(2,1)} copy(bf16[6,2,4,576,128]{4,0,3,1,2:T(8,128)(2,1)} %maximum_bitcast_fusion.1) | data formatting | bytes 14155776 | tf_op jit(solution)/shard_map/while | solution.py:127
  564.5 3.4 constant_dynamic-update-slice_fusion.20
  567.9 3.4 constant_dynamic-update-slice_fusion.19
  571.3 3.4 constant_dynamic-update-slice_fusion.18
  580.8 3.4 constant_dynamic-update-slice_fusion.10
  584.3 3.4 constant_dynamic-update-slice_fusion.9
  587.7 23.0 %collective-permute-done.15 = bf16[2,56,8,768]{3,0,2,1:T(2,128)(2,1)S(1)} collective-permute-done((bf16[2,56,8,768]{3,0,2,1:T(2,128)(2,1)}, bf16[2,56,8,768]{3,0,2,1:T(2,128)(2,1)S(1)}, u32[]{:S(2)}, u32[]{:S(2)}) %collective-permute-start.15) | collective-permute-done | bytes 1376288 | tf_op jit(solution)/shard_map/ppermute | solution.py:17
  612.8 18.7 %gather_fusion = bf16[27,2,8,8,768]{4,1,3,2,0:T(2,128)(2,1)} fusion(bf16[2,56,56,768]{3,0,2,1:T(2,128)(2,1)} %constant_dynamic-update-slice_fusion.8, s32[27]{0:T(128)S(1)} %copy-done.10), kind=kCustom, calls=%fused_computation | custom fusion | bytes 10617264 | tf_op jit(solution)/shard_map/vmap()/gather | solution.py:50
  631.5 6.0 copy.78
  637.5 11.7 %concatenate.50 = bf16[2,1728,6,128]{3,2,1,0:T(8,128)(2,1)} reshape(bf16[2,27,8,8,768]{4,3,2,1,0:T(8,128)(2,1)} %copy.78) | data formatting | bytes 10616832 | tf_op jit(solution)/shard_map/concatenate | solution.py:93
  649.2 16.5 %maximum_bitcast_fusion = bf16[6,2,3456,128]{3,0,2,1:T(8,128)(2,1)} fusion(bf16[2,1728,6,128]{3,2,1,0:T(8,128)(2,1)} %concatenate.54, bf16[2,1728,6,128]{3,2,1,0:T(8,128)(2,1)} %concatenate.50), kind=kLoop, calls=%fused_computation.30 | loop fusion | flops 5308416 | bytes 21233664 | tf_op jit(solution)/shard_map/transpose | solution.py:95
  665.7 17.3 %copy.83 = bf16[6,2,3456,128]{2,3,1,0:T(8,128)(2,1)} copy(bf16[6,2,3456,128]{3,0,2,1:T(8,128)(2,1)} %maximum_bitcast_fusion) | data formatting | bytes 21233664 | tf_op jit(solution)/shard_map/while | solution.py:127
  683.1 67.7 %while.10 = (s32[]{:T(128)}, bf16[6,256,128]{2,1,0:T(8,128)(2,1)S(1)}, bf16[6,2,4,576,128]{3,4,2,1,0:T(8,128)(2,1)}, pred[4,576]{1,0:T(4,128)(4,1)S(1)}, bf16[6,...) while((s32[]{:T(128)}, ...), condition=%wide.region_7.8_spmd, body=%wide.region_2.7_spmd.sunk | while | flops 550108160 | bytes 49083784 | solution.py:127
  (304 shorter events, 188.5 us)
Async XLA Ops:
  3.6 28.2 %collective-permute-start.16 = (bf16[2,4,4,768]{3,0,2,1:T(2,128)(2,1)}, bf16[2,4,4,768]{3,0,2,1:T(2,128)(2,1)S(1)}, u32[]{:S(2)}, u32[]{:S(2)}) collective-permute-start(bf16[2,4,4,768]{3,0,2,1:T(2,128)(2,1)} %fusion.19), channel_id=1, source_target_pairs={{0,112},{16,128},{32,144},{48,160},{64,176},{80,192},{96,208},{112... | collective-permute-start | bytes 147464 | tf_op jit(solution)/shard_map/ppermute | solution.py:17
  9.0 25.0 %collective-permute-start.17 = (bf16[2,4,4,768]{3,0,2,1:T(2,128)(2,1)}, bf16[2,4,4,768]{3,0,2,1:T(2,128)(2,1)S(1)}, u32[]{:S(2)}, u32[]{:S(2)}) collective-permute-start(bf16[2,4,4,768]{3,0,2,1:T(2,128)(2,1)} %fusion.19), channel_id=1, source_target_pairs={{0,96},{16,112},{32,128},{48,144},{64,160},{80,176},{96,192},{112,... | collective-permute-start | bytes 147464 | tf_op jit(solution)/shard_map/ppermute | solution.py:17
  10.9 25.1 %collective-permute-start.18 = (bf16[2,4,4,768]{3,0,2,1:T(2,128)(2,1)}, bf16[2,4,4,768]{3,0,2,1:T(2,128)(2,1)S(1)}, u32[]{:S(2)}, u32[]{:S(2)}) collective-permute-start(bf16[2,4,4,768]{3,0,2,1:T(2,128)(2,1)} %fusion.19), channel_id=1, source_target_pairs={{0,80},{16,96},{32,112},{48,128},{64,144},{80,160},{96,176},{112,1... | collective-permute-start | bytes 147464 | tf_op jit(solution)/shard_map/ppermute | solution.py:17
  12.9 29.2 %collective-permute-start.19 = (bf16[2,4,4,768]{3,0,2,1:T(2,128)(2,1)}, bf16[2,4,4,768]{3,0,2,1:T(2,128)(2,1)S(1)}, u32[]{:S(2)}, u32[]{:S(2)}) collective-permute-start(bf16[2,4,4,768]{3,0,2,1:T(2,128)(2,1)} %fusion.19), channel_id=1, source_target_pairs={{0,64},{16,80},{32,96},{48,112},{64,128},{80,144},{96,160},{112,17... | collective-permute-start | bytes 147464 | tf_op jit(solution)/shard_map/ppermute | solution.py:17
  14.8 31.4 %collective-permute-start.20 = (bf16[2,4,4,768]{3,0,2,1:T(2,128)(2,1)}, bf16[2,4,4,768]{3,0,2,1:T(2,128)(2,1)S(1)}, u32[]{:S(2)}, u32[]{:S(2)}) collective-permute-start(bf16[2,4,4,768]{3,0,2,1:T(2,128)(2,1)} %fusion.19), channel_id=1, source_target_pairs={{0,48},{16,64},{32,80},{48,96},{64,112},{80,128},{96,144},{112,160... | collective-permute-start | bytes 147464 | tf_op jit(solution)/shard_map/ppermute | solution.py:17
  31.8 19.3 %collective-permute-start.21 = (bf16[2,4,4,768]{3,0,2,1:T(2,128)(2,1)}, bf16[2,4,4,768]{3,0,2,1:T(2,128)(2,1)S(1)}, u32[]{:S(2)}, u32[]{:S(2)}) collective-permute-start(bf16[2,4,4,768]{3,0,2,1:T(2,128)(2,1)} %fusion.19), channel_id=1, source_target_pairs={{0,32},{16,48},{32,64},{48,80},{64,96},{80,112},{96,128},{112,144}... | collective-permute-start | bytes 147464 | tf_op jit(solution)/shard_map/ppermute | solution.py:17
  34.0 19.1 %collective-permute-start.22 = (bf16[2,4,4,768]{3,0,2,1:T(2,128)(2,1)}, bf16[2,4,4,768]{3,0,2,1:T(2,128)(2,1)S(1)}, u32[]{:S(2)}, u32[]{:S(2)}) collective-permute-start(bf16[2,4,4,768]{3,0,2,1:T(2,128)(2,1)} %fusion.19), channel_id=1, source_target_pairs={{0,16},{16,32},{32,48},{48,64},{64,80},{80,96},{96,112},{112,128},... | collective-permute-start | bytes 147464 | tf_op jit(solution)/shard_map/ppermute | solution.py:17
  36.0 19.7 %collective-permute-start.23 = (bf16[2,4,4,768]{3,0,2,1:T(2,128)(2,1)}, bf16[2,4,4,768]{3,0,2,1:T(2,128)(2,1)S(1)}, u32[]{:S(2)}, u32[]{:S(2)}) collective-permute-start(bf16[2,4,4,768]{3,0,2,1:T(2,128)(2,1)} %fusion.19), channel_id=1, source_target_pairs={{16,0},{32,16},{48,32},{64,48},{80,64},{96,80},{112,96},{128,112},... | collective-permute-start | bytes 147464 | tf_op jit(solution)/shard_map/ppermute | solution.py:17
  42.1 15.6 %collective-permute-start.24 = (bf16[2,4,4,768]{3,0,2,1:T(2,128)(2,1)}, bf16[2,4,4,768]{3,0,2,1:T(2,128)(2,1)S(1)}, u32[]{:S(2)}, u32[]{:S(2)}) collective-permute-start(bf16[2,4,4,768]{3,0,2,1:T(2,128)(2,1)} %fusion.19), channel_id=1, source_target_pairs={{32,0},{48,16},{64,32},{80,48},{96,64},{112,80},{128,96},{144,112}... | collective-permute-start | bytes 147464 | tf_op jit(solution)/shard_map/ppermute | solution.py:17
  46.2 13.5 %collective-permute-start.25 = (bf16[2,4,4,768]{3,0,2,1:T(2,128)(2,1)}, bf16[2,4,4,768]{3,0,2,1:T(2,128)(2,1)S(1)}, u32[]{:S(2)}, u32[]{:S(2)}) collective-permute-start(bf16[2,4,4,768]{3,0,2,1:T(2,128)(2,1)} %fusion.19), channel_id=1, source_target_pairs={{48,0},{64,16},{80,32},{96,48},{112,64},{128,80},{144,96},{160,112... | collective-permute-start | bytes 147464 | tf_op jit(solution)/shard_map/ppermute | solution.py:17
  51.1 12.1 %collective-permute-start.26 = (bf16[2,4,4,768]{3,0,2,1:T(2,128)(2,1)}, bf16[2,4,4,768]{3,0,2,1:T(2,128)(2,1)S(1)}, u32[]{:S(2)}, u32[]{:S(2)}) collective-permute-start(bf16[2,4,4,768]{3,0,2,1:T(2,128)(2,1)} %fusion.19), channel_id=1, source_target_pairs={{64,0},{80,16},{96,32},{112,48},{128,64},{144,80},{160,96},{176,11... | collective-permute-start | bytes 147464 | tf_op jit(solution)/shard_map/ppermute | solution.py:17
  53.1 16.2 %collective-permute-start.27 = (bf16[2,4,4,768]{3,0,2,1:T(2,128)(2,1)}, bf16[2,4,4,768]{3,0,2,1:T(2,128)(2,1)S(1)}, u32[]{:S(2)}, u32[]{:S(2)}) collective-permute-start(bf16[2,4,4,768]{3,0,2,1:T(2,128)(2,1)} %fusion.19), channel_id=1, source_target_pairs={{80,0},{96,16},{112,32},{128,48},{144,64},{160,80},{176,96},{192,1... | collective-permute-start | bytes 147464 | tf_op jit(solution)/shard_map/ppermute | solution.py:17
  55.7 15.8 %collective-permute-start.28 = (bf16[2,4,4,768]{3,0,2,1:T(2,128)(2,1)}, bf16[2,4,4,768]{3,0,2,1:T(2,128)(2,1)S(1)}, u32[]{:S(2)}, u32[]{:S(2)}) collective-permute-start(bf16[2,4,4,768]{3,0,2,1:T(2,128)(2,1)} %fusion.19), channel_id=1, source_target_pairs={{96,0},{112,16},{128,32},{144,48},{160,64},{176,80},{192,96},{208,... | collective-permute-start | bytes 147464 | tf_op jit(solution)/shard_map/ppermute | solution.py:17
  57.7 19.6 %collective-permute-start.29 = (bf16[2,4,4,768]{3,0,2,1:T(2,128)(2,1)}, bf16[2,4,4,768]{3,0,2,1:T(2,128)(2,1)S(1)}, u32[]{:S(2)}, u32[]{:S(2)}) collective-permute-start(bf16[2,4,4,768]{3,0,2,1:T(2,128)(2,1)} %fusion.19), channel_id=1, source_target_pairs={{112,0},{128,16},{144,32},{160,48},{176,64},{192,80},{208,96},{224... | collective-permute-start | bytes 147464 | tf_op jit(solution)/shard_map/ppermute | solution.py:17
  59.7 19.9 %collective-permute-start.4 = (bf16[2,8,8,768]{3,0,2,1:T(2,128)(2,1)}, bf16[2,8,8,768]{3,0,2,1:T(2,128)(2,1)S(1)}, u32[]{:S(2)}, u32[]{:S(2)}) collective-permute-start(bf16[2,8,8,768]{3,0,2,1:T(2,128)(2,1)} %fusion.18), channel_id=1, source_target_pairs={{0,48},{16,64},{32,80},{48,96},{64,112},{80,128},{96,144},{112,160... | collective-permute-start | bytes 589832 | tf_op jit(solution)/shard_map/ppermute | solution.py:17
  63.2 20.6 %collective-permute-start.5 = (bf16[2,8,8,768]{3,0,2,1:T(2,128)(2,1)}, bf16[2,8,8,768]{3,0,2,1:T(2,128)(2,1)S(1)}, u32[]{:S(2)}, u32[]{:S(2)}) collective-permute-start(bf16[2,8,8,768]{3,0,2,1:T(2,128)(2,1)} %fusion.18), channel_id=1, source_target_pairs={{0,32},{16,48},{32,64},{48,80},{64,96},{80,112},{96,128},{112,144}... | collective-permute-start | bytes 589832 | tf_op jit(solution)/shard_map/ppermute | solution.py:17
  69.3 19.9 %collective-permute-start.6 = (bf16[2,8,8,768]{3,0,2,1:T(2,128)(2,1)}, bf16[2,8,8,768]{3,0,2,1:T(2,128)(2,1)S(1)}, u32[]{:S(2)}, u32[]{:S(2)}) collective-permute-start(bf16[2,8,8,768]{3,0,2,1:T(2,128)(2,1)} %fusion.18), channel_id=1, source_target_pairs={{0,16},{16,32},{32,48},{48,64},{64,80},{80,96},{96,112},{112,128},... | collective-permute-start | bytes 589832 | tf_op jit(solution)/shard_map/ppermute | solution.py:17
  71.5 22.9 %collective-permute-start.7 = (bf16[2,8,8,768]{3,0,2,1:T(2,128)(2,1)}, bf16[2,8,8,768]{3,0,2,1:T(2,128)(2,1)S(1)}, u32[]{:S(2)}, u32[]{:S(2)}) collective-permute-start(bf16[2,8,8,768]{3,0,2,1:T(2,128)(2,1)} %fusion.18), channel_id=1, source_target_pairs={{16,0},{32,16},{48,32},{64,48},{80,64},{96,80},{112,96},{128,112},... | collective-permute-start | bytes 589832 | tf_op jit(solution)/shard_map/ppermute | solution.py:17
  77.4 18.9 %collective-permute-start.8 = (bf16[2,8,8,768]{3,0,2,1:T(2,128)(2,1)}, bf16[2,8,8,768]{3,0,2,1:T(2,128)(2,1)S(1)}, u32[]{:S(2)}, u32[]{:S(2)}) collective-permute-start(bf16[2,8,8,768]{3,0,2,1:T(2,128)(2,1)} %fusion.18), channel_id=1, source_target_pairs={{32,0},{48,16},{64,32},{80,48},{96,64},{112,80},{128,96},{144,112}... | collective-permute-start | bytes 589832 | tf_op jit(solution)/shard_map/ppermute | solution.py:17
  79.6 31.7 %collective-permute-start = (bf16[2,8,16,768]{3,2,1,0:T(8,128)(2,1)}, bf16[2,8,16,768]{3,2,1,0:T(8,128)(2,1)S(1)}, u32[]{:S(2)}, u32[]{:S(2)}) collective-permute-start(bf16[2,8,16,768]{3,2,1,0:T(8,128)(2,1)} %get-tuple-element.112), channel_id=1, source_target_pairs={{0,16},{16,32},{32,48},{48,64},{64,80},{80,96},{96,112},{112,128},... | collective-permute-start | bytes 1179656 | tf_op jit(solution)/shard_map/ppermute | solution.py:25
  83.8 28.9 %collective-permute-start.1 = (bf16[2,8,16,768]{3,2,1,0:T(8,128)(2,1)}, bf16[2,8,16,768]{3,2,1,0:T(8,128)(2,1)S(1)}, u32[]{:S(2)}, u32[]{:S(2)}) collective-permute-start(bf16[2,8,16,768]{3,2,1,0:T(8,128)(2,1)} %get-tuple-element.113), channel_id=1, source_target_pairs={{16,0},{32,16},{48,32},{64,48},{80,64},{96,80},{112,96},{128,112},... | collective-permute-start | bytes 1179656 | tf_op jit(solution)/shard_map/ppermute | solution.py:28
  89.2 140.5 %copy-start.2 = (bf16[2,8,8,768]{3,0,2,1:T(2,128)(2,1)}, bf16[2,8,8,768]{3,0,2,1:T(2,128)(2,1)S(1)}, u32[]{:S(2)}) copy-start(bf16[2,8,8,768]{3,0,2,1:T(2,128)(2,1)S(1)} %collective-permute-done.6) | copy-start | bytes 589828
  89.2 89.5 %collective-permute-start.30 = (bf16[2,60,4,768]{3,0,2,1:T(2,128)(2,1)S(1)}, bf16[2,60,4,768]{3,0,2,1:T(2,128)(2,1)S(1)}, u32[]{:S(2)}, u32[]{:S(2)}) collective-permute-start(bf16[2,60,4,768]{3,0,2,1:T(2,128)(2,1)S(1)} %constant_dynamic-update-slice_fusion.21), channel_id=1, source_target_pairs={{0,7},{1,8},{2,9},{3,10},{4,11},{5,12},{6,13},{7,14},{8,15},{16,23... | collective-permute-start | bytes 2211848 | tf_op jit(solution)/shard_map/ppermute | solution.py:17
  94.4 150.3 %copy-start.4 = (bf16[2,8,8,768]{3,0,2,1:T(2,128)(2,1)}, bf16[2,8,8,768]{3,0,2,1:T(2,128)(2,1)S(1)}, u32[]{:S(2)}) copy-start(bf16[2,8,8,768]{3,0,2,1:T(2,128)(2,1)S(1)} %collective-permute-done.7) | copy-start | bytes 589828
  94.4 10.0 %collective-permute-start.9 = (bf16[2,8,8,768]{3,0,2,1:T(2,128)(2,1)}, bf16[2,8,8,768]{3,0,2,1:T(2,128)(2,1)S(1)}, u32[]{:S(2)}, u32[]{:S(2)}) collective-permute-start(bf16[2,8,8,768]{3,0,2,1:T(2,128)(2,1)} %fusion.18), channel_id=1, source_target_pairs={{48,0},{64,16},{80,32},{96,48},{112,64},{128,80},{144,96},{160,112... | collective-permute-start | bytes 589832 | tf_op jit(solution)/shard_map/ppermute | solution.py:17
  96.3 98.2 %collective-permute-start.31 = (bf16[2,60,4,768]{3,0,2,1:T(2,128)(2,1)S(1)}, bf16[2,60,4,768]{3,0,2,1:T(2,128)(2,1)S(1)}, u32[]{:S(2)}, u32[]{:S(2)}) collective-permute-start(bf16[2,60,4,768]{3,0,2,1:T(2,128)(2,1)S(1)} %constant_dynamic-update-slice_fusion.21), channel_id=1, source_target_pairs={{0,6},{1,7},{2,8},{3,9},{4,10},{5,11},{6,12},{7,13},{8,14},{9,15},... | collective-permute-start | bytes 2211848 | tf_op jit(solution)/shard_map/ppermute | solution.py:17
  104.4 106.0 %collective-permute-start.32 = (bf16[2,60,4,768]{3,0,2,1:T(2,128)(2,1)S(1)}, bf16[2,60,4,768]{3,0,2,1:T(2,128)(2,1)S(1)}, u32[]{:S(2)}, u32[]{:S(2)}) collective-permute-start(bf16[2,60,4,768]{3,0,2,1:T(2,128)(2,1)S(1)} %constant_dynamic-update-slice_fusion.21), channel_id=1, source_target_pairs={{0,5},{1,6},{2,7},{3,8},{4,9},{5,10},{6,11},{7,12},{8,13},{9,14},{... | collective-permute-start | bytes 2211848 | tf_op jit(solution)/shard_map/ppermute | solution.py:17
  111.3 114.8 %collective-permute-start.33 = (bf16[2,60,4,768]{3,0,2,1:T(2,128)(2,1)S(1)}, bf16[2,60,4,768]{3,0,2,1:T(2,128)(2,1)S(1)}, u32[]{:S(2)}, u32[]{:S(2)}) collective-permute-start(bf16[2,60,4,768]{3,0,2,1:T(2,128)(2,1)S(1)} %constant_dynamic-update-slice_fusion.21), channel_id=1, source_target_pairs={{0,4},{1,5},{2,6},{3,7},{4,8},{5,9},{6,10},{7,11},{8,12},{9,13},{1... | collective-permute-start | bytes 2211848 | tf_op jit(solution)/shard_map/ppermute | solution.py:17
  112.7 129.2 %collective-permute-start.34 = (bf16[2,60,4,768]{3,0,2,1:T(2,128)(2,1)S(1)}, bf16[2,60,4,768]{3,0,2,1:T(2,128)(2,1)S(1)}, u32[]{:S(2)}, u32[]{:S(2)}) collective-permute-start(bf16[2,60,4,768]{3,0,2,1:T(2,128)(2,1)S(1)} %constant_dynamic-update-slice_fusion.21), channel_id=1, source_target_pairs={{0,3},{1,4},{2,5},{3,6},{4,7},{5,8},{6,9},{7,10},{8,11},{9,12},{10... | collective-permute-start | bytes 2211848 | tf_op jit(solution)/shard_map/ppermute | solution.py:17
  115.9 149.2 %copy-start.14 = (bf16[2,4,4,768]{3,0,2,1:T(2,128)(2,1)S(1)}, bf16[2,4,4,768]{3,0,2,1:T(2,128)(2,1)}, u32[]{:S(2)}) copy-start(bf16[2,4,4,768]{3,0,2,1:T(2,128)(2,1)} %copy-done.13) | copy-start | bytes 147460
  116.0 149.9 %copy-start.16 = (bf16[2,4,4,768]{3,0,2,1:T(2,128)(2,1)S(1)}, bf16[2,4,4,768]{3,0,2,1:T(2,128)(2,1)}, u32[]{:S(2)}) copy-start(bf16[2,4,4,768]{3,0,2,1:T(2,128)(2,1)} %copy-done.15) | copy-start | bytes 147460
  178.8 79.0 %collective-permute-start.35 = (bf16[2,60,4,768]{3,0,2,1:T(2,128)(2,1)S(1)}, bf16[2,60,4,768]{3,0,2,1:T(2,128)(2,1)S(1)}, u32[]{:S(2)}, u32[]{:S(2)}) collective-permute-start(bf16[2,60,4,768]{3,0,2,1:T(2,128)(2,1)S(1)} %constant_dynamic-update-slice_fusion.21), channel_id=1, source_target_pairs={{0,2},{1,3},{2,4},{3,5},{4,6},{5,7},{6,8},{7,9},{8,10},{9,11},{10,... | collective-permute-start | bytes 2211848 | tf_op jit(solution)/shard_map/ppermute | solution.py:17
  194.6 65.9 %collective-permute-start.36 = (bf16[2,60,4,768]{3,0,2,1:T(2,128)(2,1)S(1)}, bf16[2,60,4,768]{3,0,2,1:T(2,128)(2,1)S(1)}, u32[]{:S(2)}, u32[]{:S(2)}) collective-permute-start(bf16[2,60,4,768]{3,0,2,1:T(2,128)(2,1)S(1)} %constant_dynamic-update-slice_fusion.21), channel_id=1, source_target_pairs={{0,1},{1,2},{2,3},{3,4},{4,5},{5,6},{6,7},{7,8},{8,9},{9,10},{10,1... | collective-permute-start | bytes 2211848 | tf_op jit(solution)/shard_map/ppermute | solution.py:17
  210.4 62.1 %collective-permute-start.37 = (bf16[2,60,4,768]{3,0,2,1:T(2,128)(2,1)S(1)}, bf16[2,60,4,768]{3,0,2,1:T(2,128)(2,1)S(1)}, u32[]{:S(2)}, u32[]{:S(2)}) collective-permute-start(bf16[2,60,4,768]{3,0,2,1:T(2,128)(2,1)S(1)} %constant_dynamic-update-slice_fusion.21), channel_id=1, source_target_pairs={{1,0},{2,1},{3,2},{4,3},{5,4},{6,5},{7,6},{8,7},{9,8},{10,9},{11,1... | collective-permute-start | bytes 2211848 | tf_op jit(solution)/shard_map/ppermute | solution.py:17
  226.2 52.0 %collective-permute-start.38 = (bf16[2,60,4,768]{3,0,2,1:T(2,128)(2,1)S(1)}, bf16[2,60,4,768]{3,0,2,1:T(2,128)(2,1)S(1)}, u32[]{:S(2)}, u32[]{:S(2)}) collective-permute-start(bf16[2,60,4,768]{3,0,2,1:T(2,128)(2,1)S(1)} %constant_dynamic-update-slice_fusion.21), channel_id=1, source_target_pairs={{2,0},{3,1},{4,2},{5,3},{6,4},{7,5},{8,6},{9,7},{10,8},{11,9},{12,... | collective-permute-start | bytes 2211848 | tf_op jit(solution)/shard_map/ppermute | solution.py:17
  242.0 76.5 %collective-permute-start.39 = (bf16[2,60,4,768]{3,0,2,1:T(2,128)(2,1)S(1)}, bf16[2,60,4,768]{3,0,2,1:T(2,128)(2,1)S(1)}, u32[]{:S(2)}, u32[]{:S(2)}) collective-permute-start(bf16[2,60,4,768]{3,0,2,1:T(2,128)(2,1)S(1)} %constant_dynamic-update-slice_fusion.21), channel_id=1, source_target_pairs={{3,0},{4,1},{5,2},{6,3},{7,4},{8,5},{9,6},{10,7},{11,8},{12,9},{13... | collective-permute-start | bytes 2211848 | tf_op jit(solution)/shard_map/ppermute | solution.py:17
  257.8 62.6 %collective-permute-start.40 = (bf16[2,60,4,768]{3,0,2,1:T(2,128)(2,1)S(1)}, bf16[2,60,4,768]{3,0,2,1:T(2,128)(2,1)S(1)}, u32[]{:S(2)}, u32[]{:S(2)}) collective-permute-start(bf16[2,60,4,768]{3,0,2,1:T(2,128)(2,1)S(1)} %constant_dynamic-update-slice_fusion.21), channel_id=1, source_target_pairs={{4,0},{5,1},{6,2},{7,3},{8,4},{9,5},{10,6},{11,7},{12,8},{13,9},{1... | collective-permute-start | bytes 2211848 | tf_op jit(solution)/shard_map/ppermute | solution.py:17
  260.4 110.0 %collective-permute-start.41 = (bf16[2,60,4,768]{3,0,2,1:T(2,128)(2,1)S(1)}, bf16[2,60,4,768]{3,0,2,1:T(2,128)(2,1)S(1)}, u32[]{:S(2)}, u32[]{:S(2)}) collective-permute-start(bf16[2,60,4,768]{3,0,2,1:T(2,128)(2,1)S(1)} %constant_dynamic-update-slice_fusion.21), channel_id=1, source_target_pairs={{5,0},{6,1},{7,2},{8,3},{9,4},{10,5},{11,6},{12,7},{13,8},{14,9},{... | collective-permute-start | bytes 2211848 | tf_op jit(solution)/shard_map/ppermute | solution.py:17
  272.5 164.6 %collective-permute-start.42 = (bf16[2,60,4,768]{3,0,2,1:T(2,128)(2,1)S(1)}, bf16[2,60,4,768]{3,0,2,1:T(2,128)(2,1)S(1)}, u32[]{:S(2)}, u32[]{:S(2)}) collective-permute-start(bf16[2,60,4,768]{3,0,2,1:T(2,128)(2,1)S(1)} %constant_dynamic-update-slice_fusion.21), channel_id=1, source_target_pairs={{6,0},{7,1},{8,2},{9,3},{10,4},{11,5},{12,6},{13,7},{14,8},{15,9},... | collective-permute-start | bytes 2211848 | tf_op jit(solution)/shard_map/ppermute | solution.py:17
  278.2 190.7 %collective-permute-start.43 = (bf16[2,60,4,768]{3,0,2,1:T(2,128)(2,1)S(1)}, bf16[2,60,4,768]{3,0,2,1:T(2,128)(2,1)S(1)}, u32[]{:S(2)}, u32[]{:S(2)}) collective-permute-start(bf16[2,60,4,768]{3,0,2,1:T(2,128)(2,1)S(1)} %constant_dynamic-update-slice_fusion.21), channel_id=1, source_target_pairs={{7,0},{8,1},{9,2},{10,3},{11,4},{12,5},{13,6},{14,7},{15,8},{23,16... | collective-permute-start | bytes 2211848 | tf_op jit(solution)/shard_map/ppermute | solution.py:17
  318.5 190.9 %collective-permute-start.2 = (bf16[2,32,8,768]{3,2,1,0:T(8,128)(2,1)}, bf16[2,32,8,768]{3,2,1,0:T(8,128)(2,1)}, u32[]{:S(2)}, u32[]{:S(2)}) collective-permute-start(bf16[2,32,8,768]{3,2,1,0:T(8,128)(2,1)} %get-tuple-element.110), channel_id=1, source_target_pairs={{0,1},{1,2},{2,3},{3,4},{4,5},{5,6},{6,7},{7,8},{8,9},{9,10},{10,1... | collective-permute-start | bytes 2359304 | tf_op jit(solution)/shard_map/ppermute | solution.py:25
  320.4 192.6 %collective-permute-start.3 = (bf16[2,32,8,768]{3,2,1,0:T(8,128)(2,1)}, bf16[2,32,8,768]{3,2,1,0:T(8,128)(2,1)}, u32[]{:S(2)}, u32[]{:S(2)}) collective-permute-start(bf16[2,32,8,768]{3,2,1,0:T(8,128)(2,1)} %get-tuple-element.111), channel_id=1, source_target_pairs={{1,0},{2,1},{3,2},{4,3},{5,4},{6,5},{7,6},{8,7},{9,8},{10,9},{11,1... | collective-permute-start | bytes 2359304 | tf_op jit(solution)/shard_map/ppermute | solution.py:28
  370.5 192.4 %collective-permute-start.10 = (bf16[2,56,8,768]{3,0,2,1:T(2,128)(2,1)}, bf16[2,56,8,768]{3,0,2,1:T(2,128)(2,1)}, u32[]{:S(2)}, u32[]{:S(2)}) collective-permute-start(bf16[2,56,8,768]{3,0,2,1:T(2,128)(2,1)} %constant_dynamic-update-slice_fusion.1), channel_id=1, source_target_pairs={{0,3},{1,4},{2,5},{3,6},{4,7},{5,8},{6,9},{7,10},{8,11},{9,12},{10... | collective-permute-start | bytes 4128776 | tf_op jit(solution)/shard_map/ppermute | solution.py:17
  437.1 130.8 %collective-permute-start.11 = (bf16[2,56,8,768]{3,0,2,1:T(2,128)(2,1)}, bf16[2,56,8,768]{3,0,2,1:T(2,128)(2,1)}, u32[]{:S(2)}, u32[]{:S(2)}) collective-permute-start(bf16[2,56,8,768]{3,0,2,1:T(2,128)(2,1)} %constant_dynamic-update-slice_fusion.1), channel_id=1, source_target_pairs={{0,2},{1,3},{2,4},{3,5},{4,6},{5,7},{6,8},{7,9},{8,10},{9,11},{10,... | collective-permute-start | bytes 4128776 | tf_op jit(solution)/shard_map/ppermute | solution.py:17
  468.8 102.5 %collective-permute-start.12 = (bf16[2,56,8,768]{3,0,2,1:T(2,128)(2,1)}, bf16[2,56,8,768]{3,0,2,1:T(2,128)(2,1)}, u32[]{:S(2)}, u32[]{:S(2)}) collective-permute-start(bf16[2,56,8,768]{3,0,2,1:T(2,128)(2,1)} %constant_dynamic-update-slice_fusion.1), channel_id=1, source_target_pairs={{0,1},{1,2},{2,3},{3,4},{4,5},{5,6},{6,7},{7,8},{8,9},{9,10},{10,1... | collective-permute-start | bytes 4128776 | tf_op jit(solution)/shard_map/ppermute | solution.py:17
  509.4 71.4 %collective-permute-start.13 = (bf16[2,56,8,768]{3,0,2,1:T(2,128)(2,1)}, bf16[2,56,8,768]{3,0,2,1:T(2,128)(2,1)}, u32[]{:S(2)}, u32[]{:S(2)}) collective-permute-start(bf16[2,56,8,768]{3,0,2,1:T(2,128)(2,1)} %constant_dynamic-update-slice_fusion.1), channel_id=1, source_target_pairs={{1,0},{2,1},{3,2},{4,3},{5,4},{6,5},{7,6},{8,7},{9,8},{10,9},{11,1... | collective-permute-start | bytes 4128776 | tf_op jit(solution)/shard_map/ppermute | solution.py:17
  513.1 71.2 %collective-permute-start.14 = (bf16[2,56,8,768]{3,0,2,1:T(2,128)(2,1)}, bf16[2,56,8,768]{3,0,2,1:T(2,128)(2,1)}, u32[]{:S(2)}, u32[]{:S(2)}) collective-permute-start(bf16[2,56,8,768]{3,0,2,1:T(2,128)(2,1)} %constant_dynamic-update-slice_fusion.1), channel_id=1, source_target_pairs={{2,0},{3,1},{4,2},{5,3},{6,4},{7,5},{8,6},{9,7},{10,8},{11,9},{12,... | collective-permute-start | bytes 4128776 | tf_op jit(solution)/shard_map/ppermute | solution.py:17
  562.9 47.9 %collective-permute-start.15 = (bf16[2,56,8,768]{3,0,2,1:T(2,128)(2,1)}, bf16[2,56,8,768]{3,0,2,1:T(2,128)(2,1)S(1)}, u32[]{:S(2)}, u32[]{:S(2)}) collective-permute-start(bf16[2,56,8,768]{3,0,2,1:T(2,128)(2,1)} %constant_dynamic-update-slice_fusion.1), channel_id=1, source_target_pairs={{3,0},{4,1},{5,2},{6,3},{7,4},{8,5},{9,6},{10,7},{11,8},{12,9},{13... | collective-permute-start | bytes 4128776 | tf_op jit(solution)/shard_map/ppermute | solution.py:17
  (14 other events, 454.8 us)
where the time goes:
time: 768 us; the launch traced here: 753 us
  waiting for transfers between devices  229 us (30%)
  starting transfers between devices  216 us (28%)
  local copies, waits for them, and re-layouts  214 us (28%)
  other arithmetic  67.9 us (9%)
  matrix products  22.5 us (3%)
    ppermute x40, waiting for transfers between devices, passed_along(): lax.ppermute(value, axis, [(source, source + steps) for source in range(i...  229 us
    ppermute x40, starting transfers between devices, passed_along(): lax.ppermute(value, axis, [(source, source + steps) for source in range(i...  186 us
    unnamed x92, local copies, waits for them, and re-layouts  54.8 us
    gather x2, local copies, waits for them, and re-layouts, pick_block(): lax.dynamic_slice(coarse_grid, (anchor_zero, start_row, start_col, anchor...  37.8 us
    while x3, local copies, waits for them, and re-layouts, attend(): outputs = lax.map(one_pair, (query_pairs, near_pairs, far_pairs))  32.8 us
    ppermute x2, starting transfers between devices, extended(): lax.ppermute(lax.slice_in_dim(block, 0, width, axis=dim), axis, backward)  24.7 us
    concatenate x2, local copies, waits for them, and re-layouts, attend(): far_all = jnp.concatenate([pair_kv for pair_kv, usable in far_sets], axis=1)  23.4 us
    reduce_sum x12, other arithmetic, one_pair(): totals = jnp.sum(near_weights, axis=3) + jnp.sum(far_weights, axis=3)  19.2 us
  transfers between devices with their start and end apart: 44, of which 11 were waited for; matrix products, arithmetic and copies ran while one was open for 21% of the time, Pallas kernels for 0%

commit v1 on v0

v1 whole, which is shorter than its diff:
```python
import math

import jax
import jax.numpy as jnp
import numpy as np
from jax import lax
from jax.experimental import pallas as pl
from jax.experimental.pallas import tpu as pltpu
from jax.sharding import Mesh, PartitionSpec as P

BF = jnp.bfloat16
F32 = jnp.float32
NEG = -1e30
VMEM = pl.BlockSpec(memory_space=pltpu.VMEM)
SMEM = pl.BlockSpec(memory_space=pltpu.SMEM)


def split_bias(level):
    full = 2.0 * level * math.log(2.0)
    high = float(np.float32(full).astype(BF))
    return high, float(np.float32(full - high).astype(BF))


def iota(shape, dim):
    return lax.broadcasted_iota(jnp.int32, shape, dim)


def prep_kernel(q_ref, k_ref, v_ref, coarse_ref, fine_ref):
    row = iota((80, 256), 0)
    tok = iota((80, 256), 1)
    trow, tcol = tok >> 4, tok & 15
    one = (row < 64) & ((trow >> 1) == (row >> 3)) & ((tcol >> 1) == (row & 7))
    rest = row - 64
    two = (row >= 64) & ((trow >> 2) == (rest >> 2)) & ((tcol >> 2) == (rest & 3))
    pool = jnp.where(one, 0.25, jnp.where(two, 0.0625, 0.0)).astype(BF)
    k = k_ref[...]
    v = v_ref[...]
    kc = jnp.dot(pool, k, preferred_element_type=F32).astype(BF)
    vc = jnp.dot(pool, v, preferred_element_type=F32).astype(BF)
    q = (q_ref[...].astype(F32) * 0.125).astype(BF)
    for j in range(4):
        pair = slice(128 * j, 128 * j + 128)
        third = slice(512 + 64 * j, 576 + 64 * j)
        fine_ref[j, 0:256, 0:128] = k[:, pair]
        fine_ref[j, 0:256, 128:256] = v[:, pair]
        fine_ref[j, 0:256, 256:384] = jnp.concatenate([k[:, third], v[:, third]], axis=1)
        fine_ref[j, 256:384, 0:128] = q[0:128, pair]
        fine_ref[j, 256:384, 128:256] = q[128:256, pair]
        fine_ref[j, 256:384, 256:384] = jnp.concatenate(
            [q[0:128, third], q[128:256, third]], axis=1
        )
        both = jnp.concatenate([kc[:, third], vc[:, third]], axis=1)
        for core in range(2):
            coarse_ref[j, core, :, 0:128] = kc[:, pair]
            coarse_ref[j, core, :, 128:256] = vc[:, pair]
            coarse_ref[j, core, :, 256:384] = both


def unpack_kernel(o_ref, out_ref):
    for j in range(4):
        pair = slice(128 * j, 128 * j + 128)
        out_ref[0:128, pair] = o_ref[j, :, 0:128]
        out_ref[128:256, pair] = o_ref[j, :, 128:256]
    lane = iota((128, 128), 1)
    for j in (0, 2):
        first = o_ref[j, :, 256:384]
        second = o_ref[j + 1, :, 256:384]
        lanes = slice(512 + 64 * j, 640 + 64 * j)
        out_ref[0:128, lanes] = jnp.concatenate([first[:, :64], second[:, :64]], axis=1)
        out_ref[128:256, lanes] = jnp.concatenate([first[:, 64:], second[:, 64:]], axis=1)


NEAR = 1024
FAR = 27 * 64
KEYS = NEAR + 2 * FAR


def attend_kernel(
    place_ref, idx_one_ref, idx_two_ref,
    own_ref, inner_ref, outer_ref, q_ref, rc_ref, side_ref, ys_ref,
    out_ref, one_ref, two_ref, kv_ref, s_ref, p_ref,
):
    y = place_ref[0]
    z = place_ref[1]
    core = place_ref[2]

    def quarter(xs, kk):
        return slice(32 * (xs & 1) + 16 * kk, 32 * (xs & 1) + 16 * kk + 16)

    for xs in range(4):
        for kk in range(2):
            one_ref[(2 + xs) * 6 + 2 + kk] = rc_ref[xs, kk, 0:64]
            two_ref[(3 + xs // 2) * 7 + 3, quarter(xs, kk)] = rc_ref[xs, kk, 64:80]
    for s in range(2):
        for xs in range(4):
            for kk in range(2):
                base = (2 * xs + kk) * 80
                one_ref[(2 + xs) * 6 + 4 * s + kk] = side_ref[s, base:base + 64]
                col = 2 if s == 0 else 4
                two_ref[(3 + xs // 2) * 7 + col, quarter(xs, kk)] = side_ref[s, base + 64:base + 80]
                for far in (2, 3):
                    at = 640 + 128 * (far - 2) + (2 * xs + kk) * 16
                    col = 3 - far if s == 0 else 3 + far
                    two_ref[(3 + xs // 2) * 7 + col, quarter(xs, kk)] = side_ref[s, at:at + 16]
        for d in range(2):
            at0 = 832 * d
            for i in range(2):
                one_ref[(6 * d + i) * 6 + 2 + s] = ys_ref[s, at0 + 64 * i:at0 + 64 * i + 64]
                for kk in range(2):
                    at = at0 + 128 + (2 * i + kk) * 64
                    one_ref[(6 * d + i) * 6 + 4 * s + kk] = ys_ref[s, at:at + 64]
            brow = 1 + 4 * d
            for xs in range(4):
                at = at0 + 384 + xs * 16
                two_ref[(brow + xs // 2) * 7 + 3, quarter(xs, s)] = ys_ref[s, at:at + 16]
                for far in (1, 2, 3):
                    col = 3 - far if s == 0 else 3 + far
                    for kk in range(2):
                        at = at0 + 448 + 128 * (far - 1) + (2 * xs + kk) * 16
                        two_ref[(brow + xs // 2) * 7 + col, quarter(xs, kk)] = ys_ref[s, at:at + 16]
        brow = jnp.where(y >= 2, 0, 7)
        for i in range(2):
            at = 1664 + 16 * i
            two_ref[brow * 7 + 3, quarter(i, s)] = ys_ref[s, at:at + 16]
            for far in (1, 2, 3):
                col = 3 - far if s == 0 else 3 + far
                for kk in range(2):
                    at = 1664 + 32 + 64 * (far - 1) + (2 * i + kk) * 16
                    two_ref[brow * 7 + col, quarter(i, kk)] = ys_ref[s, at:at + 16]

    lane64 = iota((64, 128), 1)
    high_one, low_one = split_bias(1)
    high_two, low_two = split_bias(2)
    tok = iota((256, 128), 0)
    lane = iota((256, 128), 1)
    block = ((tok >> 7) << 1) + ((tok >> 3) & 1)
    q_feat = jnp.where((lane == block) | (lane == 4) | (lane == 5), 1.0, 0.0).astype(BF)

    def near_features(rows_wide, wide_log, col_base, tile):
        count = rows_wide << wide_log
        key = iota((count, 128), 0)
        ln = iota((count, 128), 1)
        wr = key >> wide_log
        wc = (key & ((1 << wide_log) - 1)) + col_base
        br, bc = ln >> 1, ln & 1
        row = 64 * y + 16 * tile - 8 + wr
        col = 32 * z + 16 * core - 8 + wc
        ok = (wr >= 8 * br) & (wr < 8 * br + 24) & (wc >= 8 * bc) & (wc < 8 * bc + 24)
        ok = ok & (row >= 0) & (row < 256) & (col >= 0) & (col < 256)
        return jnp.where((ln < 4) & jnp.logical_not(ok), NEG, 0.0).astype(BF)

    def place_rows(at, size, packed, features):
        kv_ref[at:at + size, 0:128] = packed[:, 0:128]
        kv_ref[at:at + size, 128:256] = features
        kv_ref[at:at + size, 256:384] = packed[:, 256:384]
        kv_ref[at:at + size, 384:512] = packed[:, 128:256]

    def one_tile(tile, carry):
        at = pl.multiple_of(tile * 256, 256)
        place_rows(0, 512, own_ref[pl.ds(at, 512)], near_features(32, 4, 8, tile))
        at = pl.multiple_of(tile * 128, 128)
        inner_col = 24 - 24 * core
        place_rows(512, 256, inner_ref[pl.ds(at, 256)], near_features(32, 3, inner_col, tile))
        place_rows(768, 256, outer_ref[pl.ds(at, 256)], near_features(32, 3, 24 - inner_col, tile))

        def far_block(j, c):
            for level, (idx_ref, win_ref, trow, high, low) in enumerate((
                (idx_one_ref, one_ref, tile, high_one, low_one),
                (idx_two_ref, two_ref, tile // 2, high_two, low_two),
            )):
                index = idx_ref[trow, j]
                packed = win_ref[jnp.maximum(index, 0)]
                top = jnp.where(index >= 0, jnp.float32(high), jnp.float32(NEG))
                feat = jnp.where(lane64 == 4, top, jnp.where(lane64 == 5, low, 0.0)).astype(BF)
                start = pl.multiple_of(NEAR + level * FAR + j * 64, 64)
                kv_ref[pl.ds(start, 64), 0:128] = packed[:, 0:128]
                kv_ref[pl.ds(start, 64), 128:256] = feat
                kv_ref[pl.ds(start, 64), 256:384] = packed[:, 256:384]
                kv_ref[pl.ds(start, 64), 384:512] = packed[:, 128:256]
            return c

        lax.fori_loop(0, 27, far_block, 0)

        q_pair = jnp.concatenate([q_ref[tile, 0:128, 0:128], q_ref[tile, 0:128, 128:256]], axis=0)
        q_last = q_ref[tile, 0:128, 256:384]
        q_third = jnp.concatenate([q_last, jnp.concatenate([q_last[:, 64:], q_last[:, :64]], axis=1)], axis=0)
        zero = jnp.zeros_like(q_pair)
        low_half = lane < 64
        outs = []
        for head in range(3):
            if head < 2:
                keep = low_half if head == 0 else jnp.logical_not(low_half)
                lhs = jnp.concatenate([jnp.where(keep, q_pair, zero), q_feat], axis=1)
                k_lanes, v_lanes = slice(0, 256), slice(384, 512)
            else:
                lhs = jnp.concatenate([q_feat, jnp.where(low_half, q_third, zero)], axis=1)
                k_lanes, v_lanes = slice(128, 384), slice(256, 384)
            s_ref[...] = lax.dot_general(
                lhs, kv_ref[:, k_lanes], (((1,), (1,)), ((), ())), preferred_element_type=F32
            )
            top = jnp.max(s_ref[...], axis=1, keepdims=True)
            weights = jnp.exp(s_ref[...] - top)
            total = jnp.sum(weights, axis=1, keepdims=True)
            p_ref[...] = weights.astype(BF)
            acc = jnp.dot(p_ref[...], kv_ref[:, v_lanes], preferred_element_type=F32)
            outs.append(acc / total)
        pair_out = jnp.where(low_half, outs[0], outs[1])
        third_out = outs[2]
        out_ref[tile, :, 0:128] = pair_out[0:128].astype(BF)
        out_ref[tile, :, 128:256] = pair_out[128:256].astype(BF)
        out_ref[tile, :, 256:384] = jnp.concatenate(
            [third_out[0:128, 64:], third_out[128:256, 64:]], axis=1
        ).astype(BF)
        return carry

    lax.fori_loop(0, 4, one_tile, 0)


def call(kernel, out_shape, in_specs, scratch=(), flops=0, nbytes=0):
    return pl.pallas_call(
        kernel,
        out_shape=out_shape,
        in_specs=in_specs,
        out_specs=jax.tree.map(lambda _: VMEM, out_shape),
        scratch_shapes=scratch,
        compiler_params=pltpu.CompilerParams(vmem_limit_bytes=56 * 2**20),
        cost_estimate=pl.CostEstimate(flops=flops, bytes_accessed=nbytes, transcendentals=0),
    )


def shape(*dims):
    return jax.ShapeDtypeStruct(dims, BF)


def z_perm(step):
    pairs = []
    for z in range(8):
        if z + step < 8:
            pairs.append((2 * z + 1, 2 * (z + step)))
        if z - step >= 0:
            pairs.append((2 * z, 2 * (z - step) + 1))
    return pairs


def body(queries, keys, values, list_one, list_two):
    y = lax.axis_index("y")
    x = lax.axis_index("x")
    z = lax.axis_index("z")
    core = lax.axis_index("core")
    up = [(i, i + 1) for i in range(3)]
    down = [(i + 1, i) for i in range(3)]
    across = [(i, i ^ 2) for i in range(4)]

    coarse, fine = call(
        prep_kernel, [shape(4, 2, 80, 384), shape(4, 384, 384)], [VMEM] * 3, nbytes=4 << 20
    )(queries.reshape(256, 768), keys.reshape(256, 768), values.reshape(256, 768))

    rc = lax.all_to_all(coarse.reshape(8, 80, 384), ("x", "core"), 0, 0, tiled=True)
    rc = rc.reshape(4, 2, 80, 384)

    z_one = lax.ppermute(rc, ("z", "core"), z_perm(1))
    last = rc[:, :, 64:80]
    z_two = lax.ppermute(last, ("z", "core"), z_perm(2))
    z_three = lax.ppermute(last, ("z", "core"), z_perm(3))

    rf = lax.all_to_all(fine, "x", 0, 0, tiled=True)
    tokens = rf[:, 0:256].reshape(64, 16, 384)
    top = lax.ppermute(tokens[56:64], "y", up)
    bottom = lax.ppermute(tokens[0:8], "y", down)
    tall = jnp.concatenate([top, tokens, bottom], axis=0)
    left, right = tall[:, 0:8], tall[:, 8:16]
    inner = lax.ppermute(jnp.where(core == 0, right, left).reshape(640, 384), "core", [(0, 1), (1, 0)])
    outer = lax.ppermute(jnp.where(core == 0, left, right).reshape(640, 384), ("z", "core"), z_perm(1))

    mine = lax.dynamic_index_in_dim(rc, core, 1, keepdims=False)

    def y_part(rows):
        return jnp.concatenate(
            [
                mine[rows, 0:64].reshape(128, 384),
                z_one[rows, :, 0:64].reshape(256, 384),
                mine[:, 64:80].reshape(64, 384),
                z_one[:, :, 64:80].reshape(128, 384),
                z_two.reshape(128, 384),
                z_three.reshape(128, 384),
            ],
            axis=0,
        )

    from_up = lax.ppermute(y_part(slice(2, 4)), "y", up)
    from_down = lax.ppermute(y_part(slice(0, 2)), "y", down)
    half = jnp.where(y < 2, 2, 0)

    def picked(array):
        return lax.dynamic_slice_in_dim(array, half, 2, axis=0)

    from_across = lax.ppermute(
        jnp.concatenate(
            [
                picked(mine)[:, 64:80].reshape(32, 384),
                picked(z_one)[:, :, 64:80].reshape(64, 384),
                picked(z_two).reshape(64, 384),
                picked(z_three).reshape(64, 384),
            ],
            axis=0,
        ),
        "y",
        across,
    )

    side = lax.all_gather(
        jnp.concatenate(
            [z_one.reshape(640, 384), z_two.reshape(128, 384), z_three.reshape(128, 384)], axis=0
        ),
        "core",
    )
    ys = lax.all_gather(jnp.concatenate([from_up, from_down, from_across], axis=0), "core")

    rows_one = 4 * y + jnp.arange(4, dtype=jnp.int32)
    entries = list_one[rows_one * 16 + 2 * z + core]
    place = (entries // 16 - (4 * y - 2)) * 6 + entries % 16 - (2 * z - 2)
    idx_one = jnp.where(entries >= 0, place, -1)
    rows_two = 2 * y + jnp.arange(2, dtype=jnp.int32)
    entries = list_two[rows_two * 8 + z]
    place = (entries // 8 - (2 * y - 3)) * 7 + entries % 8 - (z - 3)
    idx_two = jnp.where(entries >= 0, place, -1)

    out = call(
        attend_kernel,
        shape(4, 128, 384),
        [SMEM] * 3 + [VMEM] * 7,
        scratch=[
            pltpu.VMEM((48, 64, 384), BF),
            pltpu.VMEM((56, 64, 384), BF),
            pltpu.VMEM((KEYS, 512), BF),
            pltpu.VMEM((256, KEYS), F32),
            pltpu.VMEM((256, KEYS), BF),
        ],
        flops=12 * 256 * KEYS * 768,
        nbytes=10 << 20,
    )(
        jnp.stack([y, z, core]).astype(jnp.int32), idx_one, idx_two,
        tall.reshape(1280, 384), inner, outer, rf[:, 256:384], rc, side, ys,
    )
    back = lax.all_to_all(out, "x", 0, 0, tiled=True)
    tile = call(unpack_kernel, shape(256, 768), [VMEM], nbytes=1 << 20)(back)
    return tile.reshape(16, 16, 768)


def solution(mesh):
    fine_mesh = Mesh(mesh.devices.reshape(4, 4, 8, 2), ("y", "x", "z", "core"))
    spec = P(("y", "x"), ("z", "core"), None)
    return jax.shard_map(
        body, mesh=fine_mesh, in_specs=(spec, spec, spec, P(), P()), out_specs=spec, check_vma=False
    )
```

time: 768 us -> 171 us (0.22)
  the two profiles are of different devices: /device:TPU:48 before, /device:TPU:65 now
where the time goes in v1:
time: 171 us; the launch traced here: 170 us
  waiting for transfers between devices  53.4 us (31%)
  starting transfers between devices  42.7 us (25%)
  Pallas kernels  36.9 us (22%)
  between operations  13.7 us (8%)
  blocking collectives  12.8 us (7%)
  local copies, waits for them, and re-layouts  6.44 us (4%)
  other arithmetic  4.37 us (3%)
    pallas_call x1, Pallas kernels, body(): call(attend_kernel, shape(4, 128, 384), [SMEM] * 3 + [VMEM] * 7, scratch=...  32.3 us
    all_to_all x1, waiting for transfers between devices, body(): rf = lax.all_to_all(fine, 'x', 0, 0, tiled=True)  16.5 us
    ppermute x1, waiting for transfers between devices, body(): lax.ppermute(jnp.concatenate([picked(mine)[:, 64:80].reshape(32, 384), pi...  14.6 us
    all_to_all x1, blocking collectives, body(): back = lax.all_to_all(out, 'x', 0, 0, tiled=True)  12.8 us
    all_to_all x1, waiting for transfers between devices, body(): lax.all_to_all(coarse.reshape(8, 80, 384), ('x', 'core'), 0, 0, tiled=True)  9.13 us
    ppermute x1, starting transfers between devices, body(): z_three = lax.ppermute(last, ('z', 'core'), z_perm(3))  7.32 us
    ppermute x1, starting transfers between devices, body(): lax.ppermute(jnp.where(core == 0, left, right).reshape(640, 384), ('z', '...  6.01 us
    ppermute x1, starting transfers between devices, body(): top = lax.ppermute(tokens[56:64], 'y', up)  5.12 us
  transfers between devices with their start and end apart: 14, of which 8 were waited for; matrix products, arithmetic and copies ran while one was open for 6% of the time, Pallas kernels for 0%

profile of v1, /device:TPU:65, one launch (start us, length us, event | category | flops | bytes accessed | tf_op | source)
XLA Modules:
  0.0 170.3 jit_solution(15721950632510563567)
XLA Ops:
  6.5 2.8 %shard_map.55 = (bf16[4,2,80,384]{3,2,1,0:T(8,128)(2,1)}, bf16[4,384,384]{2,1,0:T(8,128)(2,1)}) custom-call(bf16[256,768]{1,0:T(8,128)(2,1)} %bitcast.58, bf16[256,768]{1,0:T(8,128)(2,1)} %bitcast.59, bf16[256,768]{1,0:T(8,128)(2,1)} %bitcast.60), custom_call_target="tpu_custom_call" | custom-call | bytes 4194304 | tf_op jit(solution)/shard_map/pallas_call | solution.py:254
  9.3 5.0 %all-to-all-start.1 = ((bf16[8,80,384]{2,1,0:T(8,128)(2,1)}), bf16[8,80,384]{2,1,0:T(8,128)(2,1)S(1)}, u32[]{:S(2)}, u32[]{:S(2)}) async-start(bf16[8,80,384]{2,1,0:T(8,128)(2,1)} %bitcast.54), calls=%async_computation.1 | async-start | bytes 983040 | tf_op jit(solution)/shard_map/all_to_all | solution.py:258
  14.3 9.1 %all-to-all-done.1 = bf16[8,80,384]{2,1,0:T(8,128)(2,1)S(1)} async-done(((bf16[8,80,384]{2,1,0:T(8,128)(2,1)}), bf16[8,80,384]{2,1,0:T(8,128)(2,1)S(1)}, u32[]{:S(2)}, u32[]{:S(2)}) %all-to-all-start.1) | async-done | bytes 491552 | tf_op jit(solution)/shard_map/all_to_all | solution.py:258
  23.4 7.3 %collective-permute-start.6 = (bf16[4,2,16,384]{3,2,1,0:T(8,128)(2,1)S(1)}, bf16[4,2,16,384]{3,2,1,0:T(8,128)(2,1)S(1)}, u32[]{:S(2)}, u32[]{:S(2)}) collective-permute-start(bf16[4,2,16,384]{3,2,1,0:T(8,128)(2,1)S(1)} %slice.72), channel_id=1, source_target_pairs={{1,6},{3,8},{5,10},{7,12},{6,1},{9,14},{8,3},{10,5},{12,7},{14,9},... | collective-permute-start | bytes 294920 | tf_op jit(solution)/shard_map/ppermute | solution.py:264
  30.8 1.9 %collective-permute-start.5 = (bf16[4,2,16,384]{3,2,1,0:T(8,128)(2,1)S(1)}, bf16[4,2,16,384]{3,2,1,0:T(8,128)(2,1)S(1)}, u32[]{:S(2)}, u32[]{:S(2)}) collective-permute-start(bf16[4,2,16,384]{3,2,1,0:T(8,128)(2,1)S(1)} %slice.72), channel_id=1, source_target_pairs={{1,4},{3,6},{5,8},{4,1},{7,10},{6,3},{9,12},{8,5},{11,14},{10,7},{... | collective-permute-start | bytes 294920 | tf_op jit(solution)/shard_map/ppermute | solution.py:263
  32.7 4.1 %collective-permute-start.4 = (bf16[4,2,80,384]{3,2,1,0:T(8,128)(2,1)S(1)}, bf16[4,2,80,384]{3,2,1,0:T(8,128)(2,1)S(1)}, u32[]{:S(2)}, u32[]{:S(2)}) collective-permute-start(bf16[4,2,80,384]{3,2,1,0:T(8,128)(2,1)S(1)} %bitcast.43), channel_id=1, source_target_pairs={{1,2},{3,4},{2,1},{5,6},{4,3},{7,8},{6,5},{9,10},{8,7},{11,12},{10... | collective-permute-start | bytes 1474568 | tf_op jit(solution)/shard_map/ppermute | solution.py:261
  36.9 0.7 constant_dynamic-update-slice_fusion.5
  37.6 2.4 %collective-permute-done.5 = bf16[4,2,16,384]{3,2,1,0:T(8,128)(2,1)S(1)} collective-permute-done((bf16[4,2,16,384]{3,2,1,0:T(8,128)(2,1)S(1)}, bf16[4,2,16,384]{3,2,1,0:T(8,128)(2,1)S(1)}, u32[]{:S(2)}, u32[]{:S(2)}) %collective-permute-start.5) | collective-permute-done | bytes 98336 | tf_op jit(solution)/shard_map/ppermute | solution.py:263
  40.0 4.1 %collective-permute-done.4 = bf16[4,2,80,384]{3,2,1,0:T(8,128)(2,1)S(1)} collective-permute-done((bf16[4,2,80,384]{3,2,1,0:T(8,128)(2,1)S(1)}, bf16[4,2,80,384]{3,2,1,0:T(8,128)(2,1)S(1)}, u32[]{:S(2)}, u32[]{:S(2)}) %collective-permute-start.4) | collective-permute-done | bytes 491552 | tf_op jit(solution)/shard_map/ppermute | solution.py:261
  44.1 0.9 pad_maximum_fusion.2
  45.0 0.0 all-gather.5.cloned.1.call-update
  45.0 0.0 all-gather.7.cloned.1.call-start
  45.1 0.0 slice-start
  45.2 0.7 constant_dynamic-update-slice_fusion.4
  45.9 0.0 slice-done
  45.9 0.6 constant_dynamic-update-slice_fusion.3
  46.5 0.7 constant_dynamic-update-slice_fusion.2
  47.2 0.7 constant_dynamic-update-slice_fusion.1
  47.9 0.7 constant_dynamic-update-slice_fusion
  48.5 3.2 %collective-permute-start.7 = (bf16[832,384]{1,0:T(8,128)(2,1)}, bf16[832,384]{1,0:T(8,128)(2,1)S(1)}, u32[]{:S(2)}, u32[]{:S(2)}) collective-permute-start(bf16[832,384]{1,0:T(8,128)(2,1)} %get-tuple-element.17), channel_id=1, source_target_pairs={{0,64},{64,128},{128,192},{1,65},{65,129},{129,193},{2,66},{66,130... | collective-permute-start | bytes 1916936 | tf_op jit(solution)/shard_map/ppermute | solution.py:290
  51.8 1.3 collective-permute-start.8
  53.2 3.8 %collective-permute-start.9 = (bf16[224,384]{1,0:T(8,128)(2,1)S(1)}, bf16[224,384]{1,0:T(8,128)(2,1)S(1)}, u32[]{:S(2)}, u32[]{:S(2)}) collective-permute-start(bf16[224,384]{1,0:T(8,128)(2,1)S(1)} %pad_maximum_fusion.3), channel_id=1, source_target_pairs={{0,128},{64,192},{128,0},{192,64},{1,129},{65,193},{129,1},{193,65... | collective-permute-start | bytes 516104 | tf_op jit(solution)/shard_map/ppermute | solution.py:297
  57.0 14.6 %collective-permute-done.9 = bf16[224,384]{1,0:T(8,128)(2,1)S(1)} collective-permute-done((bf16[224,384]{1,0:T(8,128)(2,1)S(1)}, bf16[224,384]{1,0:T(8,128)(2,1)S(1)}, u32[]{:S(2)}, u32[]{:S(2)}) %collective-permute-start.9) | collective-permute-done | bytes 172064 | tf_op jit(solution)/shard_map/ppermute | solution.py:297
  71.5 1.3 pad_maximum_fusion
  72.9 0.0 all-gather.7.cloned.1.call-update
  72.9 3.5 %all-to-all-start = ((bf16[4,384,384]{2,1,0:T(8,128)(2,1)}), bf16[4,384,384]{2,1,0:T(8,128)(2,1)S(1)}, u32[]{:S(2)}, u32[]{:S(2)}) async-start(bf16[4,384,384]{2,1,0:T(8,128)(2,1)} %get-tuple-element.7), calls=%async_computation | async-start | bytes 2359296 | tf_op jit(solution)/shard_map/all_to_all | solution.py:266
  76.5 16.5 %all-to-all-done = bf16[4,384,384]{2,1,0:T(8,128)(2,1)S(1)} async-done(((bf16[4,384,384]{2,1,0:T(8,128)(2,1)}), bf16[4,384,384]{2,1,0:T(8,128)(2,1)S(1)}, u32[]{:S(2)}, u32[]{:S(2)}) %all-to-all-start) | async-done | bytes 1179680 | tf_op jit(solution)/shard_map/all_to_all | solution.py:266
  93.0 0.1 slice.66
  93.1 5.1 %collective-permute-start = (bf16[8,16,384]{2,1,0:T(8,128)(2,1)S(1)}, bf16[8,16,384]{2,1,0:T(8,128)(2,1)S(1)}, u32[]{:S(2)}, u32[]{:S(2)}) collective-permute-start(bf16[8,16,384]{2,1,0:T(8,128)(2,1)S(1)} %get-tuple-element.11), channel_id=1, source_target_pairs={{0,64},{64,128},{128,192},{1,65},{65,129},{129,193},{2,66},{66,130... | collective-permute-start | bytes 294920 | tf_op jit(solution)/shard_map/ppermute | solution.py:268
  98.3 1.3 collective-permute-start.1
  99.6 0.3 collective-permute-done
  99.9 3.7 %collective-permute-done.1 = bf16[8,16,384]{2,1,0:T(8,128)(2,1)S(1)} collective-permute-done((bf16[8,16,384]{2,1,0:T(8,128)(2,1)S(1)}, bf16[8,16,384]{2,1,0:T(8,128)(2,1)S(1)}, u32[]{:S(2)}, u32[]{:S(2)}) %collective-permute-start.1) | collective-permute-done | bytes 98336 | tf_op jit(solution)/shard_map/ppermute | solution.py:269
  103.6 0.1 pad_maximum_fusion.1
  103.8 0.1 select_bitcast_fusion
  103.9 6.0 %collective-permute-start.3 = (bf16[640,384]{1,0:T(8,128)(2,1)S(1)}, bf16[640,384]{1,0:T(8,128)(2,1)}, u32[]{:S(2)}, u32[]{:S(2)}) collective-permute-start(bf16[640,384]{1,0:T(8,128)(2,1)S(1)} %get-tuple-element.9), channel_id=1, source_target_pairs={{1,2},{3,4},{2,1},{5,6},{4,3},{7,8},{6,5},{9,10},{8,7},{11,12},{10... | collective-permute-start | bytes 1474568 | tf_op jit(solution)/shard_map/ppermute | solution.py:273
  109.9 0.1 collective-permute-start.2
  110.0 0.6 pad_add_fusion.place_ref
  110.6 0.1 copy.7
  110.7 0.1 copy.6
  110.8 0.6 gather_fusion.1
  111.4 0.6 gather_fusion
  112.0 0.6 compare_select_fusion.2.idx_two_ref
  112.6 0.6 fusion.4.idx_one_ref
  113.2 0.8 slice.71.q_ref
  113.9 2.6 %collective-permute-done.3.outer_ref = bf16[640,384]{1,0:T(8,128)(2,1)} collective-permute-done((bf16[640,384]{1,0:T(8,128)(2,1)S(1)}, bf16[640,384]{1,0:T(8,128)(2,1)}, u32[]{:S(2)}, u32[]{:S(2)}) %collective-permute-start.3) | collective-permute-done | bytes 491552 | tf_op jit(solution)/shard_map/ppermute | solution.py:273
  116.5 32.3 %shard_map.56 = bf16[4,128,384]{2,1,0:T(8,128)(2,1)} custom-call(s32[3]{0:T(128)} %pad_add_fusion.place_ref, s32[4,27]{1,0:T(4,128)} %fusion.4.idx_one_ref, s32[2,27]{1,0:T(2,128)} %compare_select_fusion.2.idx_two_ref, bf16[1280,384]{1,0:T(8,128)(2,1)} %bitcast.40, bf16[640,384]{1,0:T(8,128)(2,1)} %collective-permute-done.2.inner_ref, ...), custom_call_target="tpu_custom_call" | custom-call | flops 10569646080 | bytes 10485760 | tf_op jit(solution)/shard_map/pallas_call | solution.py:328
  148.9 12.8 %all_to_all.15.o_ref = bf16[4,128,384]{2,1,0:T(8,128)(2,1)} all-to-all(bf16[4,128,384]{2,1,0:T(8,128)(2,1)} %shard_map.56), channel_id=1, replica_groups=mesh['y'=4,'x'=4,'z'=8,'core'=2] {'x'}, dimensions={0} | all-to-all | bytes 786432 | tf_op jit(solution)/shard_map/all_to_all | solution.py:345
  161.6 1.8 %shard_map.57 = bf16[256,768]{1,0:T(8,128)(2,1)} custom-call(bf16[4,128,384]{2,1,0:T(8,128)(2,1)} %all_to_all.15.o_ref), custom_call_target="tpu_custom_call" | custom-call | bytes 1048576 | tf_op jit(solution)/shard_map/pallas_call | solution.py:346
  (33 shorter events, 0.3 us)
Async XLA Ops:
  9.3 14.1 %all-to-all-start.1 = ((bf16[8,80,384]{2,1,0:T(8,128)(2,1)}), bf16[8,80,384]{2,1,0:T(8,128)(2,1)S(1)}, u32[]{:S(2)}, u32[]{:S(2)}) async-start(bf16[8,80,384]{2,1,0:T(8,128)(2,1)} %bitcast.54), calls=%async_computation.1 | async-start | bytes 983040 | tf_op jit(solution)/shard_map/all_to_all | solution.py:258
  14.3 102.2 %all-gather.5.cloned.1.call-start = ((), (), s32[]{:S(2)}) async-start(), calls=%async_computation.3 | async-start | bytes 2064384 | tf_op jit(solution)/shard_map/all_gather | solution.py:311
  23.4 29.6 %copy-start.1 = (bf16[8,80,384]{2,1,0:T(8,128)(2,1)}, bf16[8,80,384]{2,1,0:T(8,128)(2,1)S(1)}, u32[]{:S(2)}) copy-start(bf16[8,80,384]{2,1,0:T(8,128)(2,1)S(1)} %all-to-all-done.1) | copy-start | bytes 1474564
  23.4 14.1 %collective-permute-start.6 = (bf16[4,2,16,384]{3,2,1,0:T(8,128)(2,1)S(1)}, bf16[4,2,16,384]{3,2,1,0:T(8,128)(2,1)S(1)}, u32[]{:S(2)}, u32[]{:S(2)}) collective-permute-start(bf16[4,2,16,384]{3,2,1,0:T(8,128)(2,1)S(1)} %slice.72), channel_id=1, source_target_pairs={{1,6},{3,8},{5,10},{7,12},{6,1},{9,14},{8,3},{10,5},{12,7},{14,9},... | collective-permute-start | bytes 294920 | tf_op jit(solution)/shard_map/ppermute | solution.py:264
  30.8 9.2 %collective-permute-start.5 = (bf16[4,2,16,384]{3,2,1,0:T(8,128)(2,1)S(1)}, bf16[4,2,16,384]{3,2,1,0:T(8,128)(2,1)S(1)}, u32[]{:S(2)}, u32[]{:S(2)}) collective-permute-start(bf16[4,2,16,384]{3,2,1,0:T(8,128)(2,1)S(1)} %slice.72), channel_id=1, source_target_pairs={{1,4},{3,6},{5,8},{4,1},{7,10},{6,3},{9,12},{8,5},{11,14},{10,7},{... | collective-permute-start | bytes 294920 | tf_op jit(solution)/shard_map/ppermute | solution.py:263
  32.7 11.4 %collective-permute-start.4 = (bf16[4,2,80,384]{3,2,1,0:T(8,128)(2,1)S(1)}, bf16[4,2,80,384]{3,2,1,0:T(8,128)(2,1)S(1)}, u32[]{:S(2)}, u32[]{:S(2)}) collective-permute-start(bf16[4,2,80,384]{3,2,1,0:T(8,128)(2,1)S(1)} %bitcast.43), channel_id=1, source_target_pairs={{1,2},{3,4},{2,1},{5,6},{4,3},{7,8},{6,5},{9,10},{8,7},{11,12},{10... | collective-permute-start | bytes 1474568 | tf_op jit(solution)/shard_map/ppermute | solution.py:261
  36.8 8.2 %copy-start.2 = (bf16[4,80,384]{2,1,0:T(8,128)(2,1)}, bf16[4,80,384]{2,1,0:T(8,128)(2,1)S(1)}, u32[]{:S(2)}) copy-start(bf16[4,80,384]{2,1,0:T(8,128)(2,1)S(1)} %dynamic-slice_bitcast_fusion) | copy-start | bytes 737284
  45.0 71.5 %all-gather.7.cloned.1.call-start = ((), (), s32[]{:S(2)}) async-start(), calls=%async_computation.4 | async-start | bytes 4349952 | tf_op jit(solution)/shard_map/all_gather | solution.py:317
  45.1 0.8 slice-start
  48.5 23.0 %collective-permute-start.7 = (bf16[832,384]{1,0:T(8,128)(2,1)}, bf16[832,384]{1,0:T(8,128)(2,1)S(1)}, u32[]{:S(2)}, u32[]{:S(2)}) collective-permute-start(bf16[832,384]{1,0:T(8,128)(2,1)} %get-tuple-element.17), channel_id=1, source_target_pairs={{0,64},{64,128},{128,192},{1,65},{65,129},{129,193},{2,66},{66,130... | collective-permute-start | bytes 1916936 | tf_op jit(solution)/shard_map/ppermute | solution.py:290
  51.8 19.8 %collective-permute-start.8 = (bf16[832,384]{1,0:T(8,128)(2,1)S(1)}, bf16[832,384]{1,0:T(8,128)(2,1)S(1)}, u32[]{:S(2)}, u32[]{:S(2)}) collective-permute-start(bf16[832,384]{1,0:T(8,128)(2,1)S(1)} %get-tuple-element.18), channel_id=1, source_target_pairs={{64,0},{128,64},{192,128},{65,1},{129,65},{193,129},{66,2},{130,66... | collective-permute-start | bytes 1916936 | tf_op jit(solution)/shard_map/ppermute | solution.py:291
  53.2 18.3 %collective-permute-start.9 = (bf16[224,384]{1,0:T(8,128)(2,1)S(1)}, bf16[224,384]{1,0:T(8,128)(2,1)S(1)}, u32[]{:S(2)}, u32[]{:S(2)}) collective-permute-start(bf16[224,384]{1,0:T(8,128)(2,1)S(1)} %pad_maximum_fusion.3), channel_id=1, source_target_pairs={{0,128},{64,192},{128,0},{192,64},{1,129},{65,193},{129,1},{193,65... | collective-permute-start | bytes 516104 | tf_op jit(solution)/shard_map/ppermute | solution.py:297
  72.9 20.1 %all-to-all-start = ((bf16[4,384,384]{2,1,0:T(8,128)(2,1)}), bf16[4,384,384]{2,1,0:T(8,128)(2,1)S(1)}, u32[]{:S(2)}, u32[]{:S(2)}) async-start(bf16[4,384,384]{2,1,0:T(8,128)(2,1)} %get-tuple-element.7), calls=%async_computation | async-start | bytes 2359296 | tf_op jit(solution)/shard_map/all_to_all | solution.py:266
  93.1 6.7 %collective-permute-start = (bf16[8,16,384]{2,1,0:T(8,128)(2,1)S(1)}, bf16[8,16,384]{2,1,0:T(8,128)(2,1)S(1)}, u32[]{:S(2)}, u32[]{:S(2)}) collective-permute-start(bf16[8,16,384]{2,1,0:T(8,128)(2,1)S(1)} %get-tuple-element.11), channel_id=1, source_target_pairs={{0,64},{64,128},{128,192},{1,65},{65,129},{129,193},{2,66},{66,130... | collective-permute-start | bytes 294920 | tf_op jit(solution)/shard_map/ppermute | solution.py:268
  98.3 5.4 %collective-permute-start.1 = (bf16[8,16,384]{2,1,0:T(8,128)(2,1)S(1)}, bf16[8,16,384]{2,1,0:T(8,128)(2,1)S(1)}, u32[]{:S(2)}, u32[]{:S(2)}) collective-permute-start(bf16[8,16,384]{2,1,0:T(8,128)(2,1)S(1)} %get-tuple-element.12), channel_id=1, source_target_pairs={{64,0},{128,64},{192,128},{65,1},{129,65},{193,129},{66,2},{130,66... | collective-permute-start | bytes 294920 | tf_op jit(solution)/shard_map/ppermute | solution.py:269
  103.8 10.2 %copy-start = (bf16[80,16,384]{2,1,0:T(8,128)(2,1)}, bf16[80,16,384]{2,1,0:T(8,128)(2,1)S(1)}, u32[]{:S(2)}) copy-start(bf16[80,16,384]{2,1,0:T(8,128)(2,1)S(1)} %pad_maximum_fusion.1) | copy-start | bytes 2949124
  103.8 6.8 %copy-start.4 = (s32[64,27]{0,1:T(8,128)S(1)}, s32[64,27]{0,1:T(8,128)}, u32[]{:S(2)}) copy-start(s32[64,27]{0,1:T(8,128)} %param.9) | copy-start | bytes 20740
  103.8 6.9 %copy-start.3 = (s32[256,27]{0,1:T(8,128)S(1)}, s32[256,27]{0,1:T(8,128)}, u32[]{:S(2)}) copy-start(s32[256,27]{0,1:T(8,128)} %param.8) | copy-start | bytes 82948
  103.9 12.6 %collective-permute-start.3 = (bf16[640,384]{1,0:T(8,128)(2,1)S(1)}, bf16[640,384]{1,0:T(8,128)(2,1)}, u32[]{:S(2)}, u32[]{:S(2)}) collective-permute-start(bf16[640,384]{1,0:T(8,128)(2,1)S(1)} %get-tuple-element.9), channel_id=1, source_target_pairs={{1,2},{3,4},{2,1},{5,6},{4,3},{7,8},{6,5},{9,10},{8,7},{11,12},{10... | collective-permute-start | bytes 1474568 | tf_op jit(solution)/shard_map/ppermute | solution.py:273
  109.9 6.6 %collective-permute-start.2 = (bf16[640,384]{1,0:T(8,128)(2,1)S(1)}, bf16[640,384]{1,0:T(8,128)(2,1)}, u32[]{:S(2)}, u32[]{:S(2)}) collective-permute-start(bf16[640,384]{1,0:T(8,128)(2,1)S(1)} %get-tuple-element.10), channel_id=1, source_target_pairs={{0,1},{1,0},{2,3},{3,2},{4,5},{5,4},{6,7},{7,6},{8,9},{9,8},{10,11... | collective-permute-start | bytes 1474568 | tf_op jit(solution)/shard_map/ppermute | solution.py:272
Sparse Core Ops, SparseCore 0:
  45.2 14.7 all-gather.4
  73.0 17.0 all-gather.6

commit v2 on v1

v2 whole, which is shorter than its diff:
```python
import math

import jax
import jax.numpy as jnp
import numpy as np
from jax import lax
from jax.experimental import pallas as pl
from jax.experimental.pallas import tpu as pltpu
from jax.sharding import Mesh, PartitionSpec as P

BF = jnp.bfloat16
F32 = jnp.float32
NEG = -1e30
VMEM = pl.BlockSpec(memory_space=pltpu.VMEM)
SMEM = pl.BlockSpec(memory_space=pltpu.SMEM)


def split_bias(level):
    full = 2.0 * level * math.log(2.0)
    high = float(np.float32(full).astype(BF))
    return high, float(np.float32(full - high).astype(BF))


def iota(shape, dim):
    return lax.broadcasted_iota(jnp.int32, shape, dim)


FINE, QUERY, ONE, TWO, PACKED = 0, 256, 384, 448, 464


def prep_kernel(q_ref, k_ref, v_ref, out_ref):
    row = iota((80, 256), 0)
    tok = iota((80, 256), 1)
    trow, tcol = tok >> 4, tok & 15
    one = (row < 64) & ((trow >> 1) == (row >> 3)) & ((tcol >> 1) == (row & 7))
    rest = row - 64
    two = (row >= 64) & ((trow >> 2) == (rest >> 2)) & ((tcol >> 2) == (rest & 3))
    pool = jnp.where(one, 0.25, jnp.where(two, 0.0625, 0.0)).astype(BF)
    k = k_ref[...]
    v = v_ref[...]
    kc = jnp.dot(pool, k, preferred_element_type=F32).astype(BF)
    vc = jnp.dot(pool, v, preferred_element_type=F32).astype(BF)
    q = (q_ref[...].astype(F32) * 0.125).astype(BF)
    for j in range(4):
        pair = slice(128 * j, 128 * j + 128)
        third = slice(512 + 64 * j, 576 + 64 * j)
        out_ref[j, FINE:QUERY, 0:128] = k[:, pair]
        out_ref[j, FINE:QUERY, 128:256] = v[:, pair]
        out_ref[j, FINE:QUERY, 256:384] = jnp.concatenate([k[:, third], v[:, third]], axis=1)
        out_ref[j, QUERY:ONE, 0:128] = q[0:128, pair]
        out_ref[j, QUERY:ONE, 128:256] = q[128:256, pair]
        out_ref[j, QUERY:ONE, 256:384] = jnp.concatenate(
            [q[0:128, third], q[128:256, third]], axis=1
        )
        out_ref[j, ONE:PACKED, 0:128] = kc[:, pair]
        out_ref[j, ONE:PACKED, 128:256] = vc[:, pair]
        out_ref[j, ONE:PACKED, 256:384] = jnp.concatenate([kc[:, third], vc[:, third]], axis=1)


def unpack_kernel(o_ref, out_ref):
    for j in range(4):
        pair = slice(128 * j, 128 * j + 128)
        out_ref[0:128, pair] = o_ref[j, :, 0:128]
        out_ref[128:256, pair] = o_ref[j, :, 128:256]
    lane = iota((128, 128), 1)
    for j in (0, 2):
        first = o_ref[j, :, 256:384]
        second = o_ref[j + 1, :, 256:384]
        lanes = slice(512 + 64 * j, 640 + 64 * j)
        out_ref[0:128, lanes] = jnp.concatenate([first[:, :64], second[:, :64]], axis=1)
        out_ref[128:256, lanes] = jnp.concatenate([first[:, 64:], second[:, 64:]], axis=1)


NEAR = 1024
FAR = 27 * 64
KEYS = NEAR + 2 * FAR


CHUNKS = [(at, min(512, KEYS - at)) for at in range(0, KEYS, 512)]


def attend_kernel(
    place_ref, idx_one_ref, idx_two_ref,
    own_ref, other_ref, up_ref, down_ref, inner_ref, side_ref, other_side_ref,
    row_ref, up_two_ref, down_two_ref, across_ref,
    other_row_ref, other_up_ref, other_down_ref, other_across_ref,
    out_ref, one_ref, two_ref, tall_ref, kv_ref, s_ref,
):
    y = place_ref[0]
    z = place_ref[1]
    core = place_ref[2]

    tall_ref[0:128] = up_ref[256:384]
    tall_ref[1152:1280] = down_ref[256:384]
    for xs in range(4):
        tall_ref[128 + 256 * xs:384 + 256 * xs] = own_ref[xs, FINE:QUERY]

    def quarter(xs, kk):
        return pl.ds(pl.multiple_of(32 * (xs & 1) + 16 * kk, 16), 16)

    def put_one(row, col, block):
        one_ref[row * 6 + col] = block

    for m in range(2):
        kk = core if m == 0 else 1 - core
        mine = own_ref if m == 0 else other_ref
        base = ONE if m == 0 else 0
        for xs in range(4):
            put_one(2 + xs, 2 + kk, mine[xs, base:base + 64])
        for i in range(2):
            at = 128 * m + 64 * i
            put_one(i, 2 + kk, up_ref[at:at + 64])
            put_one(6 + i, 2 + kk, down_ref[at:at + 64])
    for side, one_side in ((core, side_ref), (1 - core, other_side_ref)):
        for m in range(2):
            kk = 1 - side if m == 0 else side
            for i in range(4):
                at = 256 * m + 64 * i
                put_one(2 + i, 4 * side + kk, one_side[at:at + 64])
            for i in range(2):
                at = 512 + 128 * m + 64 * i
                put_one(i, 4 * side + kk, one_side[at:at + 64])
                put_one(6 + i, 4 * side + kk, one_side[at + 256:at + 320])
    end = jnp.where(y >= 2, 2 * y - 1, 2 * y + 6)
    for kk, row, ups, downs, across in (
        (core, row_ref, up_two_ref, down_two_ref, across_ref),
        (1 - core, other_row_ref, other_up_ref, other_down_ref, other_across_ref),
    ):
        for col in range(8):
            for xs in range(4):
                at = 64 * col + 16 * xs
                brow = 2 * y + 2 + xs // 2
                two_ref[brow * 8 + col, quarter(xs, kk)] = row[at:at + 16]
                two_ref[(brow - 2) * 8 + col, quarter(xs, kk)] = ups[at:at + 16]
                two_ref[(brow + 2) * 8 + col, quarter(xs, kk)] = downs[at:at + 16]
            for i in range(2):
                at = 32 * col + 16 * i
                two_ref[end * 8 + col, quarter(i, kk)] = across[at:at + 16]

    lane64 = iota((64, 128), 1)
    high_one, low_one = split_bias(1)
    high_two, low_two = split_bias(2)
    tok = iota((256, 128), 0)
    lane = iota((256, 128), 1)
    block = ((tok >> 7) << 1) + ((tok >> 3) & 1)
    q_feat = jnp.where((lane == block) | (lane == 4) | (lane == 5), 1.0, 0.0).astype(BF)

    def near_features(rows_wide, wide_log, col_base, tile):
        count = rows_wide << wide_log
        key = iota((count, 128), 0)
        ln = iota((count, 128), 1)
        wr = key >> wide_log
        wc = (key & ((1 << wide_log) - 1)) + col_base
        br, bc = ln >> 1, ln & 1
        row = 64 * y + 16 * tile - 8 + wr
        col = 32 * z + 16 * core - 8 + wc
        ok = (wr >= 8 * br) & (wr < 8 * br + 24) & (wc >= 8 * bc) & (wc < 8 * bc + 24)
        ok = ok & (row >= 0) & (row < 256) & (col >= 0) & (col < 256)
        return jnp.where(
            (ln < 4) & jnp.logical_not(ok), NEG, jnp.where(ln == 6, 1.0, 0.0)
        ).astype(BF)

    def place_rows(at, size, packed, features):
        kv_ref[pl.ds(at, size), 0:128] = packed[:, 0:128]
        kv_ref[pl.ds(at, size), 128:256] = features
        kv_ref[pl.ds(at, size), 256:384] = packed[:, 256:384]
        kv_ref[pl.ds(at, size), 384:512] = packed[:, 128:256]

    def one_tile(tile, carry):
        at = pl.multiple_of(tile * 256, 256)
        place_rows(0, 512, tall_ref[pl.ds(at, 512)], near_features(32, 4, 8, tile))
        at = pl.multiple_of(tile * 128, 128)
        inner_col = 24 - 24 * core
        place_rows(512, 256, inner_ref[pl.ds(at, 256)], near_features(32, 3, inner_col, tile))
        place_rows(768, 256, side_ref[pl.ds(pl.multiple_of(1024 + tile * 128, 128), 256)], near_features(32, 3, 24 - inner_col, tile))

        def far_block(j, c):
            for level, (idx_ref, win_ref, trow, high, low) in enumerate((
                (idx_one_ref, one_ref, tile, high_one, low_one),
                (idx_two_ref, two_ref, tile // 2, high_two, low_two),
            )):
                index = idx_ref[trow, j]
                top = jnp.where(index >= 0, jnp.float32(high), jnp.float32(NEG))
                feat = jnp.where(
                    lane64 == 4, top, jnp.where(lane64 == 5, low, jnp.where(lane64 == 6, 1.0, 0.0))
                )
                start = pl.multiple_of(NEAR + level * FAR + j * 64, 64)
                place_rows(start, 64, win_ref[jnp.where(index >= 0, index, -1 - index)], feat.astype(BF))
            return c

        lax.fori_loop(0, 27, far_block, 0)

        q_pair = jnp.concatenate([own_ref[tile, QUERY:ONE, 0:128], own_ref[tile, QUERY:ONE, 128:256]], axis=0)
        q_last = own_ref[tile, QUERY:ONE, 256:384]
        q_third = jnp.concatenate([q_last, jnp.concatenate([q_last[:, 64:], q_last[:, :64]], axis=1)], axis=0)
        zero = jnp.zeros_like(q_pair)
        low_half = lane < 64
        lhs = [
            jnp.concatenate([jnp.where(low_half, q_pair, zero), q_feat], axis=1),
            jnp.concatenate([jnp.where(low_half, zero, q_pair), q_feat], axis=1),
            jnp.concatenate([q_feat, jnp.where(low_half, q_third, zero)], axis=1),
        ]

        def scores(head, at, size, top):
            lanes = slice(128, 384) if head == 2 else slice(0, 256)
            s = lax.dot_general(
                lhs[head], kv_ref[at:at + size, lanes], (((1,), (1,)), ((), ())),
                preferred_element_type=F32,
            )
            s_ref[head % 2, :, at:at + size] = s
            for c in range(0, size, 128):
                part = s[:, c:c + 128]
                top = part if top is None else jnp.maximum(top, part)
            return top

        def values(head, at, size, peak, acc):
            w = jnp.exp(s_ref[head % 2, :, at:at + size] - peak).astype(BF)
            if head == 2:
                rhs = kv_ref[at:at + size, 128:384]
            else:
                rhs = jnp.concatenate(
                    [kv_ref[at:at + size, 128:256], kv_ref[at:at + size, 384:512]], axis=1
                )
            part = jnp.dot(w, rhs, preferred_element_type=F32)
            return part if acc is None else acc + part

        top = None
        for at, size in CHUNKS:
            top = scores(0, at, size, top)
        outs = []
        for head in range(3):
            peak = jnp.max(top, axis=1, keepdims=True)
            top = acc = None
            for at, size in CHUNKS:
                if head < 2:
                    top = scores(head + 1, at, size, top)
                acc = values(head, at, size, peak, acc)
            outs.append(acc[:, 128:256] / acc[:, 6:7])
        pair_out = jnp.where(low_half, outs[0], outs[1])
        third_out = outs[2]
        out_ref[tile, :, 0:128] = pair_out[0:128].astype(BF)
        out_ref[tile, :, 128:256] = pair_out[128:256].astype(BF)
        out_ref[tile, :, 256:384] = jnp.concatenate(
            [third_out[0:128, 64:], third_out[128:256, 64:]], axis=1
        ).astype(BF)
        return carry

    lax.fori_loop(0, 4, one_tile, 0)


def call(kernel, out_shape, in_specs, scratch=(), flops=0, nbytes=0):
    return pl.pallas_call(
        kernel,
        out_shape=out_shape,
        in_specs=in_specs,
        out_specs=jax.tree.map(lambda _: VMEM, out_shape),
        scratch_shapes=scratch,
        compiler_params=pltpu.CompilerParams(vmem_limit_bytes=56 * 2**20),
        cost_estimate=pl.CostEstimate(flops=flops, bytes_accessed=nbytes, transcendentals=0),
    )


def shape(*dims):
    return jax.ShapeDtypeStruct(dims, BF)


def z_perm(step):
    pairs = []
    for z in range(8):
        if z + step < 8:
            pairs.append((2 * z + 1, 2 * (z + step)))
        if z - step >= 0:
            pairs.append((2 * z, 2 * (z - step) + 1))
    return pairs


def body(queries, keys, values, list_one, list_two):
    y = lax.axis_index("y")
    x = lax.axis_index("x")
    z = lax.axis_index("z")
    core = lax.axis_index("core")
    up = [(i, i + 1) for i in range(3)]
    down = [(i + 1, i) for i in range(3)]
    across = [(i, i ^ 2) for i in range(4)]

    entries = lax.dynamic_slice(list_one.reshape(16, 16, 27), (4 * y, 2 * z + core, 0), (4, 1, 27))[:, 0]
    where = (entries // 16 - (4 * y - 2)) * 6 + entries % 16 - (2 * z - 2)
    self_one = (2 + jnp.arange(4, dtype=jnp.int32)[:, None]) * 6 + 2 + core
    idx_one = jnp.where(entries >= 0, where, -1 - self_one)
    entries = lax.dynamic_slice(list_two.reshape(8, 8, 27), (2 * y, z, 0), (2, 1, 27))[:, 0]
    self_two = (2 * y + 2 + jnp.arange(2, dtype=jnp.int32)[:, None]) * 8 + z
    idx_two = jnp.where(entries >= 0, entries + 16, -1 - self_two)
    place = jnp.stack([y, z, core]).astype(jnp.int32)

    packed = call(prep_kernel, shape(4, PACKED, 384), [VMEM] * 3, nbytes=4 << 20)(
        queries.reshape(256, 768), keys.reshape(256, 768), values.reshape(256, 768)
    )
    rf = lax.all_to_all(packed, "x", 0, 0, tiled=True)
    rf, idx_one, idx_two, place = lax.optimization_barrier((rf, idx_one, idx_two, place))

    def over_core(array):
        return lax.ppermute(array, "core", [(0, 1), (1, 0)])

    def over_z(array, step=1):
        return lax.ppermute(array, ("z", "core"), z_perm(step))

    def strips(tokens):
        rows = tokens.shape[0] // 16
        tokens = tokens.reshape(rows, 16, 384)
        left, right = tokens[:, 0:8], tokens[:, 8:16]
        inner = jnp.where(core == 0, right, left).reshape(rows * 8, 384)
        outer = jnp.where(core == 0, left, right).reshape(rows * 8, 384)
        return inner, outer

    fine = rf[:, FINE:QUERY].reshape(1024, 384)
    other = over_core(rf[:, ONE:TWO].reshape(256, 384)).reshape(4, 64, 384)
    ones = (rf[:, ONE:TWO], other)
    two = rf[:, TWO:PACKED].reshape(1, 64, 384)
    row_two = lax.all_to_all(jnp.broadcast_to(two, (8, 64, 384)), "z", 0, 0, tiled=True)
    from_up = lax.ppermute(
        jnp.concatenate([t[2:4].reshape(128, 384) for t in ones] + [fine[896:1024]], axis=0), "y", up
    )
    from_down = lax.ppermute(
        jnp.concatenate([t[0:2].reshape(128, 384) for t in ones] + [fine[0:128]], axis=0), "y", down
    )
    row_two, from_up, from_down = lax.optimization_barrier((row_two, from_up, from_down))

    top_inner, top_outer = strips(from_up[256:384])
    middle_inner, middle_outer = strips(fine)
    bottom_inner, bottom_outer = strips(from_down[256:384])
    side = over_z(
        jnp.concatenate(
            [t.reshape(256, 384) for t in ones]
            + [from_up[0:256], from_down[0:256], top_outer, middle_outer, bottom_outer],
            axis=0,
        )
    )
    inner = over_core(jnp.concatenate([top_inner, middle_inner, bottom_inner], axis=0))
    up_two = lax.ppermute(row_two.reshape(512, 384), "y", up)
    down_two = lax.ppermute(row_two.reshape(512, 384), "y", down)
    half = jnp.where(y < 2, 1, 0)
    across_two = lax.ppermute(
        lax.dynamic_index_in_dim(row_two.reshape(8, 2, 32, 384), half, 1, keepdims=False).reshape(256, 384),
        "y",
        across,
    )
    other_row = over_core(row_two.reshape(512, 384))
    side, up_two, down_two, across_two, inner, other_row = lax.optimization_barrier(
        (side, up_two, down_two, across_two, inner, other_row)
    )

    other_side = over_core(side[0:1024])
    others = [over_core(t) for t in (up_two, down_two, across_two)]

    out = call(
        attend_kernel,
        shape(4, 128, 384),
        [SMEM] * 3 + [VMEM] * 15,
        scratch=[
            pltpu.VMEM((48, 64, 384), BF),
            pltpu.VMEM((96, 64, 384), BF),
            pltpu.VMEM((1280, 384), BF),
            pltpu.VMEM((KEYS, 512), BF),
            pltpu.VMEM((2, 256, KEYS), F32),
        ],
        flops=12 * 256 * KEYS * 768,
        nbytes=10 << 20,
    )(
        place, idx_one, idx_two, rf, other, from_up, from_down, inner, side, other_side,
        row_two.reshape(512, 384), up_two, down_two, across_two, other_row, *others,
    )
    back = lax.all_to_all(out, "x", 0, 0, tiled=True)
    tile = call(unpack_kernel, shape(256, 768), [VMEM], nbytes=1 << 20)(back)
    return tile.reshape(16, 16, 768)


def solution(mesh):
    fine_mesh = Mesh(mesh.devices.reshape(4, 4, 8, 2), ("y", "x", "z", "core"))
    spec = P(("y", "x"), ("z", "core"), None)
    return jax.shard_map(
        body, mesh=fine_mesh, in_specs=(spec, spec, spec, P(), P()), out_specs=spec, check_vma=False
    )
```

time: 171 us -> 125 us (0.73)
  the two profiles are of different devices: /device:TPU:65 before, /device:TPU:48 now
where the time goes in v2:
time: 125 us; the launch traced here: 122 us
  waiting for transfers between devices  36.7 us (29%)
  Pallas kernels  32.5 us (26%)
  starting transfers between devices  29.8 us (24%)
  blocking collectives  12.8 us (10%)
  local copies, waits for them, and re-layouts  5.7 us (5%)
  other arithmetic  4.22 us (3%)
    pallas_call x1, Pallas kernels, body(): call(attend_kernel, shape(4, 128, 384), [SMEM] * 3 + [VMEM] * 15, scratch...  28 us
    all_to_all x1, waiting for transfers between devices, body(): rf = lax.all_to_all(packed, 'x', 0, 0, tiled=True)  16.8 us
    all_to_all x1, blocking collectives, body(): back = lax.all_to_all(out, 'x', 0, 0, tiled=True)  12.8 us
    all_to_all x1, starting transfers between devices, body(): lax.all_to_all(jnp.broadcast_to(two, (8, 64, 384)), 'z', 0, 0, tiled=True)  8.57 us
    ppermute x1, waiting for transfers between devices, body(): up_two = lax.ppermute(row_two.reshape(512, 384), 'y', up)  7.9 us
    all_to_all x1, starting transfers between devices, body(): rf = lax.all_to_all(packed, 'x', 0, 0, tiled=True)  4.42 us
    unnamed x39, local copies, waits for them, and re-layouts  4.12 us
    ppermute x1, starting transfers between devices, body(): up_two = lax.ppermute(row_two.reshape(512, 384), 'y', up)  4.09 us
  transfers between devices with their start and end apart: 15, of which 8 were waited for; matrix products, arithmetic and copies ran while one was open for 4% of the time, Pallas kernels for 0%

profile of v2, /device:TPU:48, one launch (start us, length us, event | category | flops | bytes accessed | tf_op | source)
XLA Modules:
  0.0 122.1 jit_solution(14189449545317940653)
XLA Ops:
  0.0 2.7 %shard_map.55 = bf16[4,464,384]{2,1,0:T(8,128)(2,1)} custom-call(bf16[256,768]{1,0:T(8,128)(2,1)} %bitcast.71, bf16[256,768]{1,0:T(8,128)(2,1)} %bitcast.72, bf16[256,768]{1,0:T(8,128)(2,1)} %bitcast.73), custom_call_target="tpu_custom_call" | custom-call | bytes 4194304 | tf_op jit(solution)/shard_map/pallas_call | solution.py:295
  2.8 4.4 %all-to-all-start = ((bf16[4,464,384]{2,1,0:T(8,128)(2,1)}), bf16[4,464,384]{2,1,0:T(8,128)(2,1)S(1)}, u32[]{:S(2)}, u32[]{:S(2)}) async-start(bf16[4,464,384]{2,1,0:T(8,128)(2,1)} %shard_map.55), calls=%async_computation | async-start | bytes 2850816 | tf_op jit(solution)/shard_map/all_to_all | solution.py:298
  7.2 0.1 copy.11
  7.3 0.1 reshape.110
  7.4 0.1 constant_dynamic-slice_fusion.2
  7.5 0.1 copy.10
  7.6 0.6 pad_add_fusion.place_ref
  8.2 0.6 bitcast_select_fusion.idx_two_ref
  8.9 0.7 fusion.4.idx_one_ref
  9.5 16.8 %all-to-all-done.own_ref = bf16[4,464,384]{2,1,0:T(8,128)(2,1)S(1)} async-done(((bf16[4,464,384]{2,1,0:T(8,128)(2,1)}), bf16[4,464,384]{2,1,0:T(8,128)(2,1)S(1)}, u32[]{:S(2)}, u32[]{:S(2)}) %all-to-all-start) | async-done | bytes 1425440 | tf_op jit(solution)/shard_map/all_to_all | solution.py:298
  26.3 0.1 slice.69
  26.5 0.1 collective-permute-start
  26.6 1.0 broadcast_in_dim.28
  27.5 8.6 %all-to-all-start.1 = ((bf16[8,64,384]{2,1,0:T(8,128)(2,1)}), bf16[8,64,384]{2,1,0:T(8,128)(2,1)S(1)}, u32[]{:S(2)}, u32[]{:S(2)}) async-start(bf16[8,64,384]{2,1,0:T(8,128)(2,1)} %broadcast_in_dim.28), calls=%async_computation.1 | async-start | bytes 786432 | tf_op jit(solution)/shard_map/all_to_all | solution.py:319
  36.2 2.4 %collective-permute-start.2 = (bf16[384,384]{1,0:T(8,128)(2,1)S(1)}, bf16[384,384]{1,0:T(8,128)(2,1)S(1)}, u32[]{:S(2)}, u32[]{:S(2)}) collective-permute-start(bf16[384,384]{1,0:T(8,128)(2,1)S(1)} %pad_maximum_fusion.2), channel_id=1, source_target_pairs={{64,0},{128,64},{192,128},{65,1},{129,65},{193,129},{66,2},{130,66... | collective-permute-start | bytes 884744 | tf_op jit(solution)/shard_map/ppermute | solution.py:323
  38.6 3.5 %collective-permute-start.1 = (bf16[384,384]{1,0:T(8,128)(2,1)S(1)}, bf16[384,384]{1,0:T(8,128)(2,1)S(1)}, u32[]{:S(2)}, u32[]{:S(2)}) collective-permute-start(bf16[384,384]{1,0:T(8,128)(2,1)S(1)} %pad_maximum_fusion.1), channel_id=1, source_target_pairs={{0,64},{64,128},{128,192},{1,65},{65,129},{129,193},{2,66},{66,130... | collective-permute-start | bytes 884744 | tf_op jit(solution)/shard_map/ppermute | solution.py:320
  42.1 0.7 constant_dynamic-update-slice_fusion.1
  42.8 0.7 constant_dynamic-update-slice_fusion
  43.5 3.2 %collective-permute-done.2.down_ref = bf16[384,384]{1,0:T(8,128)(2,1)S(1)} collective-permute-done((bf16[384,384]{1,0:T(8,128)(2,1)S(1)}, bf16[384,384]{1,0:T(8,128)(2,1)S(1)}, u32[]{:S(2)}, u32[]{:S(2)}) %collective-permute-start.2) | collective-permute-done | bytes 294944 | tf_op jit(solution)/shard_map/ppermute | solution.py:323
  46.8 2.1 %collective-permute-done.1.up_ref = bf16[384,384]{1,0:T(8,128)(2,1)S(1)} collective-permute-done((bf16[384,384]{1,0:T(8,128)(2,1)S(1)}, bf16[384,384]{1,0:T(8,128)(2,1)S(1)}, u32[]{:S(2)}, u32[]{:S(2)}) %collective-permute-start.1) | collective-permute-done | bytes 294944 | tf_op jit(solution)/shard_map/ppermute | solution.py:320
  48.9 0.9 all-to-all-done.1
  49.9 0.8 slice_dynamic-update-slice_fusion.1
  50.6 0.7 slice_dynamic-update-slice_fusion
  51.3 0.6 bitcast_dynamic-update-slice_fusion.2
  52.0 0.9 bitcast_dynamic-update-slice_fusion
  52.8 0.6 bitcast_dynamic-update-slice_fusion.1
  53.4 3.0 %collective-permute-start.3 = (bf16[1664,384]{1,0:T(8,128)(2,1)}, bf16[1664,384]{1,0:T(8,128)(2,1)S(1)}, u32[]{:S(2)}, u32[]{:S(2)}) collective-permute-start(bf16[1664,384]{1,0:T(8,128)(2,1)} %bitcast_dynamic-update-slice_fusion.1), channel_id=1, source_target_pairs={{1,2},{3,4},{2,1},{5,6},{4,3},{7,8},{6,5},{9,10},{8,7},{11,12},{10... | collective-permute-start | bytes 3833864 | tf_op jit(solution)/shard_map/ppermute | solution.py:305
  56.6 0.4 collective-permute-start.6
  57.0 0.1 pad_maximum_fusion
  57.1 0.1 collective-permute-start.7
  57.2 4.1 %collective-permute-start.4 = (bf16[512,384]{1,0:T(8,128)(2,1)S(1)}, bf16[512,384]{1,0:T(8,128)(2,1)S(1)}, u32[]{:S(2)}, u32[]{:S(2)}) collective-permute-start(bf16[512,384]{1,0:T(8,128)(2,1)S(1)} %bitcast.60), channel_id=1, source_target_pairs={{0,64},{64,128},{128,192},{1,65},{65,129},{129,193},{2,66},{66,130... | collective-permute-start | bytes 1179656 | tf_op jit(solution)/shard_map/ppermute | solution.py:339
  61.3 2.1 %collective-permute-start.5 = (bf16[512,384]{1,0:T(8,128)(2,1)S(1)}, bf16[512,384]{1,0:T(8,128)(2,1)S(1)}, u32[]{:S(2)}, u32[]{:S(2)}) collective-permute-start(bf16[512,384]{1,0:T(8,128)(2,1)S(1)} %bitcast.61), channel_id=1, source_target_pairs={{64,0},{128,64},{192,128},{65,1},{129,65},{193,129},{66,2},{130,66... | collective-permute-start | bytes 1179656 | tf_op jit(solution)/shard_map/ppermute | solution.py:340
  63.4 1.7 %collective-permute-done.6.across_ref = bf16[256,384]{1,0:T(8,128)(2,1)S(1)} collective-permute-done((bf16[256,384]{1,0:T(8,128)(2,1)S(1)}, bf16[256,384]{1,0:T(8,128)(2,1)S(1)}, u32[]{:S(2)}, u32[]{:S(2)}) %collective-permute-start.6) | collective-permute-done | bytes 196640 | tf_op jit(solution)/shard_map/ppermute | solution.py:342
  65.1 7.9 %collective-permute-done.4.up_two_ref = bf16[512,384]{1,0:T(8,128)(2,1)S(1)} collective-permute-done((bf16[512,384]{1,0:T(8,128)(2,1)S(1)}, bf16[512,384]{1,0:T(8,128)(2,1)S(1)}, u32[]{:S(2)}, u32[]{:S(2)}) %collective-permute-start.4) | collective-permute-done | bytes 393248 | tf_op jit(solution)/shard_map/ppermute | solution.py:339
  73.0 1.4 %collective-permute-done.5.down_two_ref = bf16[512,384]{1,0:T(8,128)(2,1)S(1)} collective-permute-done((bf16[512,384]{1,0:T(8,128)(2,1)S(1)}, bf16[512,384]{1,0:T(8,128)(2,1)S(1)}, u32[]{:S(2)}, u32[]{:S(2)}) %collective-permute-start.5) | collective-permute-done | bytes 393248 | tf_op jit(solution)/shard_map/ppermute | solution.py:340
  74.4 0.1 slice.84
  74.5 0.1 collective-permute-start.9
  74.6 0.5 collective-permute-start.10
  75.1 0.1 collective-permute-start.11
  75.2 0.4 collective-permute-start.12
  75.6 2.7 %collective-permute-done.12.other_across_ref = bf16[256,384]{1,0:T(8,128)(2,1)S(1)} collective-permute-done((bf16[256,384]{1,0:T(8,128)(2,1)S(1)}, bf16[256,384]{1,0:T(8,128)(2,1)S(1)}, u32[]{:S(2)}, u32[]{:S(2)}) %collective-permute-start.12) | collective-permute-done | bytes 196640 | tf_op jit(solution)/shard_map/ppermute | solution.py:302
  78.4 0.6 copy-done.16
  79.0 0.1 copy-done.13
  79.1 0.1 copy-done.14
  79.2 0.3 copy-done.8
  79.5 28.0 %shard_map.56 = bf16[4,128,384]{2,1,0:T(8,128)(2,1)} custom-call(s32[3]{0:T(128)} %pad_add_fusion.place_ref, s32[4,27]{1,0:T(4,128)} %fusion.4.idx_one_ref, s32[2,27]{1,0:T(2,128)} %bitcast_select_fusion.idx_two_ref, bf16[4,464,384]{2,1,0:T(8,128)(2,1)} %copy-done, bf16[4,64,384]{2,1,0:T(8,128)(2,1)} %bitcast.68, bf16[384,384]{1,0:T(8,128)(2,1)} %copy-done.5, ...), custom_call_target="tpu_custom_call" | custom-call | flops 10569646080 | bytes 10485760 | tf_op jit(solution)/shard_map/pallas_call | solution.py:355
  107.4 12.8 %all_to_all.15.o_ref = bf16[4,128,384]{2,1,0:T(8,128)(2,1)} all-to-all(bf16[4,128,384]{2,1,0:T(8,128)(2,1)} %shard_map.56), channel_id=1, replica_groups=mesh['y'=4,'x'=4,'z'=8,'core'=2] {'x'}, dimensions={0} | all-to-all | bytes 786432 | tf_op jit(solution)/shard_map/all_to_all | solution.py:372
  120.3 1.8 %shard_map.57 = bf16[256,768]{1,0:T(8,128)(2,1)} custom-call(bf16[4,128,384]{2,1,0:T(8,128)(2,1)} %all_to_all.15.o_ref), custom_call_target="tpu_custom_call" | custom-call | bytes 1048576 | tf_op jit(solution)/shard_map/pallas_call | solution.py:373
  (54 shorter events, 0.4 us)
Async XLA Ops:
  2.7 4.4 %copy-start.7 = (s32[64,27]{0,1:T(8,128)S(1)}, s32[64,27]{0,1:T(8,128)}, u32[]{:S(2)}) copy-start(s32[64,27]{0,1:T(8,128)} %param.9) | copy-start | bytes 20740
  2.7 4.5 %copy-start.6 = (s32[256,27]{0,1:T(8,128)S(1)}, s32[256,27]{0,1:T(8,128)}, u32[]{:S(2)}) copy-start(s32[256,27]{0,1:T(8,128)} %param.8) | copy-start | bytes 82948
  2.8 23.6 %all-to-all-start = ((bf16[4,464,384]{2,1,0:T(8,128)(2,1)}), bf16[4,464,384]{2,1,0:T(8,128)(2,1)S(1)}, u32[]{:S(2)}, u32[]{:S(2)}) async-start(bf16[4,464,384]{2,1,0:T(8,128)(2,1)} %shard_map.55), calls=%async_computation | async-start | bytes 2850816 | tf_op jit(solution)/shard_map/all_to_all | solution.py:298
  26.3 1.2 copy-start
  26.5 9.7 %collective-permute-start = (bf16[256,384]{1,0:T(8,128)(2,1)S(1)}, bf16[256,384]{1,0:T(8,128)(2,1)S(1)}, u32[]{:S(2)}, u32[]{:S(2)}) collective-permute-start(bf16[256,384]{1,0:T(8,128)(2,1)S(1)} %bitcast.69), channel_id=1, source_target_pairs={{0,1},{1,0},{2,3},{3,2},{4,5},{5,4},{6,7},{7,6},{8,9},{9,8},{10,11... | collective-permute-start | bytes 589832 | tf_op jit(solution)/shard_map/ppermute | solution.py:302
  27.5 22.3 %all-to-all-start.1 = ((bf16[8,64,384]{2,1,0:T(8,128)(2,1)}), bf16[8,64,384]{2,1,0:T(8,128)(2,1)S(1)}, u32[]{:S(2)}, u32[]{:S(2)}) async-start(bf16[8,64,384]{2,1,0:T(8,128)(2,1)} %broadcast_in_dim.28), calls=%async_computation.1 | async-start | bytes 786432 | tf_op jit(solution)/shard_map/all_to_all | solution.py:319
  36.1 13.7 %copy-start.2 = (bf16[256,384]{1,0:T(8,128)(2,1)}, bf16[256,384]{1,0:T(8,128)(2,1)S(1)}, u32[]{:S(2)}) copy-start(bf16[256,384]{1,0:T(8,128)(2,1)S(1)} %collective-permute-done) | copy-start | bytes 589828
  36.2 10.6 %collective-permute-start.2 = (bf16[384,384]{1,0:T(8,128)(2,1)S(1)}, bf16[384,384]{1,0:T(8,128)(2,1)S(1)}, u32[]{:S(2)}, u32[]{:S(2)}) collective-permute-start(bf16[384,384]{1,0:T(8,128)(2,1)S(1)} %pad_maximum_fusion.2), channel_id=1, source_target_pairs={{64,0},{128,64},{192,128},{65,1},{129,65},{193,129},{66,2},{130,66... | collective-permute-start | bytes 884744 | tf_op jit(solution)/shard_map/ppermute | solution.py:323
  38.6 10.3 %collective-permute-start.1 = (bf16[384,384]{1,0:T(8,128)(2,1)S(1)}, bf16[384,384]{1,0:T(8,128)(2,1)S(1)}, u32[]{:S(2)}, u32[]{:S(2)}) collective-permute-start(bf16[384,384]{1,0:T(8,128)(2,1)S(1)} %pad_maximum_fusion.1), channel_id=1, source_target_pairs={{0,64},{64,128},{128,192},{1,65},{65,129},{129,193},{2,66},{66,130... | collective-permute-start | bytes 884744 | tf_op jit(solution)/shard_map/ppermute | solution.py:320
  46.8 6.7 %copy-start.4 = (bf16[384,384]{1,0:T(8,128)(2,1)}, bf16[384,384]{1,0:T(8,128)(2,1)S(1)}, u32[]{:S(2)}) copy-start(bf16[384,384]{1,0:T(8,128)(2,1)S(1)} %collective-permute-done.2.down_ref) | copy-start | bytes 884740
  48.9 4.5 %copy-start.5 = (bf16[384,384]{1,0:T(8,128)(2,1)}, bf16[384,384]{1,0:T(8,128)(2,1)S(1)}, u32[]{:S(2)}) copy-start(bf16[384,384]{1,0:T(8,128)(2,1)S(1)} %collective-permute-done.1.up_ref) | copy-start | bytes 884740
  49.8 15.3 %copy-start.1 = (bf16[8,64,384]{2,1,0:T(8,128)(2,1)}, bf16[8,64,384]{2,1,0:T(8,128)(2,1)S(1)}, u32[]{:S(2)}) copy-start(bf16[8,64,384]{2,1,0:T(8,128)(2,1)S(1)} %all-to-all-done.1) | copy-start | bytes 1179652
  53.4 20.9 %collective-permute-start.3 = (bf16[1664,384]{1,0:T(8,128)(2,1)}, bf16[1664,384]{1,0:T(8,128)(2,1)S(1)}, u32[]{:S(2)}, u32[]{:S(2)}) collective-permute-start(bf16[1664,384]{1,0:T(8,128)(2,1)} %bitcast_dynamic-update-slice_fusion.1), channel_id=1, source_target_pairs={{1,2},{3,4},{2,1},{5,6},{4,3},{7,8},{6,5},{9,10},{8,7},{11,12},{10... | collective-permute-start | bytes 3833864 | tf_op jit(solution)/shard_map/ppermute | solution.py:305
  56.6 8.5 %collective-permute-start.6 = (bf16[256,384]{1,0:T(8,128)(2,1)S(1)}, bf16[256,384]{1,0:T(8,128)(2,1)S(1)}, u32[]{:S(2)}, u32[]{:S(2)}) collective-permute-start(bf16[256,384]{1,0:T(8,128)(2,1)S(1)} %bitcast.77), channel_id=1, source_target_pairs={{0,128},{64,192},{128,0},{192,64},{1,129},{65,193},{129,1},{193,65... | collective-permute-start | bytes 589832 | tf_op jit(solution)/shard_map/ppermute | solution.py:342
  57.1 17.3 %collective-permute-start.7 = (bf16[640,384]{1,0:T(8,128)(2,1)S(1)}, bf16[640,384]{1,0:T(8,128)(2,1)S(1)}, u32[]{:S(2)}, u32[]{:S(2)}) collective-permute-start(bf16[640,384]{1,0:T(8,128)(2,1)S(1)} %pad_maximum_fusion), channel_id=1, source_target_pairs={{0,1},{1,0},{2,3},{3,2},{4,5},{5,4},{6,7},{7,6},{8,9},{9,8},{10,11... | collective-permute-start | bytes 1474568 | tf_op jit(solution)/shard_map/ppermute | solution.py:302
  57.2 15.8 %collective-permute-start.4 = (bf16[512,384]{1,0:T(8,128)(2,1)S(1)}, bf16[512,384]{1,0:T(8,128)(2,1)S(1)}, u32[]{:S(2)}, u32[]{:S(2)}) collective-permute-start(bf16[512,384]{1,0:T(8,128)(2,1)S(1)} %bitcast.60), channel_id=1, source_target_pairs={{0,64},{64,128},{128,192},{1,65},{65,129},{129,193},{2,66},{66,130... | collective-permute-start | bytes 1179656 | tf_op jit(solution)/shard_map/ppermute | solution.py:339
  61.3 13.1 %collective-permute-start.5 = (bf16[512,384]{1,0:T(8,128)(2,1)S(1)}, bf16[512,384]{1,0:T(8,128)(2,1)S(1)}, u32[]{:S(2)}, u32[]{:S(2)}) collective-permute-start(bf16[512,384]{1,0:T(8,128)(2,1)S(1)} %bitcast.61), channel_id=1, source_target_pairs={{64,0},{128,64},{192,128},{65,1},{129,65},{193,129},{66,2},{130,66... | collective-permute-start | bytes 1179656 | tf_op jit(solution)/shard_map/ppermute | solution.py:340
  65.1 13.3 %copy-start.15 = (bf16[256,384]{1,0:T(8,128)(2,1)}, bf16[256,384]{1,0:T(8,128)(2,1)S(1)}, u32[]{:S(2)}) copy-start(bf16[256,384]{1,0:T(8,128)(2,1)S(1)} %collective-permute-done.6.across_ref) | copy-start | bytes 589828
  65.1 9.3 %collective-permute-start.8 = (bf16[512,384]{1,0:T(8,128)(2,1)S(1)}, bf16[512,384]{1,0:T(8,128)(2,1)S(1)}, u32[]{:S(2)}, u32[]{:S(2)}) collective-permute-start(bf16[512,384]{1,0:T(8,128)(2,1)S(1)} %bitcast.62), channel_id=1, source_target_pairs={{0,1},{1,0},{2,3},{3,2},{4,5},{5,4},{6,7},{7,6},{8,9},{9,8},{10,11... | collective-permute-start | bytes 1179656 | tf_op jit(solution)/shard_map/ppermute | solution.py:302
  73.0 5.4 %copy-start.10 = (bf16[512,384]{1,0:T(8,128)(2,1)}, bf16[512,384]{1,0:T(8,128)(2,1)S(1)}, u32[]{:S(2)}) copy-start(bf16[512,384]{1,0:T(8,128)(2,1)S(1)} %collective-permute-done.4.up_two_ref) | copy-start | bytes 1179652
  74.4 4.0 %copy-start.11 = (bf16[512,384]{1,0:T(8,128)(2,1)}, bf16[512,384]{1,0:T(8,128)(2,1)S(1)}, u32[]{:S(2)}) copy-start(bf16[512,384]{1,0:T(8,128)(2,1)S(1)} %collective-permute-done.5.down_two_ref) | copy-start | bytes 1179652
  74.4 4.0 %copy-start.12 = (bf16[512,384]{1,0:T(8,128)(2,1)}, bf16[512,384]{1,0:T(8,128)(2,1)S(1)}, u32[]{:S(2)}) copy-start(bf16[512,384]{1,0:T(8,128)(2,1)S(1)} %collective-permute-done.8.other_row_ref) | copy-start | bytes 1179652
  74.4 4.0 %copy-start.9 = (bf16[640,384]{1,0:T(8,128)(2,1)}, bf16[640,384]{1,0:T(8,128)(2,1)S(1)}, u32[]{:S(2)}) copy-start(bf16[640,384]{1,0:T(8,128)(2,1)S(1)} %collective-permute-done.7.inner_ref) | copy-start | bytes 1474564
  74.4 4.0 %copy-start.3 = (bf16[1664,384]{1,0:T(8,128)(2,1)}, bf16[1664,384]{1,0:T(8,128)(2,1)S(1)}, u32[]{:S(2)}) copy-start(bf16[1664,384]{1,0:T(8,128)(2,1)S(1)} %collective-permute-done.3.side_ref) | copy-start | bytes 3833860
  74.5 3.8 %collective-permute-start.9 = (bf16[1024,384]{1,0:T(8,128)(2,1)S(1)}, bf16[1024,384]{1,0:T(8,128)(2,1)S(1)}, u32[]{:S(2)}, u32[]{:S(2)}) collective-permute-start(bf16[1024,384]{1,0:T(8,128)(2,1)S(1)} %slice.84), channel_id=1, source_target_pairs={{0,1},{1,0},{2,3},{3,2},{4,5},{5,4},{6,7},{7,6},{8,9},{9,8},{10,11... | collective-permute-start | bytes 2359304 | tf_op jit(solution)/shard_map/ppermute | solution.py:302
  74.6 3.7 %collective-permute-start.10 = (bf16[512,384]{1,0:T(8,128)(2,1)S(1)}, bf16[512,384]{1,0:T(8,128)(2,1)S(1)}, u32[]{:S(2)}, u32[]{:S(2)}) collective-permute-start(bf16[512,384]{1,0:T(8,128)(2,1)S(1)} %collective-permute-done.4.up_two_ref), channel_id=1, source_target_pairs={{0,1},{1,0},{2,3},{3,2},{4,5},{5,4},{6,7},{7,6},{8,9},{9,8},{10,11... | collective-permute-start | bytes 1179656 | tf_op jit(solution)/shard_map/ppermute | solution.py:302
  75.1 3.2 %collective-permute-start.11 = (bf16[512,384]{1,0:T(8,128)(2,1)S(1)}, bf16[512,384]{1,0:T(8,128)(2,1)S(1)}, u32[]{:S(2)}, u32[]{:S(2)}) collective-permute-start(bf16[512,384]{1,0:T(8,128)(2,1)S(1)} %collective-permute-done.5.down_two_ref), channel_id=1, source_target_pairs={{0,1},{1,0},{2,3},{3,2},{4,5},{5,4},{6,7},{7,6},{8,9},{9,8},{10,11... | collective-permute-start | bytes 1179656 | tf_op jit(solution)/shard_map/ppermute | solution.py:302
  75.2 3.1 %collective-permute-start.12 = (bf16[256,384]{1,0:T(8,128)(2,1)S(1)}, bf16[256,384]{1,0:T(8,128)(2,1)S(1)}, u32[]{:S(2)}, u32[]{:S(2)}) collective-permute-start(bf16[256,384]{1,0:T(8,128)(2,1)S(1)} %collective-permute-done.6.across_ref), channel_id=1, source_target_pairs={{0,1},{1,0},{2,3},{3,2},{4,5},{5,4},{6,7},{7,6},{8,9},{9,8},{10,11... | collective-permute-start | bytes 589832 | tf_op jit(solution)/shard_map/ppermute | solution.py:302
  78.3 0.7 copy-start.16
  78.3 0.8 copy-start.13
  78.3 0.9 copy-start.14
  78.3 1.2 copy-start.8

commit v3 on v2

v3 whole, which is shorter than its diff:
```python
import math

import jax
import jax.numpy as jnp
import numpy as np
from jax import lax
from jax.experimental import pallas as pl
from jax.experimental.pallas import tpu as pltpu
from jax.sharding import Mesh, PartitionSpec as P

BF = jnp.bfloat16
F32 = jnp.float32
NEG = -1e30
VMEM = pl.BlockSpec(memory_space=pltpu.VMEM)
SMEM = pl.BlockSpec(memory_space=pltpu.SMEM)


def split_bias(level):
    full = 2.0 * level * math.log(2.0)
    high = float(np.float32(full).astype(BF))
    return high, float(np.float32(full - high).astype(BF))


def iota(shape, dim):
    return lax.broadcasted_iota(jnp.int32, shape, dim)


FINE, QUERY, ONE, PACKED = 0, 256, 384, 448


def prep_kernel(q_ref, k_ref, v_ref, two_ref, out_ref):
    row = iota((80, 256), 0)
    tok = iota((80, 256), 1)
    trow, tcol = tok >> 4, tok & 15
    one = (row < 64) & ((trow >> 1) == (row >> 3)) & ((tcol >> 1) == (row & 7))
    rest = row - 64
    two = (row >= 64) & ((trow >> 2) == (rest >> 2)) & ((tcol >> 2) == (rest & 3))
    pool = jnp.where(one, 0.25, jnp.where(two, 0.0625, 0.0)).astype(BF)
    k = k_ref[...]
    v = v_ref[...]
    kc = jnp.dot(pool, k, preferred_element_type=F32).astype(BF)
    vc = jnp.dot(pool, v, preferred_element_type=F32).astype(BF)
    q = (q_ref[...].astype(F32) * 0.125).astype(BF)
    for j in range(4):
        pair = slice(128 * j, 128 * j + 128)
        third = slice(512 + 64 * j, 576 + 64 * j)
        out_ref[j, FINE:QUERY, 0:128] = k[:, pair]
        out_ref[j, FINE:QUERY, 128:256] = v[:, pair]
        out_ref[j, FINE:QUERY, 256:384] = jnp.concatenate([k[:, third], v[:, third]], axis=1)
        out_ref[j, QUERY:ONE, 0:128] = q[0:128, pair]
        out_ref[j, QUERY:ONE, 128:256] = q[128:256, pair]
        out_ref[j, QUERY:ONE, 256:384] = jnp.concatenate(
            [q[0:128, third], q[128:256, third]], axis=1
        )
        both = jnp.concatenate([kc[:, third], vc[:, third]], axis=1)
        for lanes, part in ((0, kc[:, pair]), (128, vc[:, pair]), (256, both)):
            out_ref[j, ONE:PACKED, lanes:lanes + 128] = part[0:64]
            for core in range(2):
                two_ref[j, core, :, lanes:lanes + 128] = part[64:80]


def unpack_kernel(o_ref, out_ref):
    for j in range(4):
        pair = slice(128 * j, 128 * j + 128)
        out_ref[0:128, pair] = o_ref[j, :, 0:128]
        out_ref[128:256, pair] = o_ref[j, :, 128:256]
    lane = iota((128, 128), 1)
    for j in (0, 2):
        first = o_ref[j, :, 256:384]
        second = o_ref[j + 1, :, 256:384]
        lanes = slice(512 + 64 * j, 640 + 64 * j)
        out_ref[0:128, lanes] = jnp.concatenate([first[:, :64], second[:, :64]], axis=1)
        out_ref[128:256, lanes] = jnp.concatenate([first[:, 64:], second[:, 64:]], axis=1)


NEAR = 1024
FAR = 27 * 64
KEYS = NEAR + 2 * FAR


CHUNKS = [(at, min(512, KEYS - at)) for at in range(0, KEYS, 512)]


def attend_kernel(
    place_ref, idx_one_ref, idx_two_ref,
    own_ref, other_ref, up_ref, down_ref,
    inner_ref, corner_ref, outer_ref, side_ref, other_outer_ref, other_side_ref, own_two_ref,
    z_one_ref, z_two_ref, z_three_ref, up_two_ref, down_two_ref, across_ref,
    oz_one_ref, oz_two_ref, oz_three_ref, other_up_ref, other_down_ref, other_across_ref,
    out_ref, one_ref, two_ref, tall_ref, in_ref, out_strip_ref, kv_ref, kv_next_ref, s_pair_ref, s_third_ref,
):
    y = place_ref[0]
    z = place_ref[1]
    core = place_ref[2]

    tall_ref[0:128] = up_ref[256:384]
    tall_ref[1152:1280] = down_ref[256:384]
    for xs in range(4):
        tall_ref[128 + 256 * xs:384 + 256 * xs] = own_ref[xs, FINE:QUERY]
    for strip_ref, middle_ref, ends_ref, at in (
        (in_ref, inner_ref, corner_ref, 0), (out_strip_ref, outer_ref, side_ref, 512),
    ):
        strip_ref[0:64] = ends_ref[at:at + 64]
        strip_ref[64:576] = middle_ref[at:at + 512]
        strip_ref[576:640] = ends_ref[at + 64:at + 128]

    def quarter(xs, kk):
        return pl.ds(pl.multiple_of(32 * (xs & 1) + 16 * kk, 16), 16)

    def put_one(row, col, block):
        one_ref[row * 6 + col] = block

    def put_two(brow, bcol, xs, kk, block):
        two_ref[brow * 7 + bcol, quarter(xs, kk)] = block

    for m in range(2):
        kk = core if m == 0 else 1 - core
        mine = own_ref if m == 0 else other_ref
        base = ONE if m == 0 else 0
        for xs in range(4):
            put_one(2 + xs, 2 + kk, mine[xs, base:base + 64])
        for i in range(2):
            at = 128 * m + 64 * i
            put_one(i, 2 + kk, up_ref[at:at + 64])
            put_one(6 + i, 2 + kk, down_ref[at:at + 64])
    for side, middle, ends in ((core, outer_ref, side_ref), (1 - core, other_outer_ref, other_side_ref)):
        for m in range(2):
            kk = 1 - side if m == 0 else side
            for i in range(4):
                at = 256 * m + 64 * i
                put_one(2 + i, 4 * side + kk, middle[at:at + 64])
            for i in range(2):
                at = 128 * m + 64 * i
                put_one(i, 4 * side + kk, ends[at:at + 64])
                put_one(6 + i, 4 * side + kk, ends[at + 256:at + 320])
    for xs in range(4):
        for kk in range(2):
            put_two(3 + xs // 2, 3, xs, kk, own_two_ref[xs, kk])
    end = jnp.where(y >= 2, 0, 7)
    for side, twos, ups, across in (
        (core, (z_one_ref, z_two_ref, z_three_ref), (up_two_ref, down_two_ref), across_ref),
        (
            1 - core, (oz_one_ref, oz_two_ref, oz_three_ref),
            (other_up_ref, other_down_ref), other_across_ref,
        ),
    ):
        step = 2 * side - 1
        for xs in range(4):
            put_two(1 + xs // 2, 3, xs, side, ups[0][16 * xs:16 * xs + 16])
            put_two(5 + xs // 2, 3, xs, side, ups[1][16 * xs:16 * xs + 16])
        for i in range(2):
            put_two(end, 3, i, side, across[16 * i:16 * i + 16])
        for far in (1, 2, 3):
            col = 3 + far * step
            for kk in range(2):
                for xs in range(4):
                    at = 32 * xs + 16 * kk
                    put_two(3 + xs // 2, col, xs, kk, twos[far - 1][at:at + 16])
                    at = 128 * far - 64 + at
                    put_two(1 + xs // 2, col, xs, kk, ups[0][at:at + 16])
                    put_two(5 + xs // 2, col, xs, kk, ups[1][at:at + 16])
                for i in range(2):
                    at = 64 * far - 32 + 32 * i + 16 * kk
                    put_two(end, col, i, kk, across[at:at + 16])

    lane64 = iota((64, 128), 1)
    high_one, low_one = split_bias(1)
    high_two, low_two = split_bias(2)
    tok = iota((256, 128), 0)
    lane = iota((256, 128), 1)
    block = ((tok >> 7) << 1) + ((tok >> 3) & 1)
    q_feat = jnp.where((lane == block) | (lane == 4) | (lane == 5), 1.0, 0.0).astype(BF)

    def near_features(rows_wide, wide_log, col_base, tile, first_row):
        count = rows_wide << wide_log
        key = iota((count, 128), 0)
        ln = iota((count, 128), 1)
        wr = (key >> wide_log) + first_row
        wc = (key & ((1 << wide_log) - 1)) + col_base
        br, bc = ln >> 1, ln & 1
        row = 64 * y + 16 * tile - 8 + wr
        col = 32 * z + 16 * core - 8 + wc
        ok = (wr >= 8 * br) & (wr < 8 * br + 24) & (wc >= 8 * bc) & (wc < 8 * bc + 24)
        ok = ok & (row >= 0) & (row < 256) & (col >= 0) & (col < 256)
        return jnp.where(
            (ln < 4) & jnp.logical_not(ok), NEG, jnp.where(ln == 6, 1.0, 0.0)
        ).astype(BF)

    def place_rows(kv_ref, at, size, packed, features):
        kv_ref[at:at + size, 0:128] = packed[:, 0:128]
        kv_ref[at:at + size, 128:256] = features
        kv_ref[at:at + size, 256:384] = packed[:, 256:384]
        kv_ref[at:at + size, 384:512] = packed[:, 128:256]

    inner_col = 24 - 24 * core

    def gather_steps(tile, kv_ref):
        def near(source, base, stride, first, size, at, wide_log, col_base):
            def step():
                start = pl.multiple_of(base + tile * stride + first, 128)
                features = near_features(size >> wide_log, wide_log, col_base, tile, first >> wide_log)
                place_rows(kv_ref, at + first, size, source[pl.ds(start, size)], features)

            return step

        def far(j, level):
            idx_ref, win_ref, high, low = (
                (idx_one_ref, one_ref, high_one, low_one),
                (idx_two_ref, two_ref, high_two, low_two),
            )[level]

            def step():
                index = idx_ref[tile if level == 0 else tile // 2, j]
                top = jnp.where(index >= 0, jnp.float32(high), jnp.float32(NEG))
                feat = jnp.where(lane64 == 4, top, far_rest[level])
                block = win_ref[jnp.where(index >= 0, index, -1 - index)]
                place_rows(kv_ref, NEAR + level * FAR + j * 64, 64, block, feat.astype(BF))

            return step

        steps = [near(tall_ref, 0, 256, first, 128, 0, 4, 8) for first in range(0, 512, 128)]
        for first in (0, 128):
            steps.append(near(in_ref, 0, 128, first, 128, 512, 3, inner_col))
            steps.append(near(out_strip_ref, 0, 128, first, 128, 768, 3, 24 - inner_col))
        for j in range(27):
            steps += [far(j, 0), far(j, 1)]
        return steps

    low_half = lane < 64
    far_rest = [
        jnp.where(lane64 == 5, low, jnp.where(lane64 == 6, 1.0, 0.0)) for low in (low_one, low_two)
    ]

    def compute(tile, kv_ref, steps):
        steps = list(steps)
        slots = 3 * len(CHUNKS)
        share = -(-len(steps) // slots)

        def advance():
            for step in steps[:share]:
                step()
            del steps[:share]

        q_pair = jnp.concatenate([own_ref[tile, QUERY:ONE, 0:128], own_ref[tile, QUERY:ONE, 128:256]], axis=0)
        q_last = own_ref[tile, QUERY:ONE, 256:384]
        q_third = jnp.concatenate([q_last, jnp.concatenate([q_last[:, 64:], q_last[:, :64]], axis=1)], axis=0)
        zero = jnp.zeros_like(q_pair)
        lhs_pair = jnp.concatenate(
            [
                jnp.concatenate([jnp.where(low_half, q_pair, zero), q_feat], axis=1),
                jnp.concatenate([jnp.where(low_half, zero, q_pair), q_feat], axis=1),
            ],
            axis=0,
        )
        lhs_third = jnp.concatenate([q_feat, jnp.where(low_half, q_third, zero)], axis=1)

        def scores(lhs, lanes, s_ref, at, size, top):
            s = lax.dot_general(
                lhs, kv_ref[at:at + size, lanes], (((1,), (1,)), ((), ())), preferred_element_type=F32
            )
            s_ref[:, at:at + size] = s
            for c in range(0, size, 128):
                part = s[:, c:c + 128]
                top = part if top is None else jnp.maximum(top, part)
            return top

        def values(s_ref, at, size, peak, rhs, acc):
            w = jnp.exp(s_ref[:, at:at + size] - peak).astype(BF)
            part = jnp.dot(w, rhs, preferred_element_type=F32)
            return part if acc is None else acc + part

        top = None
        for at, size in CHUNKS:
            top = scores(lhs_pair, slice(0, 256), s_pair_ref, at, size, top)
            advance()
        peak = jnp.max(top, axis=1, keepdims=True)
        top = acc = None
        for at, size in CHUNKS:
            top = scores(lhs_third, slice(128, 384), s_third_ref, at, size, top)
            rhs = jnp.concatenate([kv_ref[at:at + size, 128:256], kv_ref[at:at + size, 384:512]], axis=1)
            acc = values(s_pair_ref, at, size, peak, rhs, acc)
            advance()
        out = acc[:, 128:256] / acc[:, 6:7]
        pair_out = jnp.where(low_half, out[0:256], out[256:512])
        peak = jnp.max(top, axis=1, keepdims=True)
        acc = None
        for at, size in CHUNKS:
            acc = values(s_third_ref, at, size, peak, kv_ref[at:at + size, 128:384], acc)
            advance()
        third_out = acc[:, 128:256] / acc[:, 6:7]
        out_ref[tile, :, 0:128] = pair_out[0:128].astype(BF)
        out_ref[tile, :, 128:256] = pair_out[128:256].astype(BF)
        out_ref[tile, :, 256:384] = jnp.concatenate(
            [third_out[0:128, 64:], third_out[128:256, 64:]], axis=1
        ).astype(BF)

    for step in gather_steps(0, kv_ref):
        step()

    def two_tiles(i, carry):
        compute(2 * i, kv_ref, gather_steps(2 * i + 1, kv_next_ref))
        compute(2 * i + 1, kv_next_ref, gather_steps(jnp.minimum(2 * i + 2, 3), kv_ref))
        return carry

    lax.fori_loop(0, 2, two_tiles, 0)


def call(kernel, out_shape, in_specs, scratch=(), flops=0, nbytes=0):
    return pl.pallas_call(
        kernel,
        out_shape=out_shape,
        in_specs=in_specs,
        out_specs=jax.tree.map(lambda _: VMEM, out_shape),
        scratch_shapes=scratch,
        compiler_params=pltpu.CompilerParams(vmem_limit_bytes=56 * 2**20),
        cost_estimate=pl.CostEstimate(flops=flops, bytes_accessed=nbytes, transcendentals=0),
    )


def shape(*dims):
    return jax.ShapeDtypeStruct(dims, BF)


def attend_call(*arrays):
    return call(
        attend_kernel,
        shape(4, 128, 384),
        [SMEM] * 3 + [VMEM] * 23,
        scratch=[
            pltpu.VMEM((48, 64, 384), BF),
            pltpu.VMEM((56, 64, 384), BF),
            pltpu.VMEM((1280, 384), BF),
            pltpu.VMEM((640, 384), BF),
            pltpu.VMEM((640, 384), BF),
            pltpu.VMEM((KEYS, 512), BF),
            pltpu.VMEM((KEYS, 512), BF),
            pltpu.VMEM((512, KEYS), F32),
            pltpu.VMEM((256, KEYS), F32),
        ],
        flops=12 * 256 * KEYS * 768,
        nbytes=10 << 20,
    )(*arrays)


def z_perm(step):
    pairs = []
    for z in range(8):
        if z + step < 8:
            pairs.append((2 * z + 1, 2 * (z + step)))
        if z - step >= 0:
            pairs.append((2 * z, 2 * (z - step) + 1))
    return pairs


def body(queries, keys, values, list_one, list_two):
    y = lax.axis_index("y")
    x = lax.axis_index("x")
    z = lax.axis_index("z")
    core = lax.axis_index("core")
    up = [(i, i + 1) for i in range(3)]
    down = [(i + 1, i) for i in range(3)]
    across = [(i, i ^ 2) for i in range(4)]

    entries = lax.dynamic_slice(list_one.reshape(16, 16, 27), (4 * y, 2 * z + core, 0), (4, 1, 27))[:, 0]
    where = (entries // 16 - (4 * y - 2)) * 6 + entries % 16 - (2 * z - 2)
    self_one = (2 + jnp.arange(4, dtype=jnp.int32)[:, None]) * 6 + 2 + core
    idx_one = jnp.where(entries >= 0, where, -1 - self_one)
    entries = lax.dynamic_slice(list_two.reshape(8, 8, 27), (2 * y, z, 0), (2, 1, 27))[:, 0]
    where = (entries // 8 - (2 * y - 3)) * 7 + entries % 8 - (z - 3)
    self_two = (3 + jnp.arange(2, dtype=jnp.int32)[:, None]) * 7 + 3
    idx_two = jnp.where(entries >= 0, where, -1 - self_two)
    place = jnp.stack([y, z, core]).astype(jnp.int32)

    own_two, packed = call(
        prep_kernel, [shape(4, 2, 16, 384), shape(4, PACKED, 384)], [VMEM] * 3, nbytes=4 << 20
    )(queries.reshape(256, 768), keys.reshape(256, 768), values.reshape(256, 768))

    def over_core(array):
        return lax.ppermute(array, "core", [(0, 1), (1, 0)])

    def over_z(array, step=1):
        return lax.ppermute(array, ("z", "core"), z_perm(step))

    def strips(tokens):
        rows = tokens.shape[0] // 16
        tokens = tokens.reshape(rows, 16, 384)
        left, right = tokens[:, 0:8], tokens[:, 8:16]
        inner = jnp.where(core == 0, right, left).reshape(rows * 8, 384)
        outer = jnp.where(core == 0, left, right).reshape(rows * 8, 384)
        return inner, outer

    own_two = lax.all_to_all(own_two.reshape(8, 16, 384), ("x", "core"), 0, 0, tiled=True)
    rf = lax.all_to_all(packed, "x", 0, 0, tiled=True)
    twos = own_two.reshape(128, 384)
    twos_z = [over_z(twos, step) for step in (1, 2, 3)]
    rf, idx_one, idx_two, place, *twos_z = lax.optimization_barrier(
        (rf, idx_one, idx_two, place, *twos_z)
    )

    fine = rf[:, FINE:QUERY].reshape(1024, 384)
    other = over_core(rf[:, ONE:PACKED].reshape(256, 384)).reshape(4, 64, 384)
    ones = (rf[:, ONE:PACKED], other)
    from_up = lax.ppermute(
        jnp.concatenate([t[2:4].reshape(128, 384) for t in ones] + [fine[896:1024]], axis=0), "y", up
    )
    from_down = lax.ppermute(
        jnp.concatenate([t[0:2].reshape(128, 384) for t in ones] + [fine[0:128]], axis=0), "y", down
    )
    inner_strip, outer_strip = strips(fine)
    outer = over_z(jnp.concatenate([t.reshape(256, 384) for t in ones] + [outer_strip], axis=0))
    own_two = own_two.reshape(4, 2, 16, 384)
    mine = lax.dynamic_index_in_dim(own_two, core, 1, keepdims=False).reshape(64, 384)
    near_two = jnp.concatenate([mine, *twos_z], axis=0)
    up_two = lax.ppermute(near_two, "y", up)
    down_two = lax.ppermute(near_two, "y", down)
    half = jnp.where(y < 2, 1, 0)
    halves = [lax.dynamic_index_in_dim(mine.reshape(2, 32, 384), half, 0, keepdims=False)]
    halves += [lax.dynamic_index_in_dim(t.reshape(2, 64, 384), half, 0, keepdims=False) for t in twos_z]
    across_two = lax.ppermute(jnp.concatenate(halves, axis=0), "y", across)
    inner = over_core(inner_strip)
    from_up, from_down, outer, inner, up_two, down_two, across_two = lax.optimization_barrier(
        (from_up, from_down, outer, inner, up_two, down_two, across_two)
    )

    top_inner, top_outer = strips(from_up[256:384])
    bottom_inner, bottom_outer = strips(from_down[256:384])
    side = over_z(
        jnp.concatenate([from_up[0:256], from_down[0:256], top_outer, bottom_outer], axis=0)
    )
    corner = over_core(jnp.concatenate([top_inner, bottom_inner], axis=0))
    twos_side = [*twos_z, up_two, down_two, across_two]
    others = [over_core(t) for t in twos_side]
    other_outer = over_core(outer[0:512])
    other_side = over_core(side[0:512])

    out = attend_call(
        place, idx_one, idx_two, rf, other, from_up, from_down,
        inner, corner, outer, side, other_outer, other_side, own_two, *twos_side, *others,
    )
    back = lax.all_to_all(out, "x", 0, 0, tiled=True)
    tile = call(unpack_kernel, shape(256, 768), [VMEM], nbytes=1 << 20)(back)
    return tile.reshape(16, 16, 768)


def solution(mesh):
    fine_mesh = Mesh(mesh.devices.reshape(4, 4, 8, 2), ("y", "x", "z", "core"))
    spec = P(("y", "x"), ("z", "core"), None)
    return jax.shard_map(
        body, mesh=fine_mesh, in_specs=(spec, spec, spec, P(), P()), out_specs=spec, check_vma=False
    )
```

time: 125 us -> 124 us (level); the launches traced: 122 us -> 124 us
  starting transfers between devices: 29.8 us -> 39.3 us
  local copies, waits for them, and re-layouts: 5.7 us -> 1.93 us
  Pallas kernels: 32.5 us -> 29.2 us
  other arithmetic: 4.22 us -> 2.3 us
    ppermute x3, waiting for transfers between devices: 10.9 us -> 2.01 us  [the longest x1 2 us: body(): across_two = lax.ppermute(jnp.concatenate(halves, axis=0), 'y', across)]
    ppermute x7 -> x11, starting transfers between devices: 1.29 us -> 10.1 us  [over_core(): return lax.ppermute(array, 'core', [(0, 1), (1, 0)])]
    ppermute x1 -> x5, waiting for transfers between devices: 0.01 us -> 7.38 us  [over_z(): return lax.ppermute(array, ('z', 'core'), z_perm(step))]
    all_to_all x1, waiting for transfers between devices: 16.8 us -> 10.6 us  [body(): rf = lax.all_to_all(packed, 'x', 0, 0, tiled=True)]
    all_to_all x1, waiting for transfers between devices: 0.9 us -> 5.56 us  [body(): lax.all_to_all(own_two.reshape(8, 16, 384), ('x', 'core'), 0, 0, tiled=True)]
    all_to_all x1, starting transfers between devices: 8.57 us -> 4.3 us  [body(): lax.all_to_all(own_two.reshape(8, 16, 384), ('x', 'core'), 0, 0, tiled=True)]
    ppermute x1 -> x5, starting transfers between devices: 2.99 us -> 7.08 us  [over_z(): return lax.ppermute(array, ('z', 'core'), z_perm(step))]
    ppermute x1, starting transfers between devices: 2.36 us -> 6.28 us  [body(): lax.ppermute(jnp.concatenate([t[0:2].reshape(128, 384) for t in ones] + [...]
  transfers between devices with their start and end apart: 15 -> 23, of which waited for: 8 -> 11; matrix products, arithmetic and copies ran while one was open for 4% -> 2% of each run, Pallas kernels for 0% -> 0%
where the time goes in v3:
time: 124 us
  starting transfers between devices  39.3 us (32%)
  waiting for transfers between devices  37.4 us (30%)
  Pallas kernels  29.2 us (24%)
  blocking collectives  13 us (10%)
  other arithmetic  2.3 us (2%)
  local copies, waits for them, and re-layouts  1.93 us (2%)
    pallas_call x1, Pallas kernels, attend_call(): call(attend_kernel, shape(4, 128, 384), [SMEM] * 3 + [VMEM] * 23, scratch...  24.6 us
    all_to_all x1, blocking collectives, body(): back = lax.all_to_all(out, 'x', 0, 0, tiled=True)  13 us
    all_to_all x1, waiting for transfers between devices, body(): rf = lax.all_to_all(packed, 'x', 0, 0, tiled=True)  10.6 us
    ppermute x11, starting transfers between devices, over_core(): return lax.ppermute(array, 'core', [(0, 1), (1, 0)])  10.1 us
    ppermute x5, waiting for transfers between devices, over_z(): return lax.ppermute(array, ('z', 'core'), z_perm(step))  7.38 us
    ppermute x5, starting transfers between devices, over_z(): return lax.ppermute(array, ('z', 'core'), z_perm(step))  7.08 us
    ppermute x1, starting transfers between devices, body(): lax.ppermute(jnp.concatenate([t[0:2].reshape(128, 384) for t in ones] + [...  6.28 us
    all_to_all x1, waiting for transfers between devices, body(): lax.all_to_all(own_two.reshape(8, 16, 384), ('x', 'core'), 0, 0, tiled=True)  5.56 us
  transfers between devices with their start and end apart: 23, of which 11 were waited for; matrix products, arithmetic and copies ran while one was open for 2% of the time, Pallas kernels for 0%

profile of v3, /device:TPU:48, one launch (start us, length us, event | category | flops | bytes accessed | tf_op | source)
XLA Modules:
  0.0 123.8 jit_solution(667888273189768462)
XLA Ops:
  0.0 2.8 %shard_map.55 = (bf16[4,2,16,384]{3,2,1,0:T(8,128)(2,1)}, bf16[4,448,384]{2,1,0:T(8,128)(2,1)}) custom-call(bf16[256,768]{1,0:T(8,128)(2,1)} %bitcast.75, bf16[256,768]{1,0:T(8,128)(2,1)} %bitcast.76, bf16[256,768]{1,0:T(8,128)(2,1)} %bitcast.77), custom_call_target="tpu_custom_call" | custom-call | bytes 4194304 | tf_op jit(solution)/shard_map/pallas_call | solution.py:374
  2.8 4.3 %all-to-all-start.1 = ((bf16[8,16,384]{2,1,0:T(8,128)(2,1)}), bf16[8,16,384]{2,1,0:T(8,128)(2,1)S(1)}, u32[]{:S(2)}, u32[]{:S(2)}) async-start(bf16[8,16,384]{2,1,0:T(8,128)(2,1)} %bitcast.88), calls=%async_computation.1 | async-start | bytes 196608 | tf_op jit(solution)/shard_map/all_to_all | solution.py:392
  7.1 0.1 reshape.114
  7.2 0.1 constant_dynamic-slice_fusion.2
  7.3 5.6 %all-to-all-done.1 = bf16[8,16,384]{2,1,0:T(8,128)(2,1)S(1)} async-done(((bf16[8,16,384]{2,1,0:T(8,128)(2,1)}), bf16[8,16,384]{2,1,0:T(8,128)(2,1)S(1)}, u32[]{:S(2)}, u32[]{:S(2)}) %all-to-all-start.1) | async-done | bytes 98336 | tf_op jit(solution)/shard_map/all_to_all | solution.py:392
  12.9 3.7 %all-to-all-start = ((bf16[4,448,384]{2,1,0:T(8,128)(2,1)}), bf16[4,448,384]{2,1,0:T(8,128)(2,1)S(1)}, u32[]{:S(2)}, u32[]{:S(2)}) async-start(bf16[4,448,384]{2,1,0:T(8,128)(2,1)} %get-tuple-element.21), calls=%async_computation | async-start | bytes 2752512 | tf_op jit(solution)/shard_map/all_to_all | solution.py:393
  16.6 0.1 copy.8
  16.8 0.6 pad_add_fusion.place_ref
  17.4 0.7 compare_select_fusion.idx_two_ref
  18.1 0.7 fusion.4.idx_one_ref
  18.7 1.9 %collective-permute-start = (bf16[128,384]{1,0:T(8,128)(2,1)S(1)}, bf16[128,384]{1,0:T(8,128)(2,1)S(1)}, u32[]{:S(2)}, u32[]{:S(2)}) collective-permute-start(bf16[128,384]{1,0:T(8,128)(2,1)S(1)} %bitcast.80), channel_id=1, source_target_pairs={{1,2},{3,4},{2,1},{5,6},{4,3},{7,8},{6,5},{9,10},{8,7},{11,12},{10... | collective-permute-start | bytes 294920 | tf_op jit(solution)/shard_map/ppermute | solution.py:382
  20.6 0.7 collective-permute-start.1
  21.3 0.7 collective-permute-start.2
  22.0 2.6 %collective-permute-done.z_one_ref = bf16[128,384]{1,0:T(8,128)(2,1)S(1)} collective-permute-done((bf16[128,384]{1,0:T(8,128)(2,1)S(1)}, bf16[128,384]{1,0:T(8,128)(2,1)S(1)}, u32[]{:S(2)}, u32[]{:S(2)}) %collective-permute-start) | collective-permute-done | bytes 98336 | tf_op jit(solution)/shard_map/ppermute | solution.py:382
  24.7 10.6 %all-to-all-done.own_ref = bf16[4,448,384]{2,1,0:T(8,128)(2,1)S(1)} async-done(((bf16[4,448,384]{2,1,0:T(8,128)(2,1)}), bf16[4,448,384]{2,1,0:T(8,128)(2,1)S(1)}, u32[]{:S(2)}, u32[]{:S(2)}) %all-to-all-start) | async-done | bytes 1376288 | tf_op jit(solution)/shard_map/all_to_all | solution.py:393
  35.3 3.2 %collective-permute-start.8 = (bf16[448,384]{1,0:T(8,128)(2,1)S(1)}, bf16[448,384]{1,0:T(8,128)(2,1)S(1)}, u32[]{:S(2)}, u32[]{:S(2)}) collective-permute-start(bf16[448,384]{1,0:T(8,128)(2,1)S(1)} %pad_maximum_fusion.2), channel_id=1, source_target_pairs={{0,64},{64,128},{128,192},{1,65},{65,129},{129,193},{2,66},{66,130... | collective-permute-start | bytes 1032200 | tf_op jit(solution)/shard_map/ppermute | solution.py:414
  38.5 2.7 %collective-permute-start.9 = (bf16[448,384]{1,0:T(8,128)(2,1)S(1)}, bf16[448,384]{1,0:T(8,128)(2,1)S(1)}, u32[]{:S(2)}, u32[]{:S(2)}) collective-permute-start(bf16[448,384]{1,0:T(8,128)(2,1)S(1)} %pad_maximum_fusion.2), channel_id=1, source_target_pairs={{64,0},{128,64},{192,128},{65,1},{129,65},{193,129},{66,2},{130,66... | collective-permute-start | bytes 1032200 | tf_op jit(solution)/shard_map/ppermute | solution.py:415
  41.4 0.1 collective-permute-start.10
  41.5 0.1 collective-permute-start.3
  41.7 1.3 %collective-permute-done.3 = bf16[256,384]{1,0:T(8,128)(2,1)S(1)} collective-permute-done((bf16[256,384]{1,0:T(8,128)(2,1)S(1)}, bf16[256,384]{1,0:T(8,128)(2,1)S(1)}, u32[]{:S(2)}, u32[]{:S(2)}) %collective-permute-start.3) | collective-permute-done | bytes 196640 | tf_op jit(solution)/shard_map/ppermute | solution.py:379
  43.1 1.9 %collective-permute-start.6 = (bf16[1024,384]{1,0:T(8,128)(2,1)S(1)}, bf16[1024,384]{1,0:T(8,128)(2,1)S(1)}, u32[]{:S(2)}, u32[]{:S(2)}) collective-permute-start(bf16[1024,384]{1,0:T(8,128)(2,1)S(1)} %pad_maximum_fusion), channel_id=1, source_target_pairs={{1,2},{3,4},{2,1},{5,6},{4,3},{7,8},{6,5},{9,10},{8,7},{11,12},{10... | collective-permute-start | bytes 2359304 | tf_op jit(solution)/shard_map/ppermute | solution.py:382
  45.1 4.1 %collective-permute-start.7 = (bf16[512,384]{1,0:T(8,128)(2,1)S(1)}, bf16[512,384]{1,0:T(8,128)(2,1)S(1)}, u32[]{:S(2)}, u32[]{:S(2)}) collective-permute-start(bf16[512,384]{1,0:T(8,128)(2,1)S(1)} %get-tuple-element.39), channel_id=1, source_target_pairs={{0,1},{1,0},{2,3},{3,2},{4,5},{5,4},{6,7},{7,6},{8,9},{9,8},{10,11... | collective-permute-start | bytes 1179656 | tf_op jit(solution)/shard_map/ppermute | solution.py:379
  49.3 2.0 %collective-permute-done.10.across_ref = bf16[224,384]{1,0:T(8,128)(2,1)S(1)} collective-permute-done((bf16[224,384]{1,0:T(8,128)(2,1)S(1)}, bf16[224,384]{1,0:T(8,128)(2,1)S(1)}, u32[]{:S(2)}, u32[]{:S(2)}) %collective-permute-start.10) | collective-permute-done | bytes 172064 | tf_op jit(solution)/shard_map/ppermute | solution.py:419
  51.3 6.3 %collective-permute-start.5 = (bf16[384,384]{1,0:T(8,128)(2,1)S(1)}, bf16[384,384]{1,0:T(8,128)(2,1)S(1)}, u32[]{:S(2)}, u32[]{:S(2)}) collective-permute-start(bf16[384,384]{1,0:T(8,128)(2,1)S(1)} %pad_maximum_fusion.4), channel_id=1, source_target_pairs={{64,0},{128,64},{192,128},{65,1},{129,65},{193,129},{66,2},{130,66... | collective-permute-start | bytes 884744 | tf_op jit(solution)/shard_map/ppermute | solution.py:406
  57.6 1.9 %collective-permute-start.4 = (bf16[384,384]{1,0:T(8,128)(2,1)S(1)}, bf16[384,384]{1,0:T(8,128)(2,1)S(1)}, u32[]{:S(2)}, u32[]{:S(2)}) collective-permute-start(bf16[384,384]{1,0:T(8,128)(2,1)S(1)} %pad_maximum_fusion.3), channel_id=1, source_target_pairs={{0,64},{64,128},{128,192},{1,65},{65,129},{129,193},{2,66},{66,130... | collective-permute-start | bytes 884744 | tf_op jit(solution)/shard_map/ppermute | solution.py:403
  59.6 3.7 %collective-permute-done.5.down_ref = bf16[384,384]{1,0:T(8,128)(2,1)S(1)} collective-permute-done((bf16[384,384]{1,0:T(8,128)(2,1)S(1)}, bf16[384,384]{1,0:T(8,128)(2,1)S(1)}, u32[]{:S(2)}, u32[]{:S(2)}) %collective-permute-start.5) | collective-permute-done | bytes 294944 | tf_op jit(solution)/shard_map/ppermute | solution.py:406
  63.3 4.1 %collective-permute-done.4.up_ref = bf16[384,384]{1,0:T(8,128)(2,1)S(1)} collective-permute-done((bf16[384,384]{1,0:T(8,128)(2,1)S(1)}, bf16[384,384]{1,0:T(8,128)(2,1)S(1)}, u32[]{:S(2)}, u32[]{:S(2)}) %collective-permute-start.4) | collective-permute-done | bytes 294944 | tf_op jit(solution)/shard_map/ppermute | solution.py:403
  67.6 1.9 %collective-permute-start.12 = (bf16[640,384]{1,0:T(8,128)(2,1)S(1)}, bf16[640,384]{1,0:T(8,128)(2,1)S(1)}, u32[]{:S(2)}, u32[]{:S(2)}) collective-permute-start(bf16[640,384]{1,0:T(8,128)(2,1)S(1)} %pad_maximum_fusion.1), channel_id=1, source_target_pairs={{1,2},{3,4},{2,1},{5,6},{4,3},{7,8},{6,5},{9,10},{8,7},{11,12},{10... | collective-permute-start | bytes 1474568 | tf_op jit(solution)/shard_map/ppermute | solution.py:382
  69.6 2.8 %collective-permute-start.15 = (bf16[128,384]{1,0:T(8,128)(2,1)S(1)}, bf16[128,384]{1,0:T(8,128)(2,1)S(1)}, u32[]{:S(2)}, u32[]{:S(2)}) collective-permute-start(bf16[128,384]{1,0:T(8,128)(2,1)S(1)} %collective-permute-done.z_one_ref), channel_id=1, source_target_pairs={{0,1},{1,0},{2,3},{3,2},{4,5},{5,4},{6,7},{7,6},{8,9},{9,8},{10,11... | collective-permute-start | bytes 294920 | tf_op jit(solution)/shard_map/ppermute | solution.py:379
  72.4 0.1 collective-permute-start.16
  72.5 0.5 collective-permute-start.13
  73.0 4.8 %collective-permute-done.12.side_ref = bf16[640,384]{1,0:T(8,128)(2,1)S(1)} collective-permute-done((bf16[640,384]{1,0:T(8,128)(2,1)S(1)}, bf16[640,384]{1,0:T(8,128)(2,1)S(1)}, u32[]{:S(2)}, u32[]{:S(2)}) %collective-permute-start.12) | collective-permute-done | bytes 491552 | tf_op jit(solution)/shard_map/ppermute | solution.py:382
  77.8 1.0 collective-permute-start.14
  78.9 0.1 collective-permute-start.17
  79.0 0.5 collective-permute-start.18
  79.5 0.2 collective-permute-start.19
  79.7 0.7 collective-permute-done.17.oz_three_ref
  80.4 0.4 collective-permute-start.11
  80.8 0.9 collective-permute-done.11.corner_ref
  81.7 0.4 collective-permute-start.20
  82.1 1.0 collective-permute-done.20.other_across_ref
  83.2 0.6 copy-done.20
  83.8 0.1 copy-done.17
  83.9 0.1 copy-done.18
  84.0 0.1 copy-done.13
  84.3 24.6 %shard_map.56 = bf16[4,128,384]{2,1,0:T(8,128)(2,1)} custom-call(s32[3]{0:T(128)} %pad_add_fusion.place_ref, s32[4,27]{1,0:T(4,128)} %fusion.4.idx_one_ref, s32[2,27]{1,0:T(2,128)} %compare_select_fusion.idx_two_ref, bf16[4,448,384]{2,1,0:T(8,128)(2,1)} %copy-done, bf16[4,64,384]{2,1,0:T(8,128)(2,1)} %bitcast.68, bf16[384,384]{1,0:T(8,128)(2,1)} %copy-done.4, ...), custom_call_target="tpu_custom_call" | custom-call | flops 10569646080 | bytes 10485760 | tf_op jit(solution)/shard_map/pallas_call | solution.py:325
  108.9 13.0 %all_to_all.15.o_ref = bf16[4,128,384]{2,1,0:T(8,128)(2,1)} all-to-all(bf16[4,128,384]{2,1,0:T(8,128)(2,1)} %shard_map.56), channel_id=1, replica_groups=mesh['y'=4,'x'=4,'z'=8,'core'=2] {'x'}, dimensions={0} | all-to-all | bytes 786432 | tf_op jit(solution)/shard_map/all_to_all | solution.py:440
  121.9 1.8 %shard_map.57 = bf16[256,768]{1,0:T(8,128)(2,1)} custom-call(bf16[4,128,384]{2,1,0:T(8,128)(2,1)} %all_to_all.15.o_ref), custom_call_target="tpu_custom_call" | custom-call | bytes 1048576 | tf_op jit(solution)/shard_map/pallas_call | solution.py:441
  (87 shorter events, 1.1 us)
Async XLA Ops:
  0.0 7.1 %copy-start.10 = (s32[256,27]{0,1:T(8,128)S(1)}, s32[256,27]{0,1:T(8,128)}, u32[]{:S(2)}) copy-start(s32[256,27]{0,1:T(8,128)} %param.8) | copy-start | bytes 82948
  2.8 10.1 %all-to-all-start.1 = ((bf16[8,16,384]{2,1,0:T(8,128)(2,1)}), bf16[8,16,384]{2,1,0:T(8,128)(2,1)S(1)}, u32[]{:S(2)}, u32[]{:S(2)}) async-start(bf16[8,16,384]{2,1,0:T(8,128)(2,1)} %bitcast.88), calls=%async_computation.1 | async-start | bytes 196608 | tf_op jit(solution)/shard_map/all_to_all | solution.py:392
  12.9 9.1 %copy-start.5 = (bf16[8,16,384]{2,1,0:T(8,128)(2,1)}, bf16[8,16,384]{2,1,0:T(8,128)(2,1)S(1)}, u32[]{:S(2)}) copy-start(bf16[8,16,384]{2,1,0:T(8,128)(2,1)S(1)} %all-to-all-done.1) | copy-start | bytes 294916
  12.9 3.8 %copy-start.11 = (s32[64,27]{0,1:T(8,128)S(1)}, s32[64,27]{0,1:T(8,128)}, u32[]{:S(2)}) copy-start(s32[64,27]{0,1:T(8,128)} %param.9) | copy-start | bytes 20740
  12.9 22.4 %all-to-all-start = ((bf16[4,448,384]{2,1,0:T(8,128)(2,1)}), bf16[4,448,384]{2,1,0:T(8,128)(2,1)S(1)}, u32[]{:S(2)}, u32[]{:S(2)}) async-start(bf16[4,448,384]{2,1,0:T(8,128)(2,1)} %get-tuple-element.21), calls=%async_computation | async-start | bytes 2752512 | tf_op jit(solution)/shard_map/all_to_all | solution.py:393
  18.7 5.9 %collective-permute-start = (bf16[128,384]{1,0:T(8,128)(2,1)S(1)}, bf16[128,384]{1,0:T(8,128)(2,1)S(1)}, u32[]{:S(2)}, u32[]{:S(2)}) collective-permute-start(bf16[128,384]{1,0:T(8,128)(2,1)S(1)} %bitcast.80), channel_id=1, source_target_pairs={{1,2},{3,4},{2,1},{5,6},{4,3},{7,8},{6,5},{9,10},{8,7},{11,12},{10... | collective-permute-start | bytes 294920 | tf_op jit(solution)/shard_map/ppermute | solution.py:382
  20.6 4.0 %collective-permute-start.1 = (bf16[128,384]{1,0:T(8,128)(2,1)S(1)}, bf16[128,384]{1,0:T(8,128)(2,1)S(1)}, u32[]{:S(2)}, u32[]{:S(2)}) collective-permute-start(bf16[128,384]{1,0:T(8,128)(2,1)S(1)} %bitcast.81), channel_id=1, source_target_pairs={{1,4},{3,6},{5,8},{4,1},{7,10},{6,3},{9,12},{8,5},{11,14},{10,7},{... | collective-permute-start | bytes 294920 | tf_op jit(solution)/shard_map/ppermute | solution.py:382
  21.3 3.3 %collective-permute-start.2 = (bf16[128,384]{1,0:T(8,128)(2,1)S(1)}, bf16[128,384]{1,0:T(8,128)(2,1)S(1)}, u32[]{:S(2)}, u32[]{:S(2)}) collective-permute-start(bf16[128,384]{1,0:T(8,128)(2,1)S(1)} %bitcast.82), channel_id=1, source_target_pairs={{1,6},{3,8},{5,10},{7,12},{6,1},{9,14},{8,3},{10,5},{12,7},{14,9},... | collective-permute-start | bytes 294920 | tf_op jit(solution)/shard_map/ppermute | solution.py:382
  24.6 44.9 %copy-start.6 = (bf16[128,384]{1,0:T(8,128)(2,1)}, bf16[128,384]{1,0:T(8,128)(2,1)S(1)}, u32[]{:S(2)}) copy-start(bf16[128,384]{1,0:T(8,128)(2,1)S(1)} %collective-permute-done.z_one_ref) | copy-start | bytes 294916
  24.7 47.7 %copy-start.7 = (bf16[128,384]{1,0:T(8,128)(2,1)}, bf16[128,384]{1,0:T(8,128)(2,1)S(1)}, u32[]{:S(2)}) copy-start(bf16[128,384]{1,0:T(8,128)(2,1)S(1)} %collective-permute-done.1.z_two_ref) | copy-start | bytes 294916
  24.7 54.2 %copy-start.8 = (bf16[128,384]{1,0:T(8,128)(2,1)}, bf16[128,384]{1,0:T(8,128)(2,1)S(1)}, u32[]{:S(2)}) copy-start(bf16[128,384]{1,0:T(8,128)(2,1)S(1)} %collective-permute-done.2.z_three_ref) | copy-start | bytes 294916
  35.3 6.4 %copy-start = (bf16[4,448,384]{2,1,0:T(8,128)(2,1)}, bf16[4,448,384]{2,1,0:T(8,128)(2,1)S(1)}, u32[]{:S(2)}) copy-start(bf16[4,448,384]{2,1,0:T(8,128)(2,1)S(1)} %all-to-all-done.own_ref) | copy-start | bytes 4128772
  35.3 22.3 %collective-permute-start.8 = (bf16[448,384]{1,0:T(8,128)(2,1)S(1)}, bf16[448,384]{1,0:T(8,128)(2,1)S(1)}, u32[]{:S(2)}, u32[]{:S(2)}) collective-permute-start(bf16[448,384]{1,0:T(8,128)(2,1)S(1)} %pad_maximum_fusion.2), channel_id=1, source_target_pairs={{0,64},{64,128},{128,192},{1,65},{65,129},{129,193},{2,66},{66,130... | collective-permute-start | bytes 1032200 | tf_op jit(solution)/shard_map/ppermute | solution.py:414
  38.5 21.0 %collective-permute-start.9 = (bf16[448,384]{1,0:T(8,128)(2,1)S(1)}, bf16[448,384]{1,0:T(8,128)(2,1)S(1)}, u32[]{:S(2)}, u32[]{:S(2)}) collective-permute-start(bf16[448,384]{1,0:T(8,128)(2,1)S(1)} %pad_maximum_fusion.2), channel_id=1, source_target_pairs={{64,0},{128,64},{192,128},{65,1},{129,65},{193,129},{66,2},{130,66... | collective-permute-start | bytes 1032200 | tf_op jit(solution)/shard_map/ppermute | solution.py:415
  41.4 9.9 %collective-permute-start.10 = (bf16[224,384]{1,0:T(8,128)(2,1)S(1)}, bf16[224,384]{1,0:T(8,128)(2,1)S(1)}, u32[]{:S(2)}, u32[]{:S(2)}) collective-permute-start(bf16[224,384]{1,0:T(8,128)(2,1)S(1)} %pad_maximum_fusion.5), channel_id=1, source_target_pairs={{0,128},{64,192},{128,0},{192,64},{1,129},{65,193},{129,1},{193,65... | collective-permute-start | bytes 516104 | tf_op jit(solution)/shard_map/ppermute | solution.py:419
  41.5 1.5 %collective-permute-start.3 = (bf16[256,384]{1,0:T(8,128)(2,1)S(1)}, bf16[256,384]{1,0:T(8,128)(2,1)S(1)}, u32[]{:S(2)}, u32[]{:S(2)}) collective-permute-start(bf16[256,384]{1,0:T(8,128)(2,1)S(1)} %bitcast.69), channel_id=1, source_target_pairs={{0,1},{1,0},{2,3},{3,2},{4,5},{5,4},{6,7},{7,6},{8,9},{9,8},{10,11... | collective-permute-start | bytes 589832 | tf_op jit(solution)/shard_map/ppermute | solution.py:379
  43.0 6.2 %copy-start.1 = (bf16[256,384]{1,0:T(8,128)(2,1)}, bf16[256,384]{1,0:T(8,128)(2,1)S(1)}, u32[]{:S(2)}) copy-start(bf16[256,384]{1,0:T(8,128)(2,1)S(1)} %collective-permute-done.3) | copy-start | bytes 589828
  43.1 24.4 %collective-permute-start.6 = (bf16[1024,384]{1,0:T(8,128)(2,1)S(1)}, bf16[1024,384]{1,0:T(8,128)(2,1)S(1)}, u32[]{:S(2)}, u32[]{:S(2)}) collective-permute-start(bf16[1024,384]{1,0:T(8,128)(2,1)S(1)} %pad_maximum_fusion), channel_id=1, source_target_pairs={{1,2},{3,4},{2,1},{5,6},{4,3},{7,8},{6,5},{9,10},{8,7},{11,12},{10... | collective-permute-start | bytes 2359304 | tf_op jit(solution)/shard_map/ppermute | solution.py:382
  45.1 14.5 %collective-permute-start.7 = (bf16[512,384]{1,0:T(8,128)(2,1)S(1)}, bf16[512,384]{1,0:T(8,128)(2,1)S(1)}, u32[]{:S(2)}, u32[]{:S(2)}) collective-permute-start(bf16[512,384]{1,0:T(8,128)(2,1)S(1)} %get-tuple-element.39), channel_id=1, source_target_pairs={{0,1},{1,0},{2,3},{3,2},{4,5},{5,4},{6,7},{7,6},{8,9},{9,8},{10,11... | collective-permute-start | bytes 1179656 | tf_op jit(solution)/shard_map/ppermute | solution.py:379
  51.3 30.4 %copy-start.19 = (bf16[224,384]{1,0:T(8,128)(2,1)}, bf16[224,384]{1,0:T(8,128)(2,1)S(1)}, u32[]{:S(2)}) copy-start(bf16[224,384]{1,0:T(8,128)(2,1)S(1)} %collective-permute-done.10.across_ref) | copy-start | bytes 516100
  51.3 12.0 %collective-permute-start.5 = (bf16[384,384]{1,0:T(8,128)(2,1)S(1)}, bf16[384,384]{1,0:T(8,128)(2,1)S(1)}, u32[]{:S(2)}, u32[]{:S(2)}) collective-permute-start(bf16[384,384]{1,0:T(8,128)(2,1)S(1)} %pad_maximum_fusion.4), channel_id=1, source_target_pairs={{64,0},{128,64},{192,128},{65,1},{129,65},{193,129},{66,2},{130,66... | collective-permute-start | bytes 884744 | tf_op jit(solution)/shard_map/ppermute | solution.py:406
  57.6 21.4 %copy-start.15 = (bf16[448,384]{1,0:T(8,128)(2,1)}, bf16[448,384]{1,0:T(8,128)(2,1)S(1)}, u32[]{:S(2)}) copy-start(bf16[448,384]{1,0:T(8,128)(2,1)S(1)} %collective-permute-done.8.up_two_ref) | copy-start | bytes 1032196
  57.6 9.9 %collective-permute-start.4 = (bf16[384,384]{1,0:T(8,128)(2,1)S(1)}, bf16[384,384]{1,0:T(8,128)(2,1)S(1)}, u32[]{:S(2)}, u32[]{:S(2)}) collective-permute-start(bf16[384,384]{1,0:T(8,128)(2,1)S(1)} %pad_maximum_fusion.3), channel_id=1, source_target_pairs={{0,64},{64,128},{128,192},{1,65},{65,129},{129,193},{2,66},{66,130... | collective-permute-start | bytes 884744 | tf_op jit(solution)/shard_map/ppermute | solution.py:403
  59.5 20.0 %copy-start.16 = (bf16[448,384]{1,0:T(8,128)(2,1)}, bf16[448,384]{1,0:T(8,128)(2,1)S(1)}, u32[]{:S(2)}) copy-start(bf16[448,384]{1,0:T(8,128)(2,1)S(1)} %collective-permute-done.9.down_two_ref) | copy-start | bytes 1032196
  59.6 12.9 %copy-start.12 = (bf16[512,384]{1,0:T(8,128)(2,1)}, bf16[512,384]{1,0:T(8,128)(2,1)S(1)}, u32[]{:S(2)}) copy-start(bf16[512,384]{1,0:T(8,128)(2,1)S(1)} %collective-permute-done.7.inner_ref) | copy-start | bytes 1179652
  63.3 9.2 %copy-start.3 = (bf16[384,384]{1,0:T(8,128)(2,1)}, bf16[384,384]{1,0:T(8,128)(2,1)S(1)}, u32[]{:S(2)}) copy-start(bf16[384,384]{1,0:T(8,128)(2,1)S(1)} %collective-permute-done.5.down_ref) | copy-start | bytes 884740
  67.5 5.1 %copy-start.4 = (bf16[384,384]{1,0:T(8,128)(2,1)}, bf16[384,384]{1,0:T(8,128)(2,1)S(1)}, u32[]{:S(2)}) copy-start(bf16[384,384]{1,0:T(8,128)(2,1)S(1)} %collective-permute-done.4.up_ref) | copy-start | bytes 884740
  67.5 5.1 %copy-start.9 = (bf16[1024,384]{1,0:T(8,128)(2,1)}, bf16[1024,384]{1,0:T(8,128)(2,1)S(1)}, u32[]{:S(2)}) copy-start(bf16[1024,384]{1,0:T(8,128)(2,1)S(1)} %collective-permute-done.6.outer_ref) | copy-start | bytes 2359300
  67.6 10.1 %collective-permute-start.12 = (bf16[640,384]{1,0:T(8,128)(2,1)S(1)}, bf16[640,384]{1,0:T(8,128)(2,1)S(1)}, u32[]{:S(2)}, u32[]{:S(2)}) collective-permute-start(bf16[640,384]{1,0:T(8,128)(2,1)S(1)} %pad_maximum_fusion.1), channel_id=1, source_target_pairs={{1,2},{3,4},{2,1},{5,6},{4,3},{7,8},{6,5},{9,10},{8,7},{11,12},{10... | collective-permute-start | bytes 1474568 | tf_op jit(solution)/shard_map/ppermute | solution.py:382
  69.6 9.4 %collective-permute-start.15 = (bf16[128,384]{1,0:T(8,128)(2,1)S(1)}, bf16[128,384]{1,0:T(8,128)(2,1)S(1)}, u32[]{:S(2)}, u32[]{:S(2)}) collective-permute-start(bf16[128,384]{1,0:T(8,128)(2,1)S(1)} %collective-permute-done.z_one_ref), channel_id=1, source_target_pairs={{0,1},{1,0},{2,3},{3,2},{4,5},{5,4},{6,7},{7,6},{8,9},{9,8},{10,11... | collective-permute-start | bytes 294920 | tf_op jit(solution)/shard_map/ppermute | solution.py:379
  72.4 7.1 %collective-permute-start.16 = (bf16[128,384]{1,0:T(8,128)(2,1)S(1)}, bf16[128,384]{1,0:T(8,128)(2,1)S(1)}, u32[]{:S(2)}, u32[]{:S(2)}) collective-permute-start(bf16[128,384]{1,0:T(8,128)(2,1)S(1)} %collective-permute-done.1.z_two_ref), channel_id=1, source_target_pairs={{0,1},{1,0},{2,3},{3,2},{4,5},{5,4},{6,7},{7,6},{8,9},{9,8},{10,11... | collective-permute-start | bytes 294920 | tf_op jit(solution)/shard_map/ppermute | solution.py:379
  72.5 10.6 %collective-permute-start.13 = (bf16[512,384]{1,0:T(8,128)(2,1)S(1)}, bf16[512,384]{1,0:T(8,128)(2,1)S(1)}, u32[]{:S(2)}, u32[]{:S(2)}) collective-permute-start(bf16[512,384]{1,0:T(8,128)(2,1)S(1)} %slice.83), channel_id=1, source_target_pairs={{0,1},{1,0},{2,3},{3,2},{4,5},{5,4},{6,7},{7,6},{8,9},{9,8},{10,11... | collective-permute-start | bytes 1179656 | tf_op jit(solution)/shard_map/ppermute | solution.py:379
  77.8 5.4 %copy-start.2 = (bf16[640,384]{1,0:T(8,128)(2,1)}, bf16[640,384]{1,0:T(8,128)(2,1)S(1)}, u32[]{:S(2)}) copy-start(bf16[640,384]{1,0:T(8,128)(2,1)S(1)} %collective-permute-done.12.side_ref) | copy-start | bytes 1474564
  77.8 5.3 %collective-permute-start.14 = (bf16[512,384]{1,0:T(8,128)(2,1)S(1)}, bf16[512,384]{1,0:T(8,128)(2,1)S(1)}, u32[]{:S(2)}, u32[]{:S(2)}) collective-permute-start(bf16[512,384]{1,0:T(8,128)(2,1)S(1)} %slice.95), channel_id=1, source_target_pairs={{0,1},{1,0},{2,3},{3,2},{4,5},{5,4},{6,7},{7,6},{8,9},{9,8},{10,11... | collective-permute-start | bytes 1179656 | tf_op jit(solution)/shard_map/ppermute | solution.py:379
  78.9 1.5 %collective-permute-start.17 = (bf16[128,384]{1,0:T(8,128)(2,1)S(1)}, bf16[128,384]{1,0:T(8,128)(2,1)S(1)}, u32[]{:S(2)}, u32[]{:S(2)}) collective-permute-start(bf16[128,384]{1,0:T(8,128)(2,1)S(1)} %collective-permute-done.2.z_three_ref), channel_id=1, source_target_pairs={{0,1},{1,0},{2,3},{3,2},{4,5},{5,4},{6,7},{7,6},{8,9},{9,8},{10,11... | collective-permute-start | bytes 294920 | tf_op jit(solution)/shard_map/ppermute | solution.py:379
  79.0 4.2 %copy-start.21 = (bf16[128,384]{1,0:T(8,128)(2,1)}, bf16[128,384]{1,0:T(8,128)(2,1)S(1)}, u32[]{:S(2)}) copy-start(bf16[128,384]{1,0:T(8,128)(2,1)S(1)} %collective-permute-done.15.oz_one_ref) | copy-start | bytes 294916
  79.0 4.1 %collective-permute-start.18 = (bf16[448,384]{1,0:T(8,128)(2,1)S(1)}, bf16[448,384]{1,0:T(8,128)(2,1)S(1)}, u32[]{:S(2)}, u32[]{:S(2)}) collective-permute-start(bf16[448,384]{1,0:T(8,128)(2,1)S(1)} %collective-permute-done.8.up_two_ref), channel_id=1, source_target_pairs={{0,1},{1,0},{2,3},{3,2},{4,5},{5,4},{6,7},{7,6},{8,9},{9,8},{10,11... | collective-permute-start | bytes 1032200 | tf_op jit(solution)/shard_map/ppermute | solution.py:379
  79.5 3.7 %copy-start.22 = (bf16[128,384]{1,0:T(8,128)(2,1)}, bf16[128,384]{1,0:T(8,128)(2,1)S(1)}, u32[]{:S(2)}) copy-start(bf16[128,384]{1,0:T(8,128)(2,1)S(1)} %collective-permute-done.16.oz_two_ref) | copy-start | bytes 294916
  79.5 3.6 %collective-permute-start.19 = (bf16[448,384]{1,0:T(8,128)(2,1)S(1)}, bf16[448,384]{1,0:T(8,128)(2,1)S(1)}, u32[]{:S(2)}, u32[]{:S(2)}) collective-permute-start(bf16[448,384]{1,0:T(8,128)(2,1)S(1)} %collective-permute-done.9.down_two_ref), channel_id=1, source_target_pairs={{0,1},{1,0},{2,3},{3,2},{4,5},{5,4},{6,7},{7,6},{8,9},{9,8},{10,11... | collective-permute-start | bytes 1032200 | tf_op jit(solution)/shard_map/ppermute | solution.py:379
  80.4 2.8 %copy-start.23 = (bf16[128,384]{1,0:T(8,128)(2,1)}, bf16[128,384]{1,0:T(8,128)(2,1)S(1)}, u32[]{:S(2)}) copy-start(bf16[128,384]{1,0:T(8,128)(2,1)S(1)} %collective-permute-done.17.oz_three_ref) | copy-start | bytes 294916
  80.4 1.3 %collective-permute-start.11 = (bf16[128,384]{1,0:T(8,128)(2,1)S(1)}, bf16[128,384]{1,0:T(8,128)(2,1)S(1)}, u32[]{:S(2)}, u32[]{:S(2)}) collective-permute-start(bf16[128,384]{1,0:T(8,128)(2,1)S(1)} %pad_maximum_fusion.6), channel_id=1, source_target_pairs={{0,1},{1,0},{2,3},{3,2},{4,5},{5,4},{6,7},{7,6},{8,9},{9,8},{10,11... | collective-permute-start | bytes 294920 | tf_op jit(solution)/shard_map/ppermute | solution.py:379
  81.7 1.5 %copy-start.24 = (bf16[128,384]{1,0:T(8,128)(2,1)}, bf16[128,384]{1,0:T(8,128)(2,1)S(1)}, u32[]{:S(2)}) copy-start(bf16[128,384]{1,0:T(8,128)(2,1)S(1)} %collective-permute-done.11.corner_ref) | copy-start | bytes 294916
  81.7 1.4 %collective-permute-start.20 = (bf16[224,384]{1,0:T(8,128)(2,1)S(1)}, bf16[224,384]{1,0:T(8,128)(2,1)S(1)}, u32[]{:S(2)}, u32[]{:S(2)}) collective-permute-start(bf16[224,384]{1,0:T(8,128)(2,1)S(1)} %collective-permute-done.10.across_ref), channel_id=1, source_target_pairs={{0,1},{1,0},{2,3},{3,2},{4,5},{5,4},{6,7},{7,6},{8,9},{9,8},{10,11... | collective-permute-start | bytes 516104 | tf_op jit(solution)/shard_map/ppermute | solution.py:379
  83.1 0.7 copy-start.20
  83.1 0.8 copy-start.17
  83.1 0.9 copy-start.18
  83.1 1.0 copy-start.13
  83.2 1.1 copy-start.14

commit v4 on v3

--- a/solution.py
+++ b/solution.py
@@ -25,10 +25,10 @@
     return lax.broadcasted_iota(jnp.int32, shape, dim)
 
 
-FINE, QUERY, ONE, PACKED = 0, 256, 384, 448
-
-
-def prep_kernel(q_ref, k_ref, v_ref, two_ref, out_ref):
+FINE, QUERY, ONE, TWO, PACKED = 0, 256, 384, 448, 464
+
+
+def prep_kernel(q_ref, k_ref, v_ref, out_ref):
     row = iota((80, 256), 0)
     tok = iota((80, 256), 1)
     trow, tcol = tok >> 4, tok & 15
@@ -52,11 +52,9 @@
         out_ref[j, QUERY:ONE, 256:384] = jnp.concatenate(
             [q[0:128, third], q[128:256, third]], axis=1
         )
-        both = jnp.concatenate([kc[:, third], vc[:, third]], axis=1)
-        for lanes, part in ((0, kc[:, pair]), (128, vc[:, pair]), (256, both)):
-            out_ref[j, ONE:PACKED, lanes:lanes + 128] = part[0:64]
-            for core in range(2):
-                two_ref[j, core, :, lanes:lanes + 128] = part[64:80]
+        out_ref[j, ONE:PACKED, 0:128] = kc[:, pair]
+        out_ref[j, ONE:PACKED, 128:256] = vc[:, pair]
+        out_ref[j, ONE:PACKED, 256:384] = jnp.concatenate([kc[:, third], vc[:, third]], axis=1)
 
 
 def unpack_kernel(o_ref, out_ref):
@@ -83,11 +81,10 @@
 
 def attend_kernel(
     place_ref, idx_one_ref, idx_two_ref,
-    own_ref, other_ref, up_ref, down_ref,
-    inner_ref, corner_ref, outer_ref, side_ref, other_outer_ref, other_side_ref, own_two_ref,
-    z_one_ref, z_two_ref, z_three_ref, up_two_ref, down_two_ref, across_ref,
-    oz_one_ref, oz_two_ref, oz_three_ref, other_up_ref, other_down_ref, other_across_ref,
-    out_ref, one_ref, two_ref, tall_ref, in_ref, out_strip_ref, kv_ref, kv_next_ref, s_pair_ref, s_third_ref,
+    own_ref, other_ref, up_ref, down_ref, inner_ref, side_ref, other_side_ref,
+    row_ref, up_two_ref, down_two_ref, across_ref,
+    other_row_ref, other_up_ref, other_down_ref, other_across_ref,
+    out_ref, one_ref, two_ref, tall_ref, kv_ref, kv_next_ref, s_pair_ref, s_third_ref,
 ):
     y = place_ref[0]
     z = place_ref[1]
@@ -97,21 +94,12 @@
     tall_ref[1152:1280] = down_ref[256:384]
     for xs in range(4):
         tall_ref[128 + 256 * xs:384 + 256 * xs] = own_ref[xs, FINE:QUERY]
-    for strip_ref, middle_ref, ends_ref, at in (
-        (in_ref, inner_ref, corner_ref, 0), (out_strip_ref, outer_ref, side_ref, 512),
-    ):
-        strip_ref[0:64] = ends_ref[at:at + 64]
-        strip_ref[64:576] = middle_ref[at:at + 512]
-        strip_ref[576:640] = ends_ref[at + 64:at + 128]
 
     def quarter(xs, kk):
         return pl.ds(pl.multiple_of(32 * (xs & 1) + 16 * kk, 16), 16)
 
     def put_one(row, col, block):
         one_ref[row * 6 + col] = block
-
-    def put_two(brow, bcol, xs, kk, block):
-        two_ref[brow * 7 + bcol, quarter(xs, kk)] = block
 
     for m in range(2):
         kk = core if m == 0 else 1 - core
@@ -123,45 +111,31 @@
             at = 128 * m + 64 * i
             put_one(i, 2 + kk, up_ref[at:at + 64])
             put_one(6 + i, 2 + kk, down_ref[at:at + 64])
-    for side, middle, ends in ((core, outer_ref, side_ref), (1 - core, other_outer_ref, other_side_ref)):
+    for side, one_side in ((core, side_ref), (1 - core, other_side_ref)):
         for m in range(2):
             kk = 1 - side if m == 0 else side
             for i in range(4):
                 at = 256 * m + 64 * i
-                put_one(2 + i, 4 * side + kk, middle[at:at + 64])
+                put_one(2 + i, 4 * side + kk, one_side[at:at + 64])
             for i in range(2):
-                at = 128 * m + 64 * i
-                put_one(i, 4 * side + kk, ends[at:at + 64])
-                put_one(6 + i, 4 * side + kk, ends[at + 256:at + 320])
-    for xs in range(4):
-        for kk in range(2):
-            put_two(3 + xs // 2, 3, xs, kk, own_two_ref[xs, kk])
-    end = jnp.where(y >= 2, 0, 7)
-    for side, twos, ups, across in (
-        (core, (z_one_ref, z_two_ref, z_three_ref), (up_two_ref, down_two_ref), across_ref),
-        (
-            1 - core, (oz_one_ref, oz_two_ref, oz_three_ref),
-            (other_up_ref, other_down_ref), other_across_ref,
-        ),
+                at = 512 + 128 * m + 64 * i
+                put_one(i, 4 * side + kk, one_side[at:at + 64])
+                put_one(6 + i, 4 * side + kk, one_side[at + 256:at + 320])
+    end = jnp.where(y >= 2, 2 * y - 1, 2 * y + 6)
+    for kk, row, ups, downs, across in (
+        (core, row_ref, up_two_ref, down_two_ref, across_ref),
+        (1 - core, other_row_ref, other_up_ref, other_down_ref, other_across_ref),
     ):
-        step = 2 * side - 1
-        for xs in range(4):
-            put_two(1 + xs // 2, 3, xs, side, ups[0][16 * xs:16 * xs + 16])
-            put_two(5 + xs // 2, 3, xs, side, ups[1][16 * xs:16 * xs + 16])
-        for i in range(2):
-            put_two(end, 3, i, side, across[16 * i:16 * i + 16])
-        for far in (1, 2, 3):
-            col = 3 + far * step
-            for kk in range(2):
-                for xs in range(4):
-                    at = 32 * xs + 16 * kk
-                    put_two(3 + xs // 2, col, xs, kk, twos[far - 1][at:at + 16])
-                    at = 128 * far - 64 + at
-                    put_two(1 + xs // 2, col, xs, kk, ups[0][at:at + 16])
-                    put_two(5 + xs // 2, col, xs, kk, ups[1][at:at + 16])
-                for i in range(2):
-                    at = 64 * far - 32 + 32 * i + 16 * kk
-                    put_two(end, col, i, kk, across[at:at + 16])
+        for col in range(8):
+            for xs in range(4):
+                at = 64 * col + 16 * xs
+                brow = 2 * y + 2 + xs // 2
+                two_ref[brow * 8 + col, quarter(xs, kk)] = row[at:at + 16]
+                two_ref[(brow - 2) * 8 + col, quarter(xs, kk)] = ups[at:at + 16]
+                two_ref[(brow + 2) * 8 + col, quarter(xs, kk)] = downs[at:at + 16]
+            for i in range(2):
+                at = 32 * col + 16 * i
+                two_ref[end * 8 + col, quarter(i, kk)] = across[at:at + 16]
 
     lane64 = iota((64, 128), 1)
     high_one, low_one = split_bias(1)
@@ -220,8 +194,8 @@
 
         steps = [near(tall_ref, 0, 256, first, 128, 0, 4, 8) for first in range(0, 512, 128)]
         for first in (0, 128):
-            steps.append(near(in_ref, 0, 128, first, 128, 512, 3, inner_col))
-            steps.append(near(out_strip_ref, 0, 128, first, 128, 768, 3, 24 - inner_col))
+            steps.append(near(inner_ref, 0, 128, first, 128, 512, 3, inner_col))
+            steps.append(near(side_ref, 1024, 128, first, 128, 768, 3, 24 - inner_col))
         for j in range(27):
             steps += [far(j, 0), far(j, 1)]
         return steps
@@ -325,13 +299,11 @@
     return call(
         attend_kernel,
         shape(4, 128, 384),
-        [SMEM] * 3 + [VMEM] * 23,
+        [SMEM] * 3 + [VMEM] * 15,
         scratch=[
             pltpu.VMEM((48, 64, 384), BF),
-            pltpu.VMEM((56, 64, 384), BF),
+            pltpu.VMEM((96, 64, 384), BF),
             pltpu.VMEM((1280, 384), BF),
-            pltpu.VMEM((640, 384), BF),
-            pltpu.VMEM((640, 384), BF),
             pltpu.VMEM((KEYS, 512), BF),
             pltpu.VMEM((KEYS, 512), BF),
             pltpu.VMEM((512, KEYS), F32),
@@ -366,14 +338,15 @@
     self_one = (2 + jnp.arange(4, dtype=jnp.int32)[:, None]) * 6 + 2 + core
     idx_one = jnp.where(entries >= 0, where, -1 - self_one)
     entries = lax.dynamic_slice(list_two.reshape(8, 8, 27), (2 * y, z, 0), (2, 1, 27))[:, 0]
-    where = (entries // 8 - (2 * y - 3)) * 7 + entries % 8 - (z - 3)
-    self_two = (3 + jnp.arange(2, dtype=jnp.int32)[:, None]) * 7 + 3
-    idx_two = jnp.where(entries >= 0, where, -1 - self_two)
+    self_two = (2 * y + 2 + jnp.arange(2, dtype=jnp.int32)[:, None]) * 8 + z
+    idx_two = jnp.where(entries >= 0, entries + 16, -1 - self_two)
     place = jnp.stack([y, z, core]).astype(jnp.int32)
 
-    own_two, packed = call(
-        prep_kernel, [shape(4, 2, 16, 384), shape(4, PACKED, 384)], [VMEM] * 3, nbytes=4 << 20
-    )(queries.reshape(256, 768), keys.reshape(256, 768), values.reshape(256, 768))
+    packed = call(prep_kernel, shape(4, PACKED, 384), [VMEM] * 3, nbytes=4 << 20)(
+        queries.reshape(256, 768), keys.reshape(256, 768), values.reshape(256, 768)
+    )
+    rf = lax.all_to_all(packed, "x", 0, 0, tiled=True)
+    rf, idx_one, idx_two, place = lax.optimization_barrier((rf, idx_one, idx_two, place))
 
     def over_core(array):
         return lax.ppermute(array, "core", [(0, 1), (1, 0)])
@@ -389,53 +362,49 @@
         outer = jnp.where(core == 0, left, right).reshape(rows * 8, 384)
         return inner, outer
 
-    own_two = lax.all_to_all(own_two.reshape(8, 16, 384), ("x", "core"), 0, 0, tiled=True)
-    rf = lax.all_to_all(packed, "x", 0, 0, tiled=True)
-    twos = own_two.reshape(128, 384)
-    twos_z = [over_z(twos, step) for step in (1, 2, 3)]
-    rf, idx_one, idx_two, place, *twos_z = lax.optimization_barrier(
-        (rf, idx_one, idx_two, place, *twos_z)
-    )
-
     fine = rf[:, FINE:QUERY].reshape(1024, 384)
-    other = over_core(rf[:, ONE:PACKED].reshape(256, 384)).reshape(4, 64, 384)
-    ones = (rf[:, ONE:PACKED], other)
+    other = over_core(rf[:, ONE:TWO].reshape(256, 384)).reshape(4, 64, 384)
+    ones = (rf[:, ONE:TWO], other)
+    two = rf[:, TWO:PACKED].reshape(1, 64, 384)
+    row_two = lax.all_to_all(jnp.broadcast_to(two, (8, 64, 384)), "z", 0, 0, tiled=True)
     from_up = lax.ppermute(
         jnp.concatenate([t[2:4].reshape(128, 384) for t in ones] + [fine[896:1024]], axis=0), "y", up
     )
     from_down = lax.ppermute(
         jnp.concatenate([t[0:2].reshape(128, 384) for t in ones] + [fine[0:128]], axis=0), "y", down
     )
-    inner_strip, outer_strip = strips(fine)
-    outer = over_z(jnp.concatenate([t.reshape(256, 384) for t in ones] + [outer_strip], axis=0))
-    own_two = own_two.reshape(4, 2, 16, 384)
-    mine = lax.dynamic_index_in_dim(own_two, core, 1, keepdims=False).reshape(64, 384)
-    near_two = jnp.concatenate([mine, *twos_z], axis=0)
-    up_two = lax.ppermute(near_two, "y", up)
-    down_two = lax.ppermute(near_two, "y", down)
-    half = jnp.where(y < 2, 1, 0)
-    halves = [lax.dynamic_index_in_dim(mine.reshape(2, 32, 384), half, 0, keepdims=False)]
-    halves += [lax.dynamic_index_in_dim(t.reshape(2, 64, 384), half, 0, keepdims=False) for t in twos_z]
-    across_two = lax.ppermute(jnp.concatenate(halves, axis=0), "y", across)
-    inner = over_core(inner_strip)
-    from_up, from_down, outer, inner, up_two, down_two, across_two = lax.optimization_barrier(
-        (from_up, from_down, outer, inner, up_two, down_two, across_two)
-    )
+    row_two, from_up, from_down = lax.optimization_barrier((row_two, from_up, from_down))
 
     top_inner, top_outer = strips(from_up[256:384])
+    middle_inner, middle_outer = strips(fine)
     bottom_inner, bottom_outer = strips(from_down[256:384])
     side = over_z(
-        jnp.concatenate([from_up[0:256], from_down[0:256], top_outer, bottom_outer], axis=0)
-    )
-    corner = over_core(jnp.concatenate([top_inner, bottom_inner], axis=0))
-    twos_side = [*twos_z, up_two, down_two, across_two]
-    others = [over_core(t) for t in twos_side]
-    other_outer = over_core(outer[0:512])
-    other_side = over_core(side[0:512])
+        jnp.concatenate(
+            [t.reshape(256, 384) for t in ones]
+            + [from_up[0:256], from_down[0:256], top_outer, middle_outer, bottom_outer],
+            axis=0,
+        )
+    )
+    inner = over_core(jnp.concatenate([top_inner, middle_inner, bottom_inner], axis=0))
+    up_two = lax.ppermute(row_two.reshape(512, 384), "y", up)
+    down_two = lax.ppermute(row_two.reshape(512, 384), "y", down)
+    half = jnp.where(y < 2, 1, 0)
+    across_two = lax.ppermute(
+        lax.dynamic_index_in_dim(row_two.reshape(8, 2, 32, 384), half, 1, keepdims=False).reshape(256, 384),
+        "y",
+        across,
+    )
+    other_row = over_core(row_two.reshape(512, 384))
+    side, up_two, down_two, across_two, inner, other_row = lax.optimization_barrier(
+        (side, up_two, down_two, across_two, inner, other_row)
+    )
+
+    other_side = over_core(side[0:1024])
+    others = [over_core(t) for t in (up_two, down_two, across_two)]
 
     out = attend_call(
-        place, idx_one, idx_two, rf, other, from_up, from_down,
-        inner, corner, outer, side, other_outer, other_side, own_two, *twos_side, *others,
+        place, idx_one, idx_two, rf, other, from_up, from_down, inner, side, other_side,
+        row_two.reshape(512, 384), up_two, down_two, across_two, other_row, *others,
     )
     back = lax.all_to_all(out, "x", 0, 0, tiled=True)
     tile = call(unpack_kernel, shape(256, 768), [VMEM], nbytes=1 << 20)(back)

time: 124 us -> 121 us (0.976); the launches traced: 124 us -> 119 us
  starting transfers between devices: 39.3 us -> 29.8 us
  local copies, waits for them, and re-layouts: 1.93 us -> 5.7 us
  other arithmetic: 2.3 us -> 4.22 us
    ppermute x3, waiting for transfers between devices: 2.01 us -> 10.9 us  [the longest x1 7.89 us: body(): up_two = lax.ppermute(row_two.reshape(512, 384), 'y', up)]
    ppermute x11 -> x7, starting transfers between devices: 10.1 us -> 1.29 us  [over_core(): return lax.ppermute(array, 'core', [(0, 1), (1, 0)])]
    ppermute x5 -> x1, waiting for transfers between devices: 7.38 us -> 0.01 us  [over_z(): return lax.ppermute(array, ('z', 'core'), z_perm(step))]
    all_to_all x1, waiting for transfers between devices: 10.6 us -> 16.8 us  [body(): rf = lax.all_to_all(packed, 'x', 0, 0, tiled=True)]
    all_to_all x1, waiting for transfers between devices: 5.56 us -> 0.9 us  [body(): lax.all_to_all(jnp.broadcast_to(two, (8, 64, 384)), 'z', 0, 0, tiled=True)]
    all_to_all x1, starting transfers between devices: 4.3 us -> 8.57 us  [body(): lax.all_to_all(jnp.broadcast_to(two, (8, 64, 384)), 'z', 0, 0, tiled=True)]
    ppermute x5 -> x1, starting transfers between devices: 7.08 us -> 2.99 us  [over_z(): return lax.ppermute(array, ('z', 'core'), z_perm(step))]
    ppermute x1, starting transfers between devices: 6.28 us -> 2.36 us  [body(): lax.ppermute(jnp.concatenate([t[0:2].reshape(128, 384) for t in ones] + [...]
  transfers between devices with their start and end apart: 23 -> 15, of which waited for: 11 -> 8; matrix products, arithmetic and copies ran while one was open for 2% -> 4% of each run, Pallas kernels for 0% -> 0%
where the time goes in v4:
time: 121 us; the launch traced here: 119 us
  waiting for transfers between devices  36.7 us (30%)
  starting transfers between devices  29.8 us (25%)
  Pallas kernels  29.4 us (24%)
  blocking collectives  12.8 us (11%)
  local copies, waits for them, and re-layouts  5.7 us (5%)
  other arithmetic  4.22 us (3%)
    pallas_call x1, Pallas kernels, attend_call(): call(attend_kernel, shape(4, 128, 384), [SMEM] * 3 + [VMEM] * 15, scratch...  24.8 us
    all_to_all x1, waiting for transfers between devices, body(): rf = lax.all_to_all(packed, 'x', 0, 0, tiled=True)  16.8 us
    all_to_all x1, blocking collectives, body(): back = lax.all_to_all(out, 'x', 0, 0, tiled=True)  12.8 us
    all_to_all x1, starting transfers between devices, body(): lax.all_to_all(jnp.broadcast_to(two, (8, 64, 384)), 'z', 0, 0, tiled=True)  8.57 us
    ppermute x1, waiting for transfers between devices, body(): up_two = lax.ppermute(row_two.reshape(512, 384), 'y', up)  7.89 us
    all_to_all x1, starting transfers between devices, body(): rf = lax.all_to_all(packed, 'x', 0, 0, tiled=True)  4.42 us
    unnamed x39, local copies, waits for them, and re-layouts  4.12 us
    ppermute x1, starting transfers between devices, body(): up_two = lax.ppermute(row_two.reshape(512, 384), 'y', up)  4.09 us
  transfers between devices with their start and end apart: 15, of which 8 were waited for; matrix products, arithmetic and copies ran while one was open for 4% of the time, Pallas kernels for 0%

profile of v4, /device:TPU:48, one launch (start us, length us, event | category | flops | bytes accessed | tf_op | source)
XLA Modules:
  0.0 118.9 jit_solution(6177203028322429607)
XLA Ops:
  0.0 2.7 %shard_map.55 = bf16[4,464,384]{2,1,0:T(8,128)(2,1)} custom-call(bf16[256,768]{1,0:T(8,128)(2,1)} %bitcast.71, bf16[256,768]{1,0:T(8,128)(2,1)} %bitcast.72, bf16[256,768]{1,0:T(8,128)(2,1)} %bitcast.73), custom_call_target="tpu_custom_call" | custom-call | bytes 4194304 | tf_op jit(solution)/shard_map/pallas_call | solution.py:345
  2.8 4.4 %all-to-all-start = ((bf16[4,464,384]{2,1,0:T(8,128)(2,1)}), bf16[4,464,384]{2,1,0:T(8,128)(2,1)S(1)}, u32[]{:S(2)}, u32[]{:S(2)}) async-start(bf16[4,464,384]{2,1,0:T(8,128)(2,1)} %shard_map.55), calls=%async_computation | async-start | bytes 2850816 | tf_op jit(solution)/shard_map/all_to_all | solution.py:348
  7.2 0.1 copy.11
  7.3 0.1 reshape.110
  7.4 0.1 constant_dynamic-slice_fusion.2
  7.5 0.1 copy.10
  7.6 0.6 pad_add_fusion.place_ref
  8.2 0.6 bitcast_select_fusion.idx_two_ref
  8.9 0.7 fusion.4.idx_one_ref
  9.5 16.8 %all-to-all-done.own_ref = bf16[4,464,384]{2,1,0:T(8,128)(2,1)S(1)} async-done(((bf16[4,464,384]{2,1,0:T(8,128)(2,1)}), bf16[4,464,384]{2,1,0:T(8,128)(2,1)S(1)}, u32[]{:S(2)}, u32[]{:S(2)}) %all-to-all-start) | async-done | bytes 1425440 | tf_op jit(solution)/shard_map/all_to_all | solution.py:348
  26.3 0.1 slice.69
  26.5 0.1 collective-permute-start
  26.6 1.0 broadcast_in_dim.28
  27.5 8.6 %all-to-all-start.1 = ((bf16[8,64,384]{2,1,0:T(8,128)(2,1)}), bf16[8,64,384]{2,1,0:T(8,128)(2,1)S(1)}, u32[]{:S(2)}, u32[]{:S(2)}) async-start(bf16[8,64,384]{2,1,0:T(8,128)(2,1)} %broadcast_in_dim.28), calls=%async_computation.1 | async-start | bytes 786432 | tf_op jit(solution)/shard_map/all_to_all | solution.py:369
  36.2 2.4 %collective-permute-start.2 = (bf16[384,384]{1,0:T(8,128)(2,1)S(1)}, bf16[384,384]{1,0:T(8,128)(2,1)S(1)}, u32[]{:S(2)}, u32[]{:S(2)}) collective-permute-start(bf16[384,384]{1,0:T(8,128)(2,1)S(1)} %pad_maximum_fusion.2), channel_id=1, source_target_pairs={{64,0},{128,64},{192,128},{65,1},{129,65},{193,129},{66,2},{130,66... | collective-permute-start | bytes 884744 | tf_op jit(solution)/shard_map/ppermute | solution.py:373
  38.6 3.5 %collective-permute-start.1 = (bf16[384,384]{1,0:T(8,128)(2,1)S(1)}, bf16[384,384]{1,0:T(8,128)(2,1)S(1)}, u32[]{:S(2)}, u32[]{:S(2)}) collective-permute-start(bf16[384,384]{1,0:T(8,128)(2,1)S(1)} %pad_maximum_fusion.1), channel_id=1, source_target_pairs={{0,64},{64,128},{128,192},{1,65},{65,129},{129,193},{2,66},{66,130... | collective-permute-start | bytes 884744 | tf_op jit(solution)/shard_map/ppermute | solution.py:370
  42.1 0.7 constant_dynamic-update-slice_fusion.1
  42.8 0.7 constant_dynamic-update-slice_fusion
  43.5 3.2 %collective-permute-done.2.down_ref = bf16[384,384]{1,0:T(8,128)(2,1)S(1)} collective-permute-done((bf16[384,384]{1,0:T(8,128)(2,1)S(1)}, bf16[384,384]{1,0:T(8,128)(2,1)S(1)}, u32[]{:S(2)}, u32[]{:S(2)}) %collective-permute-start.2) | collective-permute-done | bytes 294944 | tf_op jit(solution)/shard_map/ppermute | solution.py:373
  46.8 2.1 %collective-permute-done.1.up_ref = bf16[384,384]{1,0:T(8,128)(2,1)S(1)} collective-permute-done((bf16[384,384]{1,0:T(8,128)(2,1)S(1)}, bf16[384,384]{1,0:T(8,128)(2,1)S(1)}, u32[]{:S(2)}, u32[]{:S(2)}) %collective-permute-start.1) | collective-permute-done | bytes 294944 | tf_op jit(solution)/shard_map/ppermute | solution.py:370
  48.9 0.9 all-to-all-done.1
  49.9 0.8 slice_dynamic-update-slice_fusion.1
  50.6 0.7 slice_dynamic-update-slice_fusion
  51.3 0.6 bitcast_dynamic-update-slice_fusion.2
  52.0 0.9 bitcast_dynamic-update-slice_fusion
  52.8 0.6 bitcast_dynamic-update-slice_fusion.1
  53.4 3.0 %collective-permute-start.3 = (bf16[1664,384]{1,0:T(8,128)(2,1)}, bf16[1664,384]{1,0:T(8,128)(2,1)S(1)}, u32[]{:S(2)}, u32[]{:S(2)}) collective-permute-start(bf16[1664,384]{1,0:T(8,128)(2,1)} %bitcast_dynamic-update-slice_fusion.1), channel_id=1, source_target_pairs={{1,2},{3,4},{2,1},{5,6},{4,3},{7,8},{6,5},{9,10},{8,7},{11,12},{10... | collective-permute-start | bytes 3833864 | tf_op jit(solution)/shard_map/ppermute | solution.py:355
  56.6 0.4 collective-permute-start.6
  57.0 0.1 pad_maximum_fusion
  57.1 0.1 collective-permute-start.7
  57.2 4.1 %collective-permute-start.4 = (bf16[512,384]{1,0:T(8,128)(2,1)S(1)}, bf16[512,384]{1,0:T(8,128)(2,1)S(1)}, u32[]{:S(2)}, u32[]{:S(2)}) collective-permute-start(bf16[512,384]{1,0:T(8,128)(2,1)S(1)} %bitcast.60), channel_id=1, source_target_pairs={{0,64},{64,128},{128,192},{1,65},{65,129},{129,193},{2,66},{66,130... | collective-permute-start | bytes 1179656 | tf_op jit(solution)/shard_map/ppermute | solution.py:389
  61.3 2.1 %collective-permute-start.5 = (bf16[512,384]{1,0:T(8,128)(2,1)S(1)}, bf16[512,384]{1,0:T(8,128)(2,1)S(1)}, u32[]{:S(2)}, u32[]{:S(2)}) collective-permute-start(bf16[512,384]{1,0:T(8,128)(2,1)S(1)} %bitcast.61), channel_id=1, source_target_pairs={{64,0},{128,64},{192,128},{65,1},{129,65},{193,129},{66,2},{130,66... | collective-permute-start | bytes 1179656 | tf_op jit(solution)/shard_map/ppermute | solution.py:390
  63.4 1.7 %collective-permute-done.6.across_ref = bf16[256,384]{1,0:T(8,128)(2,1)S(1)} collective-permute-done((bf16[256,384]{1,0:T(8,128)(2,1)S(1)}, bf16[256,384]{1,0:T(8,128)(2,1)S(1)}, u32[]{:S(2)}, u32[]{:S(2)}) %collective-permute-start.6) | collective-permute-done | bytes 196640 | tf_op jit(solution)/shard_map/ppermute | solution.py:392
  65.1 7.9 %collective-permute-done.4.up_two_ref = bf16[512,384]{1,0:T(8,128)(2,1)S(1)} collective-permute-done((bf16[512,384]{1,0:T(8,128)(2,1)S(1)}, bf16[512,384]{1,0:T(8,128)(2,1)S(1)}, u32[]{:S(2)}, u32[]{:S(2)}) %collective-permute-start.4) | collective-permute-done | bytes 393248 | tf_op jit(solution)/shard_map/ppermute | solution.py:389
  73.0 1.4 %collective-permute-done.5.down_two_ref = bf16[512,384]{1,0:T(8,128)(2,1)S(1)} collective-permute-done((bf16[512,384]{1,0:T(8,128)(2,1)S(1)}, bf16[512,384]{1,0:T(8,128)(2,1)S(1)}, u32[]{:S(2)}, u32[]{:S(2)}) %collective-permute-start.5) | collective-permute-done | bytes 393248 | tf_op jit(solution)/shard_map/ppermute | solution.py:390
  74.4 0.1 slice.84
  74.5 0.1 collective-permute-start.9
  74.6 0.5 collective-permute-start.10
  75.1 0.1 collective-permute-start.11
  75.2 0.4 collective-permute-start.12
  75.6 2.7 %collective-permute-done.12.other_across_ref = bf16[256,384]{1,0:T(8,128)(2,1)S(1)} collective-permute-done((bf16[256,384]{1,0:T(8,128)(2,1)S(1)}, bf16[256,384]{1,0:T(8,128)(2,1)S(1)}, u32[]{:S(2)}, u32[]{:S(2)}) %collective-permute-start.12) | collective-permute-done | bytes 196640 | tf_op jit(solution)/shard_map/ppermute | solution.py:352
  78.4 0.6 copy-done.16
  79.0 0.1 copy-done.13
  79.1 0.1 copy-done.14
  79.2 0.3 copy-done.8
  79.5 24.8 %shard_map.56 = bf16[4,128,384]{2,1,0:T(8,128)(2,1)} custom-call(s32[3]{0:T(128)} %pad_add_fusion.place_ref, s32[4,27]{1,0:T(4,128)} %fusion.4.idx_one_ref, s32[2,27]{1,0:T(2,128)} %bitcast_select_fusion.idx_two_ref, bf16[4,464,384]{2,1,0:T(8,128)(2,1)} %copy-done, bf16[4,64,384]{2,1,0:T(8,128)(2,1)} %bitcast.68, bf16[384,384]{1,0:T(8,128)(2,1)} %copy-done.5, ...), custom_call_target="tpu_custom_call" | custom-call | flops 10569646080 | bytes 10485760 | tf_op jit(solution)/shard_map/pallas_call | solution.py:299
  104.3 12.8 %all_to_all.15.o_ref = bf16[4,128,384]{2,1,0:T(8,128)(2,1)} all-to-all(bf16[4,128,384]{2,1,0:T(8,128)(2,1)} %shard_map.56), channel_id=1, replica_groups=mesh['y'=4,'x'=4,'z'=8,'core'=2] {'x'}, dimensions={0} | all-to-all | bytes 786432 | tf_op jit(solution)/shard_map/all_to_all | solution.py:409
  117.1 1.8 %shard_map.57 = bf16[256,768]{1,0:T(8,128)(2,1)} custom-call(bf16[4,128,384]{2,1,0:T(8,128)(2,1)} %all_to_all.15.o_ref), custom_call_target="tpu_custom_call" | custom-call | bytes 1048576 | tf_op jit(solution)/shard_map/pallas_call | solution.py:410
  (54 shorter events, 0.4 us)
Async XLA Ops:
  2.7 4.4 %copy-start.7 = (s32[64,27]{0,1:T(8,128)S(1)}, s32[64,27]{0,1:T(8,128)}, u32[]{:S(2)}) copy-start(s32[64,27]{0,1:T(8,128)} %param.9) | copy-start | bytes 20740
  2.7 4.5 %copy-start.6 = (s32[256,27]{0,1:T(8,128)S(1)}, s32[256,27]{0,1:T(8,128)}, u32[]{:S(2)}) copy-start(s32[256,27]{0,1:T(8,128)} %param.8) | copy-start | bytes 82948
  2.8 23.6 %all-to-all-start = ((bf16[4,464,384]{2,1,0:T(8,128)(2,1)}), bf16[4,464,384]{2,1,0:T(8,128)(2,1)S(1)}, u32[]{:S(2)}, u32[]{:S(2)}) async-start(bf16[4,464,384]{2,1,0:T(8,128)(2,1)} %shard_map.55), calls=%async_computation | async-start | bytes 2850816 | tf_op jit(solution)/shard_map/all_to_all | solution.py:348
  26.3 1.2 %copy-start = (bf16[4,464,384]{2,1,0:T(8,128)(2,1)}, bf16[4,464,384]{2,1,0:T(8,128)(2,1)S(1)}, u32[]{:S(2)}) copy-start(bf16[4,464,384]{2,1,0:T(8,128)(2,1)S(1)} %all-to-all-done.own_ref) | copy-start | bytes 4276228
  26.5 9.7 %collective-permute-start = (bf16[256,384]{1,0:T(8,128)(2,1)S(1)}, bf16[256,384]{1,0:T(8,128)(2,1)S(1)}, u32[]{:S(2)}, u32[]{:S(2)}) collective-permute-start(bf16[256,384]{1,0:T(8,128)(2,1)S(1)} %bitcast.69), channel_id=1, source_target_pairs={{0,1},{1,0},{2,3},{3,2},{4,5},{5,4},{6,7},{7,6},{8,9},{9,8},{10,11... | collective-permute-start | bytes 589832 | tf_op jit(solution)/shard_map/ppermute | solution.py:352
  27.5 22.3 %all-to-all-start.1 = ((bf16[8,64,384]{2,1,0:T(8,128)(2,1)}), bf16[8,64,384]{2,1,0:T(8,128)(2,1)S(1)}, u32[]{:S(2)}, u32[]{:S(2)}) async-start(bf16[8,64,384]{2,1,0:T(8,128)(2,1)} %broadcast_in_dim.28), calls=%async_computation.1 | async-start | bytes 786432 | tf_op jit(solution)/shard_map/all_to_all | solution.py:369
  36.1 13.7 %copy-start.2 = (bf16[256,384]{1,0:T(8,128)(2,1)}, bf16[256,384]{1,0:T(8,128)(2,1)S(1)}, u32[]{:S(2)}) copy-start(bf16[256,384]{1,0:T(8,128)(2,1)S(1)} %collective-permute-done) | copy-start | bytes 589828
  36.2 10.6 %collective-permute-start.2 = (bf16[384,384]{1,0:T(8,128)(2,1)S(1)}, bf16[384,384]{1,0:T(8,128)(2,1)S(1)}, u32[]{:S(2)}, u32[]{:S(2)}) collective-permute-start(bf16[384,384]{1,0:T(8,128)(2,1)S(1)} %pad_maximum_fusion.2), channel_id=1, source_target_pairs={{64,0},{128,64},{192,128},{65,1},{129,65},{193,129},{66,2},{130,66... | collective-permute-start | bytes 884744 | tf_op jit(solution)/shard_map/ppermute | solution.py:373
  38.6 10.3 %collective-permute-start.1 = (bf16[384,384]{1,0:T(8,128)(2,1)S(1)}, bf16[384,384]{1,0:T(8,128)(2,1)S(1)}, u32[]{:S(2)}, u32[]{:S(2)}) collective-permute-start(bf16[384,384]{1,0:T(8,128)(2,1)S(1)} %pad_maximum_fusion.1), channel_id=1, source_target_pairs={{0,64},{64,128},{128,192},{1,65},{65,129},{129,193},{2,66},{66,130... | collective-permute-start | bytes 884744 | tf_op jit(solution)/shard_map/ppermute | solution.py:370
  46.8 6.7 %copy-start.4 = (bf16[384,384]{1,0:T(8,128)(2,1)}, bf16[384,384]{1,0:T(8,128)(2,1)S(1)}, u32[]{:S(2)}) copy-start(bf16[384,384]{1,0:T(8,128)(2,1)S(1)} %collective-permute-done.2.down_ref) | copy-start | bytes 884740
  48.9 4.5 %copy-start.5 = (bf16[384,384]{1,0:T(8,128)(2,1)}, bf16[384,384]{1,0:T(8,128)(2,1)S(1)}, u32[]{:S(2)}) copy-start(bf16[384,384]{1,0:T(8,128)(2,1)S(1)} %collective-permute-done.1.up_ref) | copy-start | bytes 884740
  49.8 15.3 %copy-start.1 = (bf16[8,64,384]{2,1,0:T(8,128)(2,1)}, bf16[8,64,384]{2,1,0:T(8,128)(2,1)S(1)}, u32[]{:S(2)}) copy-start(bf16[8,64,384]{2,1,0:T(8,128)(2,1)S(1)} %all-to-all-done.1) | copy-start | bytes 1179652
  53.4 20.9 %collective-permute-start.3 = (bf16[1664,384]{1,0:T(8,128)(2,1)}, bf16[1664,384]{1,0:T(8,128)(2,1)S(1)}, u32[]{:S(2)}, u32[]{:S(2)}) collective-permute-start(bf16[1664,384]{1,0:T(8,128)(2,1)} %bitcast_dynamic-update-slice_fusion.1), channel_id=1, source_target_pairs={{1,2},{3,4},{2,1},{5,6},{4,3},{7,8},{6,5},{9,10},{8,7},{11,12},{10... | collective-permute-start | bytes 3833864 | tf_op jit(solution)/shard_map/ppermute | solution.py:355
  56.6 8.5 %collective-permute-start.6 = (bf16[256,384]{1,0:T(8,128)(2,1)S(1)}, bf16[256,384]{1,0:T(8,128)(2,1)S(1)}, u32[]{:S(2)}, u32[]{:S(2)}) collective-permute-start(bf16[256,384]{1,0:T(8,128)(2,1)S(1)} %bitcast.77), channel_id=1, source_target_pairs={{0,128},{64,192},{128,0},{192,64},{1,129},{65,193},{129,1},{193,65... | collective-permute-start | bytes 589832 | tf_op jit(solution)/shard_map/ppermute | solution.py:392
  57.1 17.3 %collective-permute-start.7 = (bf16[640,384]{1,0:T(8,128)(2,1)S(1)}, bf16[640,384]{1,0:T(8,128)(2,1)S(1)}, u32[]{:S(2)}, u32[]{:S(2)}) collective-permute-start(bf16[640,384]{1,0:T(8,128)(2,1)S(1)} %pad_maximum_fusion), channel_id=1, source_target_pairs={{0,1},{1,0},{2,3},{3,2},{4,5},{5,4},{6,7},{7,6},{8,9},{9,8},{10,11... | collective-permute-start | bytes 1474568 | tf_op jit(solution)/shard_map/ppermute | solution.py:352
  57.2 15.8 %collective-permute-start.4 = (bf16[512,384]{1,0:T(8,128)(2,1)S(1)}, bf16[512,384]{1,0:T(8,128)(2,1)S(1)}, u32[]{:S(2)}, u32[]{:S(2)}) collective-permute-start(bf16[512,384]{1,0:T(8,128)(2,1)S(1)} %bitcast.60), channel_id=1, source_target_pairs={{0,64},{64,128},{128,192},{1,65},{65,129},{129,193},{2,66},{66,130... | collective-permute-start | bytes 1179656 | tf_op jit(solution)/shard_map/ppermute | solution.py:389
  61.3 13.1 %collective-permute-start.5 = (bf16[512,384]{1,0:T(8,128)(2,1)S(1)}, bf16[512,384]{1,0:T(8,128)(2,1)S(1)}, u32[]{:S(2)}, u32[]{:S(2)}) collective-permute-start(bf16[512,384]{1,0:T(8,128)(2,1)S(1)} %bitcast.61), channel_id=1, source_target_pairs={{64,0},{128,64},{192,128},{65,1},{129,65},{193,129},{66,2},{130,66... | collective-permute-start | bytes 1179656 | tf_op jit(solution)/shard_map/ppermute | solution.py:390
  65.1 13.2 %copy-start.15 = (bf16[256,384]{1,0:T(8,128)(2,1)}, bf16[256,384]{1,0:T(8,128)(2,1)S(1)}, u32[]{:S(2)}) copy-start(bf16[256,384]{1,0:T(8,128)(2,1)S(1)} %collective-permute-done.6.across_ref) | copy-start | bytes 589828
  65.1 9.3 %collective-permute-start.8 = (bf16[512,384]{1,0:T(8,128)(2,1)S(1)}, bf16[512,384]{1,0:T(8,128)(2,1)S(1)}, u32[]{:S(2)}, u32[]{:S(2)}) collective-permute-start(bf16[512,384]{1,0:T(8,128)(2,1)S(1)} %bitcast.62), channel_id=1, source_target_pairs={{0,1},{1,0},{2,3},{3,2},{4,5},{5,4},{6,7},{7,6},{8,9},{9,8},{10,11... | collective-permute-start | bytes 1179656 | tf_op jit(solution)/shard_map/ppermute | solution.py:352
  73.0 5.4 %copy-start.10 = (bf16[512,384]{1,0:T(8,128)(2,1)}, bf16[512,384]{1,0:T(8,128)(2,1)S(1)}, u32[]{:S(2)}) copy-start(bf16[512,384]{1,0:T(8,128)(2,1)S(1)} %collective-permute-done.4.up_two_ref) | copy-start | bytes 1179652
  74.4 4.0 %copy-start.11 = (bf16[512,384]{1,0:T(8,128)(2,1)}, bf16[512,384]{1,0:T(8,128)(2,1)S(1)}, u32[]{:S(2)}) copy-start(bf16[512,384]{1,0:T(8,128)(2,1)S(1)} %collective-permute-done.5.down_two_ref) | copy-start | bytes 1179652
  74.4 4.0 %copy-start.12 = (bf16[512,384]{1,0:T(8,128)(2,1)}, bf16[512,384]{1,0:T(8,128)(2,1)S(1)}, u32[]{:S(2)}) copy-start(bf16[512,384]{1,0:T(8,128)(2,1)S(1)} %collective-permute-done.8.other_row_ref) | copy-start | bytes 1179652
  74.4 4.0 %copy-start.9 = (bf16[640,384]{1,0:T(8,128)(2,1)}, bf16[640,384]{1,0:T(8,128)(2,1)S(1)}, u32[]{:S(2)}) copy-start(bf16[640,384]{1,0:T(8,128)(2,1)S(1)} %collective-permute-done.7.inner_ref) | copy-start | bytes 1474564
  74.4 4.0 %copy-start.3 = (bf16[1664,384]{1,0:T(8,128)(2,1)}, bf16[1664,384]{1,0:T(8,128)(2,1)S(1)}, u32[]{:S(2)}) copy-start(bf16[1664,384]{1,0:T(8,128)(2,1)S(1)} %collective-permute-done.3.side_ref) | copy-start | bytes 3833860
  74.5 3.8 %collective-permute-start.9 = (bf16[1024,384]{1,0:T(8,128)(2,1)S(1)}, bf16[1024,384]{1,0:T(8,128)(2,1)S(1)}, u32[]{:S(2)}, u32[]{:S(2)}) collective-permute-start(bf16[1024,384]{1,0:T(8,128)(2,1)S(1)} %slice.84), channel_id=1, source_target_pairs={{0,1},{1,0},{2,3},{3,2},{4,5},{5,4},{6,7},{7,6},{8,9},{9,8},{10,11... | collective-permute-start | bytes 2359304 | tf_op jit(solution)/shard_map/ppermute | solution.py:352
  74.6 3.7 %collective-permute-start.10 = (bf16[512,384]{1,0:T(8,128)(2,1)S(1)}, bf16[512,384]{1,0:T(8,128)(2,1)S(1)}, u32[]{:S(2)}, u32[]{:S(2)}) collective-permute-start(bf16[512,384]{1,0:T(8,128)(2,1)S(1)} %collective-permute-done.4.up_two_ref), channel_id=1, source_target_pairs={{0,1},{1,0},{2,3},{3,2},{4,5},{5,4},{6,7},{7,6},{8,9},{9,8},{10,11... | collective-permute-start | bytes 1179656 | tf_op jit(solution)/shard_map/ppermute | solution.py:352
  75.1 3.2 %collective-permute-start.11 = (bf16[512,384]{1,0:T(8,128)(2,1)S(1)}, bf16[512,384]{1,0:T(8,128)(2,1)S(1)}, u32[]{:S(2)}, u32[]{:S(2)}) collective-permute-start(bf16[512,384]{1,0:T(8,128)(2,1)S(1)} %collective-permute-done.5.down_two_ref), channel_id=1, source_target_pairs={{0,1},{1,0},{2,3},{3,2},{4,5},{5,4},{6,7},{7,6},{8,9},{9,8},{10,11... | collective-permute-start | bytes 1179656 | tf_op jit(solution)/shard_map/ppermute | solution.py:352
  75.2 3.1 %collective-permute-start.12 = (bf16[256,384]{1,0:T(8,128)(2,1)S(1)}, bf16[256,384]{1,0:T(8,128)(2,1)S(1)}, u32[]{:S(2)}, u32[]{:S(2)}) collective-permute-start(bf16[256,384]{1,0:T(8,128)(2,1)S(1)} %collective-permute-done.6.across_ref), channel_id=1, source_target_pairs={{0,1},{1,0},{2,3},{3,2},{4,5},{5,4},{6,7},{7,6},{8,9},{9,8},{10,11... | collective-permute-start | bytes 589832 | tf_op jit(solution)/shard_map/ppermute | solution.py:352
  78.3 0.7 copy-start.16
  78.3 0.8 copy-start.13
  78.3 0.9 copy-start.14
  78.3 1.2 copy-start.8

commit v5 on v4

--- a/solution.py
+++ b/solution.py
@@ -81,10 +81,11 @@
 
 def attend_kernel(
     place_ref, idx_one_ref, idx_two_ref,
-    own_ref, other_ref, up_ref, down_ref, inner_ref, side_ref, other_side_ref,
+    own_ref, other_ref, up_ref, down_ref,
+    inner_ref, outer_ref, side_ref, other_outer_ref, other_side_ref,
     row_ref, up_two_ref, down_two_ref, across_ref,
     other_row_ref, other_up_ref, other_down_ref, other_across_ref,
-    out_ref, one_ref, two_ref, tall_ref, kv_ref, kv_next_ref, s_pair_ref, s_third_ref,
+    out_ref, one_ref, two_ref, tall_ref, strip_ref, kv_ref, kv_next_ref, s_pair_ref, s_third_ref,
 ):
     y = place_ref[0]
     z = place_ref[1]
@@ -94,6 +95,10 @@
     tall_ref[1152:1280] = down_ref[256:384]
     for xs in range(4):
         tall_ref[128 + 256 * xs:384 + 256 * xs] = own_ref[xs, FINE:QUERY]
+
+    strip_ref[0:64] = side_ref[512:576]
+    strip_ref[64:576] = outer_ref[512:1024]
+    strip_ref[576:640] = side_ref[576:640]
 
     def quarter(xs, kk):
         return pl.ds(pl.multiple_of(32 * (xs & 1) + 16 * kk, 16), 16)
@@ -111,16 +116,16 @@
             at = 128 * m + 64 * i
             put_one(i, 2 + kk, up_ref[at:at + 64])
             put_one(6 + i, 2 + kk, down_ref[at:at + 64])
-    for side, one_side in ((core, side_ref), (1 - core, other_side_ref)):
+    for side, middle, ends in ((core, outer_ref, side_ref), (1 - core, other_outer_ref, other_side_ref)):
         for m in range(2):
             kk = 1 - side if m == 0 else side
             for i in range(4):
                 at = 256 * m + 64 * i
-                put_one(2 + i, 4 * side + kk, one_side[at:at + 64])
+                put_one(2 + i, 4 * side + kk, middle[at:at + 64])
             for i in range(2):
-                at = 512 + 128 * m + 64 * i
-                put_one(i, 4 * side + kk, one_side[at:at + 64])
-                put_one(6 + i, 4 * side + kk, one_side[at + 256:at + 320])
+                at = 128 * m + 64 * i
+                put_one(i, 4 * side + kk, ends[at:at + 64])
+                put_one(6 + i, 4 * side + kk, ends[at + 256:at + 320])
     end = jnp.where(y >= 2, 2 * y - 1, 2 * y + 6)
     for kk, row, ups, downs, across in (
         (core, row_ref, up_two_ref, down_two_ref, across_ref),
@@ -195,7 +200,7 @@
         steps = [near(tall_ref, 0, 256, first, 128, 0, 4, 8) for first in range(0, 512, 128)]
         for first in (0, 128):
             steps.append(near(inner_ref, 0, 128, first, 128, 512, 3, inner_col))
-            steps.append(near(side_ref, 1024, 128, first, 128, 768, 3, 24 - inner_col))
+            steps.append(near(strip_ref, 0, 128, first, 128, 768, 3, 24 - inner_col))
         for j in range(27):
             steps += [far(j, 0), far(j, 1)]
         return steps
@@ -299,11 +304,12 @@
     return call(
         attend_kernel,
         shape(4, 128, 384),
-        [SMEM] * 3 + [VMEM] * 15,
+        [SMEM] * 3 + [VMEM] * 17,
         scratch=[
             pltpu.VMEM((48, 64, 384), BF),
             pltpu.VMEM((96, 64, 384), BF),
             pltpu.VMEM((1280, 384), BF),
+            pltpu.VMEM((640, 384), BF),
             pltpu.VMEM((KEYS, 512), BF),
             pltpu.VMEM((KEYS, 512), BF),
             pltpu.VMEM((512, KEYS), F32),
@@ -373,17 +379,14 @@
     from_down = lax.ppermute(
         jnp.concatenate([t[0:2].reshape(128, 384) for t in ones] + [fine[0:128]], axis=0), "y", down
     )
-    row_two, from_up, from_down = lax.optimization_barrier((row_two, from_up, from_down))
+    middle_inner, middle_outer = strips(fine)
+    outer = over_z(jnp.concatenate([t.reshape(256, 384) for t in ones] + [middle_outer], axis=0))
+    row_two, from_up, from_down, outer = lax.optimization_barrier((row_two, from_up, from_down, outer))
 
     top_inner, top_outer = strips(from_up[256:384])
-    middle_inner, middle_outer = strips(fine)
     bottom_inner, bottom_outer = strips(from_down[256:384])
     side = over_z(
-        jnp.concatenate(
-            [t.reshape(256, 384) for t in ones]
-            + [from_up[0:256], from_down[0:256], top_outer, middle_outer, bottom_outer],
-            axis=0,
-        )
+        jnp.concatenate([from_up[0:256], from_down[0:256], top_outer, bottom_outer], axis=0)
     )
     inner = over_core(jnp.concatenate([top_inner, middle_inner, bottom_inner], axis=0))
     up_two = lax.ppermute(row_two.reshape(512, 384), "y", up)
@@ -399,11 +402,13 @@
         (side, up_two, down_two, across_two, inner, other_row)
     )
 
-    other_side = over_core(side[0:1024])
+    other_outer = over_core(outer[0:512])
+    other_side = over_core(side[0:512])
     others = [over_core(t) for t in (up_two, down_two, across_two)]
 
     out = attend_call(
-        place, idx_one, idx_two, rf, other, from_up, from_down, inner, side, other_side,
+        place, idx_one, idx_two, rf, other, from_up, from_down,
+        inner, outer, side, other_outer, other_side,
         row_two.reshape(512, 384), up_two, down_two, across_two, other_row, *others,
     )
     back = lax.all_to_all(out, "x", 0, 0, tiled=True)

time: 121 us -> 122 us (level)
  starting transfers between devices: 29.8 us -> 33.6 us
  other arithmetic: 4.22 us -> 2.17 us
  local copies, waits for them, and re-layouts: 5.7 us -> 3.76 us
  waiting for transfers between devices: 36.7 us -> 38.3 us
    ppermute x1, waiting for transfers between devices: 2.12 us -> 5.33 us  [body(): lax.ppermute(jnp.concatenate([t[2:4].reshape(128, 384) for t in ones] + [...]
    ppermute x1, waiting for transfers between devices: 7.89 us -> 4.75 us  [body(): up_two = lax.ppermute(row_two.reshape(512, 384), 'y', up)]
    unnamed x39 -> x37, local copies, waits for them, and re-layouts: 4.12 us -> 1.1 us
    ppermute x1, waiting for transfers between devices: 1.38 us -> 3.92 us  [body(): down_two = lax.ppermute(row_two.reshape(512, 384), 'y', down)]
    ppermute x1, starting transfers between devices: 2.15 us -> 4.31 us  [body(): down_two = lax.ppermute(row_two.reshape(512, 384), 'y', down)]
    ppermute x1 -> x2, starting transfers between devices: 2.99 us -> 4.72 us  [over_z(): return lax.ppermute(array, ('z', 'core'), z_perm(step))]
    unnamed x2 -> x0, other arithmetic: 1.49 us -> none
    ppermute x7 -> x8, waiting for transfers between devices: 2.68 us -> 2.12 us  [over_core(): return lax.ppermute(array, 'core', [(0, 1), (1, 0)])]
  transfers between devices with their start and end apart: 15 -> 17, of which waited for: 8 -> 8; matrix products, arithmetic and copies ran while one was open for 4% -> 4% of each run, Pallas kernels for 0% -> 0%
where the time goes in v5:
time: 122 us; the launch traced here: 120 us
  waiting for transfers between devices  38.3 us (31%)
  starting transfers between devices  33.6 us (28%)
  Pallas kernels  29.3 us (24%)
  blocking collectives  12.8 us (10%)
  local copies, waits for them, and re-layouts  3.76 us (3%)
  other arithmetic  2.17 us (2%)
    pallas_call x1, Pallas kernels, attend_call(): call(attend_kernel, shape(4, 128, 384), [SMEM] * 3 + [VMEM] * 17, scratch...  24.7 us
    all_to_all x1, waiting for transfers between devices, body(): rf = lax.all_to_all(packed, 'x', 0, 0, tiled=True)  16.9 us
    all_to_all x1, blocking collectives, body(): back = lax.all_to_all(out, 'x', 0, 0, tiled=True)  12.8 us
    all_to_all x1, starting transfers between devices, body(): lax.all_to_all(jnp.broadcast_to(two, (8, 64, 384)), 'z', 0, 0, tiled=True)  8.57 us
    ppermute x1, waiting for transfers between devices, body(): lax.ppermute(jnp.concatenate([t[2:4].reshape(128, 384) for t in ones] + [...  5.33 us
    ppermute x1, waiting for transfers between devices, body(): up_two = lax.ppermute(row_two.reshape(512, 384), 'y', up)  4.75 us
    ppermute x2, starting transfers between devices, over_z(): return lax.ppermute(array, ('z', 'core'), z_perm(step))  4.72 us
    all_to_all x1, starting transfers between devices, body(): rf = lax.all_to_all(packed, 'x', 0, 0, tiled=True)  4.42 us
  transfers between devices with their start and end apart: 17, of which 8 were waited for; matrix products, arithmetic and copies ran while one was open for 4% of the time, Pallas kernels for 0%

profile of v5, /device:TPU:48, one launch (start us, length us, event | category | flops | bytes accessed | tf_op | source)
XLA Modules:
  0.0 120.4 jit_solution(11013338593647535942)
XLA Ops:
  0.0 2.8 %shard_map.55 = bf16[4,464,384]{2,1,0:T(8,128)(2,1)} custom-call(bf16[256,768]{1,0:T(8,128)(2,1)} %bitcast.66, bf16[256,768]{1,0:T(8,128)(2,1)} %bitcast.67, bf16[256,768]{1,0:T(8,128)(2,1)} %bitcast.68), custom_call_target="tpu_custom_call" | custom-call | bytes 4194304 | tf_op jit(solution)/shard_map/pallas_call | solution.py:351
  2.8 4.4 %all-to-all-start = ((bf16[4,464,384]{2,1,0:T(8,128)(2,1)}), bf16[4,464,384]{2,1,0:T(8,128)(2,1)S(1)}, u32[]{:S(2)}, u32[]{:S(2)}) async-start(bf16[4,464,384]{2,1,0:T(8,128)(2,1)} %shard_map.55), calls=%async_computation | async-start | bytes 2850816 | tf_op jit(solution)/shard_map/all_to_all | solution.py:354
  7.2 0.1 copy.11
  7.3 0.1 reshape.110
  7.4 0.1 constant_dynamic-slice_fusion.2
  7.5 0.1 copy.10
  7.6 0.6 pad_add_fusion.place_ref
  8.2 0.6 bitcast_select_fusion.idx_two_ref
  8.8 0.6 fusion.4.idx_one_ref
  9.4 16.9 %all-to-all-done.own_ref = bf16[4,464,384]{2,1,0:T(8,128)(2,1)S(1)} async-done(((bf16[4,464,384]{2,1,0:T(8,128)(2,1)}), bf16[4,464,384]{2,1,0:T(8,128)(2,1)S(1)}, u32[]{:S(2)}, u32[]{:S(2)}) %all-to-all-start) | async-done | bytes 1425440 | tf_op jit(solution)/shard_map/all_to_all | solution.py:354
  26.4 0.1 slice.72
  26.5 0.1 collective-permute-start
  26.6 1.0 broadcast_in_dim.28
  27.5 8.6 %all-to-all-start.1 = ((bf16[8,64,384]{2,1,0:T(8,128)(2,1)}), bf16[8,64,384]{2,1,0:T(8,128)(2,1)S(1)}, u32[]{:S(2)}, u32[]{:S(2)}) async-start(bf16[8,64,384]{2,1,0:T(8,128)(2,1)} %broadcast_in_dim.28), calls=%async_computation.1 | async-start | bytes 786432 | tf_op jit(solution)/shard_map/all_to_all | solution.py:375
  36.1 0.1 select_bitcast_fusion
  36.2 0.0 collective-permute-done
  36.3 0.1 pad_maximum_fusion
  36.3 1.9 %collective-permute-start.3 = (bf16[1024,384]{1,0:T(8,128)(2,1)S(1)}, bf16[1024,384]{1,0:T(8,128)(2,1)}, u32[]{:S(2)}, u32[]{:S(2)}) collective-permute-start(bf16[1024,384]{1,0:T(8,128)(2,1)S(1)} %pad_maximum_fusion), channel_id=1, source_target_pairs={{1,2},{3,4},{2,1},{5,6},{4,3},{7,8},{6,5},{9,10},{8,7},{11,12},{10... | collective-permute-start | bytes 2359304 | tf_op jit(solution)/shard_map/ppermute | solution.py:361
  38.4 3.2 %collective-permute-start.1 = (bf16[384,384]{1,0:T(8,128)(2,1)S(1)}, bf16[384,384]{1,0:T(8,128)(2,1)S(1)}, u32[]{:S(2)}, u32[]{:S(2)}) collective-permute-start(bf16[384,384]{1,0:T(8,128)(2,1)S(1)} %pad_maximum_fusion.3), channel_id=1, source_target_pairs={{0,64},{64,128},{128,192},{1,65},{65,129},{129,193},{2,66},{66,130... | collective-permute-start | bytes 884744 | tf_op jit(solution)/shard_map/ppermute | solution.py:376
  41.6 2.7 %collective-permute-start.2 = (bf16[384,384]{1,0:T(8,128)(2,1)S(1)}, bf16[384,384]{1,0:T(8,128)(2,1)S(1)}, u32[]{:S(2)}, u32[]{:S(2)}) collective-permute-start(bf16[384,384]{1,0:T(8,128)(2,1)S(1)} %pad_maximum_fusion.4), channel_id=1, source_target_pairs={{64,0},{128,64},{192,128},{65,1},{129,65},{193,129},{66,2},{130,66... | collective-permute-start | bytes 884744 | tf_op jit(solution)/shard_map/ppermute | solution.py:379
  44.3 5.3 %collective-permute-done.1.up_ref = bf16[384,384]{1,0:T(8,128)(2,1)S(1)} collective-permute-done((bf16[384,384]{1,0:T(8,128)(2,1)S(1)}, bf16[384,384]{1,0:T(8,128)(2,1)S(1)}, u32[]{:S(2)}, u32[]{:S(2)}) %collective-permute-start.1) | collective-permute-done | bytes 294944 | tf_op jit(solution)/shard_map/ppermute | solution.py:376
  49.6 3.5 %collective-permute-done.2.down_ref = bf16[384,384]{1,0:T(8,128)(2,1)S(1)} collective-permute-done((bf16[384,384]{1,0:T(8,128)(2,1)S(1)}, bf16[384,384]{1,0:T(8,128)(2,1)S(1)}, u32[]{:S(2)}, u32[]{:S(2)}) %collective-permute-start.2) | collective-permute-done | bytes 294944 | tf_op jit(solution)/shard_map/ppermute | solution.py:379
  53.1 1.1 collective-permute-done.3.outer_ref
  54.3 0.4 collective-permute-start.7
  54.7 0.1 pad_maximum_fusion.1
  54.8 2.8 %collective-permute-start.4 = (bf16[640,384]{1,0:T(8,128)(2,1)S(1)}, bf16[640,384]{1,0:T(8,128)(2,1)S(1)}, u32[]{:S(2)}, u32[]{:S(2)}) collective-permute-start(bf16[640,384]{1,0:T(8,128)(2,1)S(1)} %pad_maximum_fusion.1), channel_id=1, source_target_pairs={{1,2},{3,4},{2,1},{5,6},{4,3},{7,8},{6,5},{9,10},{8,7},{11,12},{10... | collective-permute-start | bytes 1474568 | tf_op jit(solution)/shard_map/ppermute | solution.py:361
  57.6 0.1 pad_maximum_fusion.2
  57.7 0.8 collective-permute-start.8
  58.5 0.1 collective-permute-start.9
  58.6 4.3 %collective-permute-start.6 = (bf16[512,384]{1,0:T(8,128)(2,1)S(1)}, bf16[512,384]{1,0:T(8,128)(2,1)S(1)}, u32[]{:S(2)}, u32[]{:S(2)}) collective-permute-start(bf16[512,384]{1,0:T(8,128)(2,1)S(1)} %bitcast.60), channel_id=1, source_target_pairs={{64,0},{128,64},{192,128},{65,1},{129,65},{193,129},{66,2},{130,66... | collective-permute-start | bytes 1179656 | tf_op jit(solution)/shard_map/ppermute | solution.py:393
  62.9 0.7 collective-permute-done.7.across_ref
  63.6 3.2 %collective-permute-start.5 = (bf16[512,384]{1,0:T(8,128)(2,1)S(1)}, bf16[512,384]{1,0:T(8,128)(2,1)S(1)}, u32[]{:S(2)}, u32[]{:S(2)}) collective-permute-start(bf16[512,384]{1,0:T(8,128)(2,1)S(1)} %bitcast.61), channel_id=1, source_target_pairs={{0,64},{64,128},{128,192},{1,65},{65,129},{129,193},{2,66},{66,130... | collective-permute-start | bytes 1179656 | tf_op jit(solution)/shard_map/ppermute | solution.py:392
  66.8 1.0 slice.87
  67.9 0.1 collective-permute-start.10
  68.0 3.9 %collective-permute-done.6.down_two_ref = bf16[512,384]{1,0:T(8,128)(2,1)S(1)} collective-permute-done((bf16[512,384]{1,0:T(8,128)(2,1)S(1)}, bf16[512,384]{1,0:T(8,128)(2,1)S(1)}, u32[]{:S(2)}, u32[]{:S(2)}) %collective-permute-start.6) | collective-permute-done | bytes 393248 | tf_op jit(solution)/shard_map/ppermute | solution.py:393
  71.9 4.7 %collective-permute-done.5.up_two_ref = bf16[512,384]{1,0:T(8,128)(2,1)S(1)} collective-permute-done((bf16[512,384]{1,0:T(8,128)(2,1)S(1)}, bf16[512,384]{1,0:T(8,128)(2,1)S(1)}, u32[]{:S(2)}, u32[]{:S(2)}) %collective-permute-start.5) | collective-permute-done | bytes 393248 | tf_op jit(solution)/shard_map/ppermute | solution.py:392
  76.7 0.1 collective-permute-start.11
  76.8 0.5 collective-permute-start.12
  77.3 0.1 collective-permute-start.13
  77.4 0.4 collective-permute-start.14
  77.8 2.1 %collective-permute-done.14.other_across_ref = bf16[256,384]{1,0:T(8,128)(2,1)S(1)} collective-permute-done((bf16[256,384]{1,0:T(8,128)(2,1)S(1)}, bf16[256,384]{1,0:T(8,128)(2,1)S(1)}, u32[]{:S(2)}, u32[]{:S(2)}) %collective-permute-start.14) | collective-permute-done | bytes 196640 | tf_op jit(solution)/shard_map/ppermute | solution.py:358
  80.0 0.6 copy-done.17
  80.6 0.1 copy-done.13
  80.7 0.1 copy-done.14
  80.9 0.1 copy-done.15
  81.0 24.7 %shard_map.56 = bf16[4,128,384]{2,1,0:T(8,128)(2,1)} custom-call(s32[3]{0:T(128)} %pad_add_fusion.place_ref, s32[4,27]{1,0:T(4,128)} %fusion.4.idx_one_ref, s32[2,27]{1,0:T(2,128)} %bitcast_select_fusion.idx_two_ref, bf16[4,464,384]{2,1,0:T(8,128)(2,1)} %copy-done, bf16[4,64,384]{2,1,0:T(8,128)(2,1)} %bitcast.63, bf16[384,384]{1,0:T(8,128)(2,1)} %copy-done.4, ...), custom_call_target="tpu_custom_call" | custom-call | flops 10569646080 | bytes 10485760 | tf_op jit(solution)/shard_map/pallas_call | solution.py:304
  105.7 12.8 %all_to_all.15.o_ref = bf16[4,128,384]{2,1,0:T(8,128)(2,1)} all-to-all(bf16[4,128,384]{2,1,0:T(8,128)(2,1)} %shard_map.56), channel_id=1, replica_groups=mesh['y'=4,'x'=4,'z'=8,'core'=2] {'x'}, dimensions={0} | all-to-all | bytes 786432 | tf_op jit(solution)/shard_map/all_to_all | solution.py:414
  118.5 1.8 %shard_map.57 = bf16[256,768]{1,0:T(8,128)(2,1)} custom-call(bf16[4,128,384]{2,1,0:T(8,128)(2,1)} %all_to_all.15.o_ref), custom_call_target="tpu_custom_call" | custom-call | bytes 1048576 | tf_op jit(solution)/shard_map/pallas_call | solution.py:415
  (58 shorter events, 0.4 us)
Async XLA Ops:
  2.8 4.4 %copy-start.7 = (s32[64,27]{0,1:T(8,128)S(1)}, s32[64,27]{0,1:T(8,128)}, u32[]{:S(2)}) copy-start(s32[64,27]{0,1:T(8,128)} %param.9) | copy-start | bytes 20740
  2.8 4.5 %copy-start.6 = (s32[256,27]{0,1:T(8,128)S(1)}, s32[256,27]{0,1:T(8,128)}, u32[]{:S(2)}) copy-start(s32[256,27]{0,1:T(8,128)} %param.8) | copy-start | bytes 82948
  2.8 23.6 %all-to-all-start = ((bf16[4,464,384]{2,1,0:T(8,128)(2,1)}), bf16[4,464,384]{2,1,0:T(8,128)(2,1)S(1)}, u32[]{:S(2)}, u32[]{:S(2)}) async-start(bf16[4,464,384]{2,1,0:T(8,128)(2,1)} %shard_map.55), calls=%async_computation | async-start | bytes 2850816 | tf_op jit(solution)/shard_map/all_to_all | solution.py:354
  26.3 9.9 %copy-start = (bf16[4,464,384]{2,1,0:T(8,128)(2,1)}, bf16[4,464,384]{2,1,0:T(8,128)(2,1)S(1)}, u32[]{:S(2)}) copy-start(bf16[4,464,384]{2,1,0:T(8,128)(2,1)S(1)} %all-to-all-done.own_ref) | copy-start | bytes 4276228
  26.5 9.8 %collective-permute-start = (bf16[256,384]{1,0:T(8,128)(2,1)S(1)}, bf16[256,384]{1,0:T(8,128)(2,1)S(1)}, u32[]{:S(2)}, u32[]{:S(2)}) collective-permute-start(bf16[256,384]{1,0:T(8,128)(2,1)S(1)} %bitcast.64), channel_id=1, source_target_pairs={{0,1},{1,0},{2,3},{3,2},{4,5},{5,4},{6,7},{7,6},{8,9},{9,8},{10,11... | collective-permute-start | bytes 589832 | tf_op jit(solution)/shard_map/ppermute | solution.py:358
  27.5 25.5 %all-to-all-start.1 = ((bf16[8,64,384]{2,1,0:T(8,128)(2,1)}), bf16[8,64,384]{2,1,0:T(8,128)(2,1)S(1)}, u32[]{:S(2)}, u32[]{:S(2)}) async-start(bf16[8,64,384]{2,1,0:T(8,128)(2,1)} %broadcast_in_dim.28), calls=%async_computation.1 | async-start | bytes 786432 | tf_op jit(solution)/shard_map/all_to_all | solution.py:375
  36.2 2.1 %copy-start.2 = (bf16[256,384]{1,0:T(8,128)(2,1)}, bf16[256,384]{1,0:T(8,128)(2,1)S(1)}, u32[]{:S(2)}) copy-start(bf16[256,384]{1,0:T(8,128)(2,1)S(1)} %collective-permute-done) | copy-start | bytes 589828
  36.3 17.8 %collective-permute-start.3 = (bf16[1024,384]{1,0:T(8,128)(2,1)S(1)}, bf16[1024,384]{1,0:T(8,128)(2,1)}, u32[]{:S(2)}, u32[]{:S(2)}) collective-permute-start(bf16[1024,384]{1,0:T(8,128)(2,1)S(1)} %pad_maximum_fusion), channel_id=1, source_target_pairs={{1,2},{3,4},{2,1},{5,6},{4,3},{7,8},{6,5},{9,10},{8,7},{11,12},{10... | collective-permute-start | bytes 2359304 | tf_op jit(solution)/shard_map/ppermute | solution.py:361
  38.4 11.2 %collective-permute-start.1 = (bf16[384,384]{1,0:T(8,128)(2,1)S(1)}, bf16[384,384]{1,0:T(8,128)(2,1)S(1)}, u32[]{:S(2)}, u32[]{:S(2)}) collective-permute-start(bf16[384,384]{1,0:T(8,128)(2,1)S(1)} %pad_maximum_fusion.3), channel_id=1, source_target_pairs={{0,64},{64,128},{128,192},{1,65},{65,129},{129,193},{2,66},{66,130... | collective-permute-start | bytes 884744 | tf_op jit(solution)/shard_map/ppermute | solution.py:376
  41.6 11.5 %collective-permute-start.2 = (bf16[384,384]{1,0:T(8,128)(2,1)S(1)}, bf16[384,384]{1,0:T(8,128)(2,1)S(1)}, u32[]{:S(2)}, u32[]{:S(2)}) collective-permute-start(bf16[384,384]{1,0:T(8,128)(2,1)S(1)} %pad_maximum_fusion.4), channel_id=1, source_target_pairs={{64,0},{128,64},{192,128},{65,1},{129,65},{193,129},{66,2},{130,66... | collective-permute-start | bytes 884744 | tf_op jit(solution)/shard_map/ppermute | solution.py:379
  49.6 5.2 %copy-start.4 = (bf16[384,384]{1,0:T(8,128)(2,1)}, bf16[384,384]{1,0:T(8,128)(2,1)S(1)}, u32[]{:S(2)}) copy-start(bf16[384,384]{1,0:T(8,128)(2,1)S(1)} %collective-permute-done.1.up_ref) | copy-start | bytes 884740
  53.1 1.7 %copy-start.5 = (bf16[384,384]{1,0:T(8,128)(2,1)}, bf16[384,384]{1,0:T(8,128)(2,1)S(1)}, u32[]{:S(2)}) copy-start(bf16[384,384]{1,0:T(8,128)(2,1)S(1)} %collective-permute-done.2.down_ref) | copy-start | bytes 884740
  53.1 10.5 %copy-start.1 = (bf16[8,64,384]{2,1,0:T(8,128)(2,1)}, bf16[8,64,384]{2,1,0:T(8,128)(2,1)S(1)}, u32[]{:S(2)}) copy-start(bf16[8,64,384]{2,1,0:T(8,128)(2,1)S(1)} %all-to-all-done.1) | copy-start | bytes 1179652
  54.3 9.3 %collective-permute-start.7 = (bf16[256,384]{1,0:T(8,128)(2,1)S(1)}, bf16[256,384]{1,0:T(8,128)(2,1)S(1)}, u32[]{:S(2)}, u32[]{:S(2)}) collective-permute-start(bf16[256,384]{1,0:T(8,128)(2,1)S(1)} %bitcast.74), channel_id=1, source_target_pairs={{0,128},{64,192},{128,0},{192,64},{1,129},{65,193},{129,1},{193,65... | collective-permute-start | bytes 589832 | tf_op jit(solution)/shard_map/ppermute | solution.py:395
  54.8 21.8 %collective-permute-start.4 = (bf16[640,384]{1,0:T(8,128)(2,1)S(1)}, bf16[640,384]{1,0:T(8,128)(2,1)S(1)}, u32[]{:S(2)}, u32[]{:S(2)}) collective-permute-start(bf16[640,384]{1,0:T(8,128)(2,1)S(1)} %pad_maximum_fusion.1), channel_id=1, source_target_pairs={{1,2},{3,4},{2,1},{5,6},{4,3},{7,8},{6,5},{9,10},{8,7},{11,12},{10... | collective-permute-start | bytes 1474568 | tf_op jit(solution)/shard_map/ppermute | solution.py:361
  57.7 19.0 %collective-permute-start.8 = (bf16[640,384]{1,0:T(8,128)(2,1)S(1)}, bf16[640,384]{1,0:T(8,128)(2,1)S(1)}, u32[]{:S(2)}, u32[]{:S(2)}) collective-permute-start(bf16[640,384]{1,0:T(8,128)(2,1)S(1)} %pad_maximum_fusion.2), channel_id=1, source_target_pairs={{0,1},{1,0},{2,3},{3,2},{4,5},{5,4},{6,7},{7,6},{8,9},{9,8},{10,11... | collective-permute-start | bytes 1474568 | tf_op jit(solution)/shard_map/ppermute | solution.py:358
  58.5 9.4 %collective-permute-start.9 = (bf16[512,384]{1,0:T(8,128)(2,1)S(1)}, bf16[512,384]{1,0:T(8,128)(2,1)S(1)}, u32[]{:S(2)}, u32[]{:S(2)}) collective-permute-start(bf16[512,384]{1,0:T(8,128)(2,1)S(1)} %bitcast.59), channel_id=1, source_target_pairs={{0,1},{1,0},{2,3},{3,2},{4,5},{5,4},{6,7},{7,6},{8,9},{9,8},{10,11... | collective-permute-start | bytes 1179656 | tf_op jit(solution)/shard_map/ppermute | solution.py:358
  58.6 13.3 %collective-permute-start.6 = (bf16[512,384]{1,0:T(8,128)(2,1)S(1)}, bf16[512,384]{1,0:T(8,128)(2,1)S(1)}, u32[]{:S(2)}, u32[]{:S(2)}) collective-permute-start(bf16[512,384]{1,0:T(8,128)(2,1)S(1)} %bitcast.60), channel_id=1, source_target_pairs={{64,0},{128,64},{192,128},{65,1},{129,65},{193,129},{66,2},{130,66... | collective-permute-start | bytes 1179656 | tf_op jit(solution)/shard_map/ppermute | solution.py:393
  63.6 16.4 %copy-start.16 = (bf16[256,384]{1,0:T(8,128)(2,1)}, bf16[256,384]{1,0:T(8,128)(2,1)S(1)}, u32[]{:S(2)}) copy-start(bf16[256,384]{1,0:T(8,128)(2,1)S(1)} %collective-permute-done.7.across_ref) | copy-start | bytes 589828
  63.6 13.0 %collective-permute-start.5 = (bf16[512,384]{1,0:T(8,128)(2,1)S(1)}, bf16[512,384]{1,0:T(8,128)(2,1)S(1)}, u32[]{:S(2)}, u32[]{:S(2)}) collective-permute-start(bf16[512,384]{1,0:T(8,128)(2,1)S(1)} %bitcast.61), channel_id=1, source_target_pairs={{0,64},{64,128},{128,192},{1,65},{65,129},{129,193},{2,66},{66,130... | collective-permute-start | bytes 1179656 | tf_op jit(solution)/shard_map/ppermute | solution.py:392
  67.9 12.1 %copy-start.9 = (bf16[512,384]{1,0:T(8,128)(2,1)}, bf16[512,384]{1,0:T(8,128)(2,1)S(1)}, u32[]{:S(2)}) copy-start(bf16[512,384]{1,0:T(8,128)(2,1)S(1)} %collective-permute-done.9.other_row_ref) | copy-start | bytes 1179652
  67.9 10.0 %collective-permute-start.10 = (bf16[512,384]{1,0:T(8,128)(2,1)S(1)}, bf16[512,384]{1,0:T(8,128)(2,1)S(1)}, u32[]{:S(2)}, u32[]{:S(2)}) collective-permute-start(bf16[512,384]{1,0:T(8,128)(2,1)S(1)} %slice.87), channel_id=1, source_target_pairs={{0,1},{1,0},{2,3},{3,2},{4,5},{5,4},{6,7},{7,6},{8,9},{9,8},{10,11... | collective-permute-start | bytes 1179656 | tf_op jit(solution)/shard_map/ppermute | solution.py:358
  71.9 8.1 %copy-start.10 = (bf16[512,384]{1,0:T(8,128)(2,1)}, bf16[512,384]{1,0:T(8,128)(2,1)S(1)}, u32[]{:S(2)}) copy-start(bf16[512,384]{1,0:T(8,128)(2,1)S(1)} %collective-permute-done.6.down_two_ref) | copy-start | bytes 1179652
  76.6 3.4 %copy-start.11 = (bf16[512,384]{1,0:T(8,128)(2,1)}, bf16[512,384]{1,0:T(8,128)(2,1)S(1)}, u32[]{:S(2)}) copy-start(bf16[512,384]{1,0:T(8,128)(2,1)S(1)} %collective-permute-done.5.up_two_ref) | copy-start | bytes 1179652
  76.6 3.4 %copy-start.3 = (bf16[640,384]{1,0:T(8,128)(2,1)}, bf16[640,384]{1,0:T(8,128)(2,1)S(1)}, u32[]{:S(2)}) copy-start(bf16[640,384]{1,0:T(8,128)(2,1)S(1)} %collective-permute-done.4.side_ref) | copy-start | bytes 1474564
  76.6 3.4 %copy-start.8 = (bf16[640,384]{1,0:T(8,128)(2,1)}, bf16[640,384]{1,0:T(8,128)(2,1)S(1)}, u32[]{:S(2)}) copy-start(bf16[640,384]{1,0:T(8,128)(2,1)S(1)} %collective-permute-done.8.inner_ref) | copy-start | bytes 1474564
  76.7 3.2 %collective-permute-start.11 = (bf16[512,384]{1,0:T(8,128)(2,1)S(1)}, bf16[512,384]{1,0:T(8,128)(2,1)S(1)}, u32[]{:S(2)}, u32[]{:S(2)}) collective-permute-start(bf16[512,384]{1,0:T(8,128)(2,1)S(1)} %slice.88), channel_id=1, source_target_pairs={{0,1},{1,0},{2,3},{3,2},{4,5},{5,4},{6,7},{7,6},{8,9},{9,8},{10,11... | collective-permute-start | bytes 1179656 | tf_op jit(solution)/shard_map/ppermute | solution.py:358
  76.8 3.1 %collective-permute-start.12 = (bf16[512,384]{1,0:T(8,128)(2,1)S(1)}, bf16[512,384]{1,0:T(8,128)(2,1)S(1)}, u32[]{:S(2)}, u32[]{:S(2)}) collective-permute-start(bf16[512,384]{1,0:T(8,128)(2,1)S(1)} %collective-permute-done.5.up_two_ref), channel_id=1, source_target_pairs={{0,1},{1,0},{2,3},{3,2},{4,5},{5,4},{6,7},{7,6},{8,9},{9,8},{10,11... | collective-permute-start | bytes 1179656 | tf_op jit(solution)/shard_map/ppermute | solution.py:358
  77.3 2.6 %collective-permute-start.13 = (bf16[512,384]{1,0:T(8,128)(2,1)S(1)}, bf16[512,384]{1,0:T(8,128)(2,1)S(1)}, u32[]{:S(2)}, u32[]{:S(2)}) collective-permute-start(bf16[512,384]{1,0:T(8,128)(2,1)S(1)} %collective-permute-done.6.down_two_ref), channel_id=1, source_target_pairs={{0,1},{1,0},{2,3},{3,2},{4,5},{5,4},{6,7},{7,6},{8,9},{9,8},{10,11... | collective-permute-start | bytes 1179656 | tf_op jit(solution)/shard_map/ppermute | solution.py:358
  77.4 2.5 %collective-permute-start.14 = (bf16[256,384]{1,0:T(8,128)(2,1)S(1)}, bf16[256,384]{1,0:T(8,128)(2,1)S(1)}, u32[]{:S(2)}, u32[]{:S(2)}) collective-permute-start(bf16[256,384]{1,0:T(8,128)(2,1)S(1)} %collective-permute-done.7.across_ref), channel_id=1, source_target_pairs={{0,1},{1,0},{2,3},{3,2},{4,5},{5,4},{6,7},{7,6},{8,9},{9,8},{10,11... | collective-permute-start | bytes 589832 | tf_op jit(solution)/shard_map/ppermute | solution.py:358
  77.8 2.2 %copy-start.12 = (bf16[512,384]{1,0:T(8,128)(2,1)}, bf16[512,384]{1,0:T(8,128)(2,1)S(1)}, u32[]{:S(2)}) copy-start(bf16[512,384]{1,0:T(8,128)(2,1)S(1)} %collective-permute-done.10.other_outer_ref) | copy-start | bytes 1179652
  79.9 0.7 copy-start.17
  79.9 0.8 copy-start.13
  79.9 0.9 copy-start.14
  80.0 1.0 copy-start.15
